TPU v7x, 128 devices: a whole 4x4x4 slice. The times are simulated.
128 devices in a mesh: row: 32 (over z, y, core), col: 4 (over x).
Axes of the slice: x: 4, y: 4, z: 4, core: 2. Of those that a mesh axis runs over, the one named last changes fastest.
Arguments:
- panel_v: bfloat16 [2, 32, 2048, 256], P(None, 'row'), may hold values from -0.8984375 to 0.8984375
- head_v: bfloat16 [2048, 256], replicated, may hold values from -0.13183594 to 0.13183594
- head_u: bfloat16 [2048, 256], replicated, may hold values from -0.1875 to 0.1875
- diag_inverse: bfloat16 [2, 2048, 2048], P(None, 'col', 'row'), as said below
- diag_next: float32 [2048, 2048], P('row', 'col'), may hold values from -0.3 to 0.3
- ranks: int32 [2, 32], P(None, 'row'), may hold values from 64 to 256
- trail_col: int32 [32, 4, 4], P('row'), may hold values from 0 to 31
Outputs:
- panel0_factor: bfloat16 [32, 2048, 256], P('row', 'col')
- panel1_factor: bfloat16 [32, 2048, 256], P('row', 'col')
- coupling: float32 [32, 256, 256], P('row')
- head_image: bfloat16 [2048, 256], P('col')
- next_diagonal: float32 [2048, 2048], P('row', 'col')
- trail_cores: float32 [32, 4, 4, 512, 512], P('row', 'col')
Inputs may be any that keep to these rules, and one draw needn't show every extreme that they name: `diag_inverse`: lower triangular, with diagonal entries between 0.5 and 2 and small entries below the diagonal.
All inputs are finite; a program needn't handle non-finite values.
Results may differ from a plain program's by a relative error of at most 0.0057.
Values may be sent and summed in bfloat16 or wider, within the bound.
No kernel may reach another device: no remote copies, remote signals or barrier semaphores. Data moves between devices by JAX's collectives and lax.ppermute only.
A program may use at most 128 MiB of HBM per device.

v0:
```python
import jax
import jax.numpy as jnp
from jax import lax
from jax.experimental import pallas as pl
from jax.experimental.pallas import tpu as pltpu
from jax.sharding import PartitionSpec as P

BF = jnp.bfloat16
F32 = jnp.float32


def row_perm(dz, dy, dc):
    def at(z, y, c):
        return ((z % 4) * 4 + (y % 4)) * 2 + c

    return [
        (at(z, y, c), at(z + dz, y + dy, c ^ dc))
        for z in range(4)
        for y in range(4)
        for c in range(2)
    ]


def along_y(x, step):
    return lax.ppermute(x, "row", row_perm(0, step, 0))


def along_z(x, step):
    return lax.ppermute(x, "row", row_perm(step, 0, 0))


def other_core(x):
    return lax.ppermute(x, "row", row_perm(0, 0, 1))


def along_x(x, step):
    return lax.ppermute(x, "col", [(i, (i + step) % 4) for i in range(4)])


def ring(x, shift):
    before, after = lax.optimization_barrier((shift(x, 1), shift(x, -1)))
    half = x.shape[0] // 2
    opposite_low = shift(before[:half], 1)
    opposite_high = shift(after[half:], -1)
    return [x, before, after, opposite_low, opposite_high]


def gather_chips(x):
    first = jnp.concatenate(ring(x[0], along_y), axis=0)
    second = jnp.concatenate(ring(x[1], along_z), axis=0)
    return ring(first, along_z), ring(second, along_y)


def slot_of(distance):
    return jnp.where(distance == 0, 0, jnp.where(distance == 3, 1, jnp.where(distance == 1, 2, 3)))


DISTANCE = (0, 3, 1, 2)
VMEM = pl.BlockSpec(memory_space=pltpu.VMEM)
SMEM = pl.BlockSpec(memory_space=pltpu.SMEM)


def unit(size):
    rows = lax.broadcasted_iota(jnp.int32, (size, size), 0)
    cols = lax.broadcasted_iota(jnp.int32, (size, size), 1)
    return jnp.where(rows == cols, 1.0, 0.0).astype(BF)


def flip(x):
    return lax.dot_general(
        unit(x.shape[1]), x, (((1,), (1,)), ((), ())), preferred_element_type=F32
    )


def solve_kernel(where, *refs):
    pieces, (right0, right1, right2), (out, *thin), (whole, turned) = (
        refs[:10],
        refs[10:13],
        refs[13:18],
        refs[18:],
    )
    piece = out.shape[0]
    half = piece // 2
    width = whole.shape[1] // 16
    for part in range(2):
        for slow in range(4):
            for fast in range(4):
                if slow < 3:
                    ref, at = pieces[5 * part + slow], fast
                else:
                    ref, at = pieces[5 * part + 3 + fast // 2], fast % 2
                dz, dy = (slow, fast) if part == 0 else (fast, slow)
                z = lax.rem(where[0] + DISTANCE[dz], 4)
                y = lax.rem(where[1] + DISTANCE[dy], 4)
                start = pl.multiple_of((z * 4 + y) * width, width)
                whole[part * half : (part + 1) * half, pl.ds(start, width)] = ref[
                    at * half : (at + 1) * half, :
                ]
    rank = right0.shape[1]
    for n, right in enumerate((right0, right1, right2)):
        out[:, n * rank : (n + 1) * rank] = jnp.dot(
            whole[...], right[...], preferred_element_type=F32
        ).astype(BF)
    turned[...] = flip(out[:, : 2 * rank]).astype(BF)
    quarter = rank // 4
    for step in range(4):
        q = lax.rem(where[2] + step, 4)
        for a in range(2):
            start = pl.multiple_of(a * rank + q * quarter, quarter)
            thin[step][a * quarter : (a + 1) * quarter, :] = turned[pl.ds(start, quarter), :]


def solve(where, pieces, rights):
    piece = pieces[0].shape[0] // 2
    tile_size, rank = rights[0].shape
    return pl.pallas_call(
        solve_kernel,
        out_shape=[jax.ShapeDtypeStruct((piece, 3 * rank), BF)]
        + [jax.ShapeDtypeStruct((rank // 2, piece), BF)] * 4,
        in_specs=[SMEM] + [VMEM] * 13,
        out_specs=[VMEM] * 5,
        scratch_shapes=[
            pltpu.VMEM((piece, tile_size), BF),
            pltpu.VMEM((2 * rank, piece), BF),
        ],
        compiler_params=pltpu.CompilerParams(vmem_limit_bytes=40 * 2**20),
        cost_estimate=pl.CostEstimate(
            flops=2 * piece * tile_size * 3 * rank, bytes_accessed=8 * 2**20, transcendentals=0
        ),
        name="solve",
    )(where, *pieces, *rights)


def pick_kernel(places, products, mats, out, heads):
    rank = mats.shape[1]
    quarter = rank // 4
    count = places.shape[1]
    for a in range(2):
        for i in range(count):
            rows = pl.ds(pl.multiple_of(places[a, i] * quarter, quarter), quarter)
            heads[i * quarter : (i + 1) * quarter, :] = products[rows, 2 * rank :].astype(BF)
        low = jnp.dot(heads[...], mats[a], preferred_element_type=F32)
        for i in range(count):
            rows = pl.ds(pl.multiple_of(places[a, i] * quarter, quarter), quarter)
            mine = low[i * quarter : (i + 1) * quarter, :]
            out[a, i, :, :rank] = (mine[:, :rank] + products[rows, a * rank : (a + 1) * rank]).astype(BF)
            out[a, i, :, rank:] = mine[:, rank:].astype(BF)


def pick(places, products, mats):
    count = places.shape[1]
    rank = mats.shape[1]
    return pl.pallas_call(
        pick_kernel,
        out_shape=jax.ShapeDtypeStruct((2, count, rank // 4, 2 * rank), BF),
        in_specs=[SMEM, VMEM, VMEM],
        out_specs=VMEM,
        scratch_shapes=[pltpu.VMEM((count * rank // 4, rank), BF)],
        compiler_params=pltpu.CompilerParams(vmem_limit_bytes=40 * 2**20),
        cost_estimate=pl.CostEstimate(
            flops=2**29, bytes_accessed=10 * 2**20, transcendentals=0
        ),
        name="pick",
    )(places, products, mats)


def settle_kernel(landed, out):
    rank = landed.shape[4] // 2
    for p in range(2):
        x = landed[p, :, 0].reshape(rank, 2 * rank)
        direct = flip(x[:, :rank])
        crossed = flip(x[:, rank:])
        cols = slice(p * rank, (p + 1) * rank)
        out[0, :rank, cols] = direct if p == 0 else crossed
        out[0, rank:, cols] = crossed if p == 0 else direct


def settle(landed):
    _, cols, slots, quarter, width = landed.shape
    return pl.pallas_call(
        settle_kernel,
        grid=(slots,),
        out_shape=jax.ShapeDtypeStruct((slots, width, width), F32),
        in_specs=[pl.BlockSpec((2, cols, 1, quarter, width), lambda s: (0, 0, s, 0, 0))],
        out_specs=pl.BlockSpec((1, width, width), lambda s: (s, 0, 0)),
        cost_estimate=pl.CostEstimate(flops=2**30, bytes_accessed=6 * 2**20, transcendentals=0),
        name="settle",
    )(landed)


def body(panel_v, head_v, head_u, diag_inverse, diag_next, ranks, trail_col):
    tile_size = panel_v.shape[2]
    rank = panel_v.shape[3]
    piece = tile_size // 4
    quarter = rank // 4
    col_id = lax.axis_index("col")
    row_id = lax.axis_index("row")
    core = row_id % 2
    my_y = (row_id // 2) % 4
    my_z = row_id // 8
    on_zero = core == 0

    def pick_core(zero, one):
        return jnp.where(on_zero, zero, one)

    inv_mine = pick_core(diag_inverse[0], diag_inverse[1])
    inv_theirs = other_core(pick_core(diag_inverse[1], diag_inverse[0]))
    inv_pair = jnp.concatenate(
        [pick_core(inv_mine, inv_theirs), pick_core(inv_theirs, inv_mine)], axis=1
    ).reshape(2, piece // 2, -1)
    inv_pair, panel_v = lax.optimization_barrier((inv_pair, panel_v))
    part0, part1 = gather_chips(inv_pair)
    keep = (jnp.arange(rank)[None, None, :] < ranks[:, :, None]).astype(BF)
    masked = (panel_v * keep[:, :, None, :])[:, 0]
    mine = pick_core(masked[0], masked[1])
    theirs = other_core(pick_core(masked[1], masked[0]))
    rights = [pick_core(mine, theirs), pick_core(theirs, mine), pick_core(head_v, head_u)]
    where = jnp.stack([my_z, my_y, col_id]).astype(jnp.int32)
    solved, *thin_parts = solve(where, part0 + part1, rights)

    passed = other_core(
        jnp.concatenate(
            [
                pick_core(solved[:, rank : 2 * rank], solved[:, :rank]),
                solved[:, 2 * rank :],
            ],
            axis=1,
        )
    )
    own = pick_core(solved[:, :rank], solved[:, rank : 2 * rank])
    factor_first = pick_core(own, passed[:, :rank])
    factor_second = pick_core(passed[:, :rank], own)
    head_image = pick_core(passed[:, rank:], solved[:, 2 * rank :])

    thin = jnp.concatenate(
        [
            thin_parts[0],
            along_x(thin_parts[1], 1),
            along_x(thin_parts[3], -1),
            along_x(thin_parts[2], 2),
        ],
        axis=1,
    ).reshape(2, quarter, tile_size)
    gathered0, gathered1 = gather_chips(thin)

    whole = jnp.concatenate(ring(solved, along_x), axis=0)
    head = whole[:, 2 * rank :]
    small = lax.dot_general(whole, head, (((0,), (0,)), ((), ())), preferred_element_type=F32)
    small_other = other_core(small)
    small_zero = pick_core(small, small_other)
    coupling = pick_core(small_zero[:rank], small_zero[rank : 2 * rank])
    gram_h = small_zero[2 * rank :]

    def split(x):
        high = x.astype(BF)
        return high, (x - high.astype(F32)).astype(BF)

    band = tile_size // 32
    upper_band = lax.dynamic_slice_in_dim(head_u, row_id * band, band, 0)
    upper_piece = lax.dynamic_slice_in_dim(head_u, col_id * piece, piece, 0)

    def dot(a, b):
        return jnp.dot(a, b, preferred_element_type=F32)

    gram_high, gram_low = split(gram_h)
    middle_high, middle_low = split(dot(upper_band, gram_high) + dot(upper_band, gram_low))
    next_diagonal = diag_next - (
        dot(middle_high, upper_piece.T) + dot(middle_low, upper_piece.T)
    )

    pieces = gathered0 + gathered1
    products = jnp.concatenate([dot(p, whole) for p in pieces], axis=0)
    mats = []
    for a in range(2):
        c_mine = small[a * rank : (a + 1) * rank]
        c_other = small_other[a * rank : (a + 1) * rank]
        w = jnp.dot(small_other[2 * rank :], c_mine.T, precision=lax.Precision.HIGHEST)
        mats.append(
            jnp.concatenate([pick_core(w, jnp.zeros_like(w)), -c_other.T], axis=1).astype(BF)
        )
    tiles = trail_col[0]
    slots = tiles.shape[1]
    other_tiles = other_core(tiles.astype(F32)).astype(jnp.int32)
    j = jnp.stack([pick_core(tiles, other_tiles), pick_core(other_tiles, tiles)]).reshape(2, -1)
    sy = slot_of(((j // 2) % 4 - my_y) % 4)
    sz = slot_of((j // 8 - my_z) % 4)
    places = jnp.where(j % 2 == 0, sz * 4 + sy, 16 + sy * 4 + sz)
    picked = pick(places, products, jnp.stack(mats))
    chip_groups = [[(2 * chip + m) * 4 + c for m in range(2) for c in range(4)] for chip in range(16)]
    landed = lax.all_to_all(
        picked.reshape(8, slots, quarter, 2 * rank),
        ("row", "col"),
        0,
        0,
        axis_index_groups=chip_groups,
        tiled=True,
    )
    cores = settle(landed.reshape(2, 4, slots, quarter, 2 * rank))
    trail_cores = cores.reshape(1, 1, slots, 2 * rank, 2 * rank)
    return (
        factor_first[None],
        factor_second[None],
        coupling[None],
        head_image,
        next_diagonal,
        trail_cores,
    )


def solution(mesh):
    return jax.shard_map(
        body,
        mesh=mesh,
        in_specs=(
            P(None, "row", None, None),
            P(),
            P(),
            P(None, "col", "row"),
            P("row", "col"),
            P(None, "row"),
            P("row", None, None),
        ),
        out_specs=(
            P("row", "col", None),
            P("row", "col", None),
            P("row", None, None),
            P("col", None),
            P("row", "col"),
            P("row", "col", None, None, None),
        ),
        check_vma=False,
    )
```

profile of v0, /device:TPU:1, one launch (start us, length us, event | category | flops | bytes accessed | tf_op | source)
XLA Modules:
  0.0 167.3 jit_solution(7526132849014862186)
XLA Ops:
  0.7 0.9 select_bitcast_fusion.3
  1.6 1.5 collective-permute-start
  3.8 1.3 broadcast_select_fusion.1.refs_12_
  5.4 1.4 collective-permute-start.1
  6.9 1.5 collective-permute-start.2
  8.4 1.6 collective-permute-start.9
  10.0 2.1 %collective-permute-start.10 = (bf16[256,128]{1,0:T(8,128)(2,1)S(1)}, bf16[256,128]{1,0:T(8,128)(2,1)S(1)}, u32[]{:S(2)}, u32[]{:S(2)}) collective-permute-start(bf16[256,128]{1,0:T(8,128)(2,1)S(1)} %get-tuple-element.71), channel_id=1, source_target_pairs={{0,96},{4,100},{8,104},{12,108},{16,112},{20,116},{24,120},{28,124... | collective-permute-start | bytes 196616 | tf_op jit(solution)/shard_map/ppermute | solution.py:29
  12.1 1.7 %broadcast_multiply_fusion = bf16[2,1,2048,256]{3,2,1,0:T(8,128)(2,1)S(1)} fusion(bf16[2,1,2048,256]{3,2,1,0:T(8,128)(2,1)} %param.7, bf16[2,256]{1,0:T(2,128)(2,1)S(1)} %compare_convert_fusion), kind=kLoop, calls=%fused_computation.24 | loop fusion | flops 1048576 | bytes 4195328 | tf_op jit(solution)/shard_map/mul | solution.py:214
  13.9 1.3 select_bitcast_fusion
  15.2 1.2 collective-permute-start.17
  16.6 2.7 %collective-permute-start.4 = (bf16[128,128]{1,0:T(8,128)(2,1)S(1)}, bf16[128,128]{1,0:T(8,128)(2,1)S(1)}, u32[]{:S(2)}, u32[]{:S(2)}) collective-permute-start(bf16[128,128]{1,0:T(8,128)(2,1)S(1)} %slice.137), channel_id=1, source_target_pairs={{0,24},{4,28},{8,0},{12,4},{16,8},{20,12},{24,16},{28,20},{32,56},... | collective-permute-start | bytes 98312 | tf_op jit(solution)/shard_map/ppermute | solution.py:25
  19.3 1.1 collective-permute-done.3
  20.4 1.7 %collective-permute-start.12 = (bf16[128,128]{1,0:T(8,128)(2,1)S(1)}, bf16[128,128]{1,0:T(8,128)(2,1)S(1)}, u32[]{:S(2)}, u32[]{:S(2)}) collective-permute-start(bf16[128,128]{1,0:T(8,128)(2,1)S(1)} %slice.142), channel_id=1, source_target_pairs={{0,96},{4,100},{8,104},{12,108},{16,112},{20,116},{24,120},{28,124... | collective-permute-start | bytes 98312 | tf_op jit(solution)/shard_map/ppermute | solution.py:29
  22.3 1.0 collective-permute-done.11
  23.3 1.7 collective-permute-start.6
  25.1 2.7 %collective-permute-start.14 = (bf16[1024,128]{1,0:T(8,128)(2,1)S(1)}, bf16[1024,128]{1,0:T(8,128)(2,1)S(1)}, u32[]{:S(2)}, u32[]{:S(2)}) collective-permute-start(bf16[1024,128]{1,0:T(8,128)(2,1)S(1)} %constant_dynamic-update-slice_fusion.5.refs_5_), channel_id=1, source_target_pairs={{0,24},{4,28},{8,0},{12,4},{16,8},{20,12},{24,16},{28,20},{32,56},... | collective-permute-start | bytes 786440 | tf_op jit(solution)/shard_map/ppermute | solution.py:25
  28.0 1.8 %collective-permute-done.5.refs_1_ = bf16[1024,128]{1,0:T(8,128)(2,1)S(1)} collective-permute-done((bf16[1024,128]{1,0:T(8,128)(2,1)S(1)}, bf16[1024,128]{1,0:T(8,128)(2,1)S(1)}, u32[]{:S(2)}, u32[]{:S(2)}) %collective-permute-start.5) | collective-permute-done | bytes 262176 | tf_op jit(solution)/shard_map/ppermute | solution.py:29
  29.9 2.7 %collective-permute-start.8 = (bf16[512,128]{1,0:T(8,128)(2,1)S(1)}, bf16[512,128]{1,0:T(8,128)(2,1)S(1)}, u32[]{:S(2)}, u32[]{:S(2)}) collective-permute-start(bf16[512,128]{1,0:T(8,128)(2,1)S(1)} %slice.139), channel_id=1, source_target_pairs={{0,96},{4,100},{8,104},{12,108},{16,112},{20,116},{24,120},{28,124... | collective-permute-start | bytes 393224 | tf_op jit(solution)/shard_map/ppermute | solution.py:29
  32.8 2.7 %collective-permute-start.16 = (bf16[512,128]{1,0:T(8,128)(2,1)S(1)}, bf16[512,128]{1,0:T(8,128)(2,1)S(1)}, u32[]{:S(2)}, u32[]{:S(2)}) collective-permute-start(bf16[512,128]{1,0:T(8,128)(2,1)S(1)} %slice.144), channel_id=1, source_target_pairs={{0,24},{4,28},{8,0},{12,4},{16,8},{20,12},{24,16},{28,20},{32,56},... | collective-permute-start | bytes 393224 | tf_op jit(solution)/shard_map/ppermute | solution.py:25
  35.5 2.0 %bitcast_select_fusion = (bf16[2048,256]{1,0:T(8,128)(2,1)S(1)}, bf16[2048,256]{1,0:T(8,128)(2,1)S(1)}) fusion(bf16[2048,256]{1,0:T(8,128)(2,1)} %collective-permute-done.17, pred[]{:T(512)S(6)} %eq.32, bf16[2,1,2048,256]{3,2,1,0:T(8,128)(2,1)} %copy-done.2), kind=kLoop, calls=%fused_computation.21 | loop fusion | flops 1572864 | bytes 5243904 | tf_op jit(solution)/shard_map/jit(_where)/select_n | solution.py:204
  38.1 3.2 %solve.1 = (bf16[512,768]{1,0:T(8,128)(2,1)S(1)}, bf16[128,512]{1,0:T(8,128)(2,1)S(1)}, bf16[128,512]{1,0:T(8,128)(2,1)S(1)}, bf16[128,512]{1,0:T(8,128)(2,1)S(1)}, bf16[128,512]{1,0:T(8,128)(2,1)S(1)}) custom-call(s32[3]{0:T(128)S(1)} %pad_add_fusion.1.where, bf16[1024,128]{1,0:T(8,128)(2,1)S(1)} %constant_dynamic-update-slice_fusion.refs_0_, ...), custom_call_target="tpu_custom_call" | custom-call | flops 1610612736 | bytes 8388608 | tf_op jit(solution)/shard_map/solve/pallas_call | solution.py:116
  41.3 1.3 collective-permute-start.25
  42.6 1.5 collective-permute-start.26
  44.2 1.6 collective-permute-start.27
  46.5 3.1 %collective-permute-done.27 = bf16[128,512]{1,0:T(8,128)(2,1)S(1)} collective-permute-done((bf16[128,512]{1,0:T(8,128)(2,1)S(1)}, bf16[128,512]{1,0:T(8,128)(2,1)S(1)}, u32[]{:S(2)}, u32[]{:S(2)}) %collective-permute-start.27) | collective-permute-done | bytes 131104 | tf_op jit(solution)/shard_map/ppermute | solution.py:37
  49.6 0.9 fusion.32
  50.6 2.7 %collective-permute-start.29 = (bf16[64,2048]{1,0:T(8,128)(2,1)S(1)}, bf16[64,2048]{1,0:T(8,128)(2,1)S(1)}, u32[]{:S(2)}, u32[]{:S(2)}) collective-permute-start(bf16[64,2048]{1,0:T(8,128)(2,1)S(1)} %get-tuple-element.68), channel_id=1, source_target_pairs={{0,24},{4,28},{8,0},{12,4},{16,8},{20,12},{24,16},{28,20},{32,56},... | collective-permute-start | bytes 786440 | tf_op jit(solution)/shard_map/ppermute | solution.py:25
  53.5 2.5 %collective-permute-start.20 = (bf16[512,768]{1,0:T(8,128)(2,1)S(1)}, bf16[512,768]{1,0:T(8,128)(2,1)S(1)}, u32[]{:S(2)}, u32[]{:S(2)}) collective-permute-start(bf16[512,768]{1,0:T(8,128)(2,1)S(1)} %get-tuple-element.41), channel_id=1, source_target_pairs={{0,3},{1,0},{2,1},{3,2},{4,7},{5,4},{6,5},{7,6},{8,11},{9,8},{10,9... | collective-permute-start | bytes 2359304 | tf_op jit(solution)/shard_map/ppermute | solution.py:37
  56.0 0.9 pad_maximum_fusion
  57.1 2.7 %collective-permute-start.37 = (bf16[64,2048]{1,0:T(8,128)(2,1)S(1)}, bf16[64,2048]{1,0:T(8,128)(2,1)S(1)}, u32[]{:S(2)}, u32[]{:S(2)}) collective-permute-start(bf16[64,2048]{1,0:T(8,128)(2,1)S(1)} %get-tuple-element.65), channel_id=1, source_target_pairs={{0,96},{4,100},{8,104},{12,108},{16,112},{20,116},{24,120},{28,124... | collective-permute-start | bytes 786440 | tf_op jit(solution)/shard_map/ppermute | solution.py:29
  61.3 2.2 %collective-permute-done.36 = bf16[64,2048]{1,0:T(8,128)(2,1)S(1)} collective-permute-done((bf16[64,2048]{1,0:T(8,128)(2,1)S(1)}, bf16[64,2048]{1,0:T(8,128)(2,1)S(1)}, u32[]{:S(2)}, u32[]{:S(2)}) %collective-permute-start.36) | collective-permute-done | bytes 262176 | tf_op jit(solution)/shard_map/ppermute | solution.py:29
  63.5 1.5 collective-permute-start.31
  65.0 0.8 constant_dynamic-update-slice_fusion.27
  66.6 2.7 %collective-permute-start.39 = (bf16[32,2048]{1,0:T(8,128)(2,1)S(1)}, bf16[32,2048]{1,0:T(8,128)(2,1)S(1)}, u32[]{:S(2)}, u32[]{:S(2)}) collective-permute-start(bf16[32,2048]{1,0:T(8,128)(2,1)S(1)} %slice.165), channel_id=1, source_target_pairs={{0,96},{4,100},{8,104},{12,108},{16,112},{20,116},{24,120},{28,124... | collective-permute-start | bytes 393224 | tf_op jit(solution)/shard_map/ppermute | solution.py:29
  70.6 2.7 %collective-permute-start.33 = (bf16[256,2048]{1,0:T(8,128)(2,1)}, bf16[256,2048]{1,0:T(8,128)(2,1)}, u32[]{:S(2)}, u32[]{:S(2)}) collective-permute-start(bf16[256,2048]{1,0:T(8,128)(2,1)} %constant_dynamic-update-slice_fusion.19), channel_id=1, source_target_pairs={{0,96},{4,100},{8,104},{12,108},{16,112},{20,116},{24,120},{28,124... | collective-permute-start | bytes 3145736 | tf_op jit(solution)/shard_map/ppermute | solution.py:29
  74.1 2.7 %collective-permute-start.22 = (bf16[256,768]{1,0:T(8,128)(2,1)S(1)}, bf16[256,768]{1,0:T(8,128)(2,1)S(1)}, u32[]{:S(2)}, u32[]{:S(2)}) collective-permute-start(bf16[256,768]{1,0:T(8,128)(2,1)S(1)} %slice.152), channel_id=1, source_target_pairs={{0,3},{1,0},{2,1},{3,2},{4,7},{5,4},{6,5},{7,6},{8,11},{9,8},{10,9... | collective-permute-start | bytes 1179656 | tf_op jit(solution)/shard_map/ppermute | solution.py:37
  77.6 3.9 %collective-permute-done.21 = bf16[256,768]{1,0:T(8,128)(2,1)S(1)} collective-permute-done((bf16[256,768]{1,0:T(8,128)(2,1)S(1)}, bf16[256,768]{1,0:T(8,128)(2,1)S(1)}, u32[]{:S(2)}, u32[]{:S(2)}) %collective-permute-start.21) | collective-permute-done | bytes 393248 | tf_op jit(solution)/shard_map/ppermute | solution.py:37
  82.0 1.7 copy-done
  83.7 1.0 fusion.5
  85.0 12.0 %collective-permute-start.23 = (f32[768,256]{0,1:T(8,128)S(1)}, f32[768,256]{0,1:T(8,128)S(1)}, u32[]{:S(2)}, u32[]{:S(2)}) collective-permute-start(f32[768,256]{0,1:T(8,128)S(1)} %copy.14), channel_id=1, source_target_pairs={{0,4},{4,0},{8,12},{12,8},{16,20},{20,16},{24,28},{28,24},{32,36},... | collective-permute-start | bytes 2359304 | tf_op jit(solution)/shard_map/ppermute | solution.py:33
  97.0 3.2 %convolution_dynamic-update-slice_fusion.5 = f32[2048,768]{1,0:T(8,128)S(1)} fusion(bf16[256,2048]{1,0:T(8,128)(2,1)} %constant_dynamic-update-slice_fusion.19, bf16[2048,768]{1,0:T(8,128)(2,1)} %copy-done), kind=kOutput, calls=%fused_computation.5 | convolution fusion | flops 805306368 | bytes 4980736 | tf_op jit(solution)/shard_map/dot_general | solution.py:263
  100.3 1.2 slice.161
  101.6 1.1 slice.162
  102.7 2.7 %collective-permute-start.35 = (bf16[128,2048]{1,0:T(8,128)(2,1)S(1)}, bf16[128,2048]{1,0:T(8,128)(2,1)S(1)}, u32[]{:S(2)}, u32[]{:S(2)}) collective-permute-start(bf16[128,2048]{1,0:T(8,128)(2,1)S(1)} %slice.162), channel_id=1, source_target_pairs={{0,96},{4,100},{8,104},{12,108},{16,112},{20,116},{24,120},{28,124... | collective-permute-start | bytes 1572872 | tf_op jit(solution)/shard_map/ppermute | solution.py:29
  105.5 1.1 slice.166
  106.6 1.1 collective-permute-start.42
  107.7 1.1 slice.167
  108.8 2.2 %convolution_dynamic-update-slice_fusion.4 = f32[2048,768]{1,0:T(8,128)S(1)} fusion(f32[2048,768]{1,0:T(8,128)S(1)} %convolution_dynamic-update-slice_fusion.5, bf16[256,2048]{1,0:T(8,128)(2,1)} %collective-permute-done.32, bf16[2048,768]{1,0:T(8,128)(2,1)S(1)} %copy-done.1), kind=kOutput, calls=%fused_computation.4 | convolution fusion | flops 805306368 | bytes 4980736 | tf_op jit(solution)/shard_map/dot_general | solution.py:263
  111.0 2.2 %convolution_dynamic-update-slice_fusion.3 = f32[2048,768]{1,0:T(8,128)S(1)} fusion(f32[2048,768]{1,0:T(8,128)S(1)} %convolution_dynamic-update-slice_fusion.4, bf16[256,2048]{1,0:T(8,128)(2,1)} %collective-permute-done.33, bf16[2048,768]{1,0:T(8,128)(2,1)S(1)} %copy-done.1), kind=kOutput, calls=%fused_computation.3 | convolution fusion | flops 805306368 | bytes 4980736 | tf_op jit(solution)/shard_map/dot_general | solution.py:263
  113.2 1.9 %collective-permute-start.43 = (bf16[128,2048]{1,0:T(8,128)(2,1)S(1)}, bf16[128,2048]{1,0:T(8,128)(2,1)S(1)}, u32[]{:S(2)}, u32[]{:S(2)}) collective-permute-start(bf16[128,2048]{1,0:T(8,128)(2,1)S(1)} %slice.167), channel_id=1, source_target_pairs={{0,24},{4,28},{8,0},{12,4},{16,8},{20,12},{24,16},{28,20},{32,56},... | collective-permute-start | bytes 1572872 | tf_op jit(solution)/shard_map/ppermute | solution.py:25
  117.7 2.2 %convolution_dynamic-update-slice_fusion.2 = f32[2048,768]{1,0:T(8,128)S(1)} fusion(f32[2048,768]{1,0:T(8,128)S(1)} %convolution_dynamic-update-slice_fusion.8, bf16[256,2048]{1,0:T(8,128)(2,1)} %constant_dynamic-update-slice_fusion.24, bf16[2048,768]{1,0:T(8,128)(2,1)S(1)} %copy-done.1), kind=kOutput, calls=%fused_computation.2 | convolution fusion | flops 805306368 | bytes 4980736 | tf_op jit(solution)/shard_map/dot_general | solution.py:263
  119.9 2.2 %convolution_dynamic-update-slice_fusion.1 = f32[2048,768]{1,0:T(8,128)S(1)} fusion(f32[2048,768]{1,0:T(8,128)S(1)} %convolution_dynamic-update-slice_fusion.2, bf16[256,2048]{1,0:T(8,128)(2,1)} %collective-permute-done.40, bf16[2048,768]{1,0:T(8,128)(2,1)S(1)} %copy-done.1), kind=kOutput, calls=%fused_computation.1 | convolution fusion | flops 805306368 | bytes 4980736 | tf_op jit(solution)/shard_map/dot_general | solution.py:263
  122.1 2.2 %convolution_dynamic-update-slice_fusion = f32[2048,768]{1,0:T(8,128)S(1)} fusion(f32[2048,768]{1,0:T(8,128)S(1)} %convolution_dynamic-update-slice_fusion.1, bf16[256,2048]{1,0:T(8,128)(2,1)} %collective-permute-done.41, bf16[2048,768]{1,0:T(8,128)(2,1)S(1)} %copy-done.1), kind=kOutput, calls=%fused_computation | convolution fusion | flops 805306368 | bytes 4980736 | tf_op jit(solution)/shard_map/dot_general | solution.py:263
  125.8 2.6 %pick.1 = bf16[2,16,64,512]{3,2,1,0:T(8,128)(2,1)} custom-call(s32[2,16]{1,0:T(2,128)S(1)} %compare_select_fusion.12.places, f32[2048,768]{1,0:T(8,128)S(1)} %convolution_dynamic-update-slice_fusion.6.products, bf16[2,256,512]{2,1,0:T(8,128)(2,1)S(1)} %maximum_maximum_fusion.mats), custom_call_target="tpu_custom_call" | custom-call | flops 536870912 | bytes 10485760 | tf_op jit(solution)/shard_map/pick/pallas_call | solution.py:153
  128.4 6.6 %all-to-all-start = ((bf16[8,4,64,512]{3,2,1,0:T(8,128)(2,1)}), bf16[8,4,64,512]{3,2,1,0:T(8,128)(2,1)S(1)}, u32[]{:S(2)}, u32[]{:S(2)}) async-start(bf16[8,4,64,512]{3,2,1,0:T(8,128)(2,1)} %bitcast.21), calls=%async_computation | async-start | bytes 4194304 | tf_op jit(solution)/shard_map/all_to_all | solution.py:290
  135.0 0.9 slice_select_fusion
  135.9 1.4 copy.15
  137.4 1.0 fusion.17
  138.4 0.9 convolution_add_fusion.1
  139.6 0.9 fusion.4
  140.4 0.7 fusion.11
  141.2 20.0 %all-to-all-done = bf16[8,4,64,512]{3,2,1,0:T(8,128)(2,1)S(1)} async-done(((bf16[8,4,64,512]{3,2,1,0:T(8,128)(2,1)}), bf16[8,4,64,512]{3,2,1,0:T(8,128)(2,1)S(1)}, u32[]{:S(2)}, u32[]{:S(2)}) %all-to-all-start) | async-done | bytes 2097184 | tf_op jit(solution)/shard_map/all_to_all | solution.py:290
  161.2 1.3 copy-done.3
  162.5 4.7 %settle.1 = f32[4,512,512]{2,1,0:T(8,128)} custom-call(bf16[2,4,4,64,512]{4,3,2,1,0:T(8,128)(2,1)} %bitcast.69), custom_call_target="tpu_custom_call" | custom-call | flops 1073741824 | bytes 6291456 | tf_op jit(solution)/shard_map/settle/pallas_call | solution.py:180
  (138 shorter events, 14.0 us)
Async XLA Ops:
  0.6 4.6 %copy-start.7 = (bf16[2,512,64]{1,2,0:T(8,128)(2,1)S(1)}, bf16[2,512,64]{1,2,0:T(8,128)(2,1)}, u32[]{:S(2)}) copy-start(bf16[2,512,64]{1,2,0:T(8,128)(2,1)} %param.10) | copy-start | bytes 393220
  0.6 4.5 %copy-start.10 = (s32[2,1]{0,1:T(1,128)S(1)}, s32[2,1]{0,1:T(1,128)}, u32[]{:S(2)}) copy-start(s32[2,1]{0,1:T(1,128)} %param.12) | copy-start | bytes 28
  1.6 3.6 %collective-permute-start = (bf16[512,64]{0,1:T(8,128)(2,1)S(1)}, bf16[512,64]{0,1:T(8,128)(2,1)S(1)}, u32[]{:S(2)}, u32[]{:S(2)}) collective-permute-start(bf16[512,64]{0,1:T(8,128)(2,1)S(1)} %select_bitcast_fusion.3), channel_id=1, source_target_pairs={{0,4},{4,0},{8,12},{12,8},{16,20},{20,16},{24,28},{28,24},{32,36},... | collective-permute-start | bytes 196616 | tf_op jit(solution)/shard_map/ppermute | solution.py:33
  3.8 21.3 %collective-permute-start.24 = (f32[4,4]{1,0:T(4,128)S(1)}, f32[4,4]{1,0:T(4,128)S(1)}, u32[]{:S(2)}, u32[]{:S(2)}) collective-permute-start(f32[4,4]{1,0:T(4,128)S(1)} %bitcast_convert_fusion), channel_id=1, source_target_pairs={{0,4},{4,0},{8,12},{12,8},{16,20},{20,16},{24,28},{28,24},{32,36},... | collective-permute-start | bytes 200 | tf_op jit(solution)/shard_map/ppermute | solution.py:33
  5.4 9.7 %collective-permute-start.1 = (bf16[256,128]{1,0:T(8,128)(2,1)S(1)}, bf16[256,128]{1,0:T(8,128)(2,1)S(1)}, u32[]{:S(2)}, u32[]{:S(2)}) collective-permute-start(bf16[256,128]{1,0:T(8,128)(2,1)S(1)} %get-tuple-element.72), channel_id=1, source_target_pairs={{0,8},{4,12},{8,16},{12,20},{16,24},{20,28},{24,0},{28,4},{32,40},... | collective-permute-start | bytes 196616 | tf_op jit(solution)/shard_map/ppermute | solution.py:25
  6.9 9.5 %collective-permute-start.2 = (bf16[256,128]{1,0:T(8,128)(2,1)S(1)}, bf16[256,128]{1,0:T(8,128)(2,1)S(1)}, u32[]{:S(2)}, u32[]{:S(2)}) collective-permute-start(bf16[256,128]{1,0:T(8,128)(2,1)S(1)} %get-tuple-element.72), channel_id=1, source_target_pairs={{0,24},{4,28},{8,0},{12,4},{16,8},{20,12},{24,16},{28,20},{32,56},... | collective-permute-start | bytes 196616 | tf_op jit(solution)/shard_map/ppermute | solution.py:25
  8.4 8.2 %collective-permute-start.9 = (bf16[256,128]{1,0:T(8,128)(2,1)S(1)}, bf16[256,128]{1,0:T(8,128)(2,1)S(1)}, u32[]{:S(2)}, u32[]{:S(2)}) collective-permute-start(bf16[256,128]{1,0:T(8,128)(2,1)S(1)} %get-tuple-element.71), channel_id=1, source_target_pairs={{0,32},{4,36},{8,40},{12,44},{16,48},{20,52},{24,56},{28,60},{32,6... | collective-permute-start | bytes 196616 | tf_op jit(solution)/shard_map/ppermute | solution.py:29
  10.0 6.5 %collective-permute-start.10 = (bf16[256,128]{1,0:T(8,128)(2,1)S(1)}, bf16[256,128]{1,0:T(8,128)(2,1)S(1)}, u32[]{:S(2)}, u32[]{:S(2)}) collective-permute-start(bf16[256,128]{1,0:T(8,128)(2,1)S(1)} %get-tuple-element.71), channel_id=1, source_target_pairs={{0,96},{4,100},{8,104},{12,108},{16,112},{20,116},{24,120},{28,124... | collective-permute-start | bytes 196616 | tf_op jit(solution)/shard_map/ppermute | solution.py:29
  13.9 13.8 %copy-start.2 = (bf16[2,1,2048,256]{3,2,1,0:T(8,128)(2,1)}, bf16[2,1,2048,256]{3,2,1,0:T(8,128)(2,1)S(1)}, u32[]{:S(2)}) copy-start(bf16[2,1,2048,256]{3,2,1,0:T(8,128)(2,1)S(1)} %broadcast_multiply_fusion) | copy-start | bytes 6291460
  13.9 13.9 %copy-start.9 = (s32[1,4,4]{2,1,0:T(4,128)S(1)}, s32[1,4,4]{2,1,0:T(4,128)}, u32[]{:S(2)}) copy-start(s32[1,4,4]{2,1,0:T(4,128)} %param.13) | copy-start | bytes 196
  15.2 20.4 %collective-permute-start.17 = (bf16[2048,256]{1,0:T(8,128)(2,1)}, bf16[2048,256]{1,0:T(8,128)(2,1)}, u32[]{:S(2)}, u32[]{:S(2)}) collective-permute-start(bf16[2048,256]{1,0:T(8,128)(2,1)} %select_bitcast_fusion), channel_id=1, source_target_pairs={{0,4},{4,0},{8,12},{12,8},{16,20},{20,16},{24,28},{28,24},{32,36},... | collective-permute-start | bytes 3145736 | tf_op jit(solution)/shard_map/ppermute | solution.py:33
  16.4 4.0 %collective-permute-start.3 = (bf16[128,128]{1,0:T(8,128)(2,1)S(1)}, bf16[128,128]{1,0:T(8,128)(2,1)S(1)}, u32[]{:S(2)}, u32[]{:S(2)}) collective-permute-start(bf16[128,128]{1,0:T(8,128)(2,1)S(1)} %slice.136), channel_id=1, source_target_pairs={{0,8},{4,12},{8,16},{12,20},{16,24},{20,28},{24,0},{28,4},{32,40},... | collective-permute-start | bytes 98312 | tf_op jit(solution)/shard_map/ppermute | solution.py:25
  16.6 5.5 %collective-permute-start.4 = (bf16[128,128]{1,0:T(8,128)(2,1)S(1)}, bf16[128,128]{1,0:T(8,128)(2,1)S(1)}, u32[]{:S(2)}, u32[]{:S(2)}) collective-permute-start(bf16[128,128]{1,0:T(8,128)(2,1)S(1)} %slice.137), channel_id=1, source_target_pairs={{0,24},{4,28},{8,0},{12,4},{16,8},{20,12},{24,16},{28,20},{32,56},... | collective-permute-start | bytes 98312 | tf_op jit(solution)/shard_map/ppermute | solution.py:25
  19.3 4.0 %collective-permute-start.11 = (bf16[128,128]{1,0:T(8,128)(2,1)S(1)}, bf16[128,128]{1,0:T(8,128)(2,1)S(1)}, u32[]{:S(2)}, u32[]{:S(2)}) collective-permute-start(bf16[128,128]{1,0:T(8,128)(2,1)S(1)} %slice.141), channel_id=1, source_target_pairs={{0,32},{4,36},{8,40},{12,44},{16,48},{20,52},{24,56},{28,60},{32,6... | collective-permute-start | bytes 98312 | tf_op jit(solution)/shard_map/ppermute | solution.py:29
  20.4 4.5 %collective-permute-start.12 = (bf16[128,128]{1,0:T(8,128)(2,1)S(1)}, bf16[128,128]{1,0:T(8,128)(2,1)S(1)}, u32[]{:S(2)}, u32[]{:S(2)}) collective-permute-start(bf16[128,128]{1,0:T(8,128)(2,1)S(1)} %slice.142), channel_id=1, source_target_pairs={{0,96},{4,100},{8,104},{12,108},{16,112},{20,116},{24,120},{28,124... | collective-permute-start | bytes 98312 | tf_op jit(solution)/shard_map/ppermute | solution.py:29
  22.2 7.6 %collective-permute-start.5 = (bf16[1024,128]{1,0:T(8,128)(2,1)S(1)}, bf16[1024,128]{1,0:T(8,128)(2,1)S(1)}, u32[]{:S(2)}, u32[]{:S(2)}) collective-permute-start(bf16[1024,128]{1,0:T(8,128)(2,1)S(1)} %constant_dynamic-update-slice_fusion.refs_0_), channel_id=1, source_target_pairs={{0,32},{4,36},{8,40},{12,44},{16,48},{20,52},{24,56},{28,60},{32,6... | collective-permute-start | bytes 786440 | tf_op jit(solution)/shard_map/ppermute | solution.py:29
  23.3 6.6 %collective-permute-start.6 = (bf16[1024,128]{1,0:T(8,128)(2,1)S(1)}, bf16[1024,128]{1,0:T(8,128)(2,1)S(1)}, u32[]{:S(2)}, u32[]{:S(2)}) collective-permute-start(bf16[1024,128]{1,0:T(8,128)(2,1)S(1)} %constant_dynamic-update-slice_fusion.refs_0_), channel_id=1, source_target_pairs={{0,96},{4,100},{8,104},{12,108},{16,112},{20,116},{24,120},{28,124... | collective-permute-start | bytes 786440 | tf_op jit(solution)/shard_map/ppermute | solution.py:29
  25.0 7.7 %collective-permute-start.13 = (bf16[1024,128]{1,0:T(8,128)(2,1)S(1)}, bf16[1024,128]{1,0:T(8,128)(2,1)S(1)}, u32[]{:S(2)}, u32[]{:S(2)}) collective-permute-start(bf16[1024,128]{1,0:T(8,128)(2,1)S(1)} %constant_dynamic-update-slice_fusion.5.refs_5_), channel_id=1, source_target_pairs={{0,8},{4,12},{8,16},{12,20},{16,24},{20,28},{24,0},{28,4},{32,40},... | collective-permute-start | bytes 786440 | tf_op jit(solution)/shard_map/ppermute | solution.py:25
  25.1 7.6 %collective-permute-start.14 = (bf16[1024,128]{1,0:T(8,128)(2,1)S(1)}, bf16[1024,128]{1,0:T(8,128)(2,1)S(1)}, u32[]{:S(2)}, u32[]{:S(2)}) collective-permute-start(bf16[1024,128]{1,0:T(8,128)(2,1)S(1)} %constant_dynamic-update-slice_fusion.5.refs_5_), channel_id=1, source_target_pairs={{0,24},{4,28},{8,0},{12,4},{16,8},{20,12},{24,16},{28,20},{32,56},... | collective-permute-start | bytes 786440 | tf_op jit(solution)/shard_map/ppermute | solution.py:25
  29.8 7.7 %collective-permute-start.7 = (bf16[512,128]{1,0:T(8,128)(2,1)S(1)}, bf16[512,128]{1,0:T(8,128)(2,1)S(1)}, u32[]{:S(2)}, u32[]{:S(2)}) collective-permute-start(bf16[512,128]{1,0:T(8,128)(2,1)S(1)} %slice.138), channel_id=1, source_target_pairs={{0,32},{4,36},{8,40},{12,44},{16,48},{20,52},{24,56},{28,60},{32,6... | collective-permute-start | bytes 393224 | tf_op jit(solution)/shard_map/ppermute | solution.py:29
  29.9 7.6 %collective-permute-start.8 = (bf16[512,128]{1,0:T(8,128)(2,1)S(1)}, bf16[512,128]{1,0:T(8,128)(2,1)S(1)}, u32[]{:S(2)}, u32[]{:S(2)}) collective-permute-start(bf16[512,128]{1,0:T(8,128)(2,1)S(1)} %slice.139), channel_id=1, source_target_pairs={{0,96},{4,100},{8,104},{12,108},{16,112},{20,116},{24,120},{28,124... | collective-permute-start | bytes 393224 | tf_op jit(solution)/shard_map/ppermute | solution.py:29
  32.7 5.4 %collective-permute-start.15 = (bf16[512,128]{1,0:T(8,128)(2,1)S(1)}, bf16[512,128]{1,0:T(8,128)(2,1)S(1)}, u32[]{:S(2)}, u32[]{:S(2)}) collective-permute-start(bf16[512,128]{1,0:T(8,128)(2,1)S(1)} %slice.143), channel_id=1, source_target_pairs={{0,8},{4,12},{8,16},{12,20},{16,24},{20,28},{24,0},{28,4},{32,40},... | collective-permute-start | bytes 393224 | tf_op jit(solution)/shard_map/ppermute | solution.py:25
  32.8 5.3 %collective-permute-start.16 = (bf16[512,128]{1,0:T(8,128)(2,1)S(1)}, bf16[512,128]{1,0:T(8,128)(2,1)S(1)}, u32[]{:S(2)}, u32[]{:S(2)}) collective-permute-start(bf16[512,128]{1,0:T(8,128)(2,1)S(1)} %slice.144), channel_id=1, source_target_pairs={{0,24},{4,28},{8,0},{12,4},{16,8},{20,12},{24,16},{28,20},{32,56},... | collective-permute-start | bytes 393224 | tf_op jit(solution)/shard_map/ppermute | solution.py:25
  41.3 5.1 %collective-permute-start.25 = (bf16[128,512]{1,0:T(8,128)(2,1)S(1)}, bf16[128,512]{1,0:T(8,128)(2,1)S(1)}, u32[]{:S(2)}, u32[]{:S(2)}) collective-permute-start(bf16[128,512]{1,0:T(8,128)(2,1)S(1)} %get-tuple-element.45), channel_id=1, source_target_pairs={{0,1},{1,2},{2,3},{3,0},{4,5},{5,6},{6,7},{7,4},{8,9},{9,10},{10,1... | collective-permute-start | bytes 393224 | tf_op jit(solution)/shard_map/ppermute | solution.py:37
  42.6 3.9 %collective-permute-start.26 = (bf16[128,512]{1,0:T(8,128)(2,1)S(1)}, bf16[128,512]{1,0:T(8,128)(2,1)S(1)}, u32[]{:S(2)}, u32[]{:S(2)}) collective-permute-start(bf16[128,512]{1,0:T(8,128)(2,1)S(1)} %get-tuple-element.46), channel_id=1, source_target_pairs={{0,3},{1,0},{2,1},{3,2},{4,7},{5,4},{6,5},{7,6},{8,11},{9,8},{10,9... | collective-permute-start | bytes 393224 | tf_op jit(solution)/shard_map/ppermute | solution.py:37
  44.2 5.4 %collective-permute-start.27 = (bf16[128,512]{1,0:T(8,128)(2,1)S(1)}, bf16[128,512]{1,0:T(8,128)(2,1)S(1)}, u32[]{:S(2)}, u32[]{:S(2)}) collective-permute-start(bf16[128,512]{1,0:T(8,128)(2,1)S(1)} %get-tuple-element.47), channel_id=1, source_target_pairs={{0,2},{1,3},{2,0},{3,1},{4,6},{5,7},{6,4},{7,5},{8,10},{9,11},{10,... | collective-permute-start | bytes 393224 | tf_op jit(solution)/shard_map/ppermute | solution.py:37
  50.6 6.5 %collective-permute-start.28 = (bf16[64,2048]{1,0:T(8,128)(2,1)S(1)}, bf16[64,2048]{1,0:T(8,128)(2,1)S(1)}, u32[]{:S(2)}, u32[]{:S(2)}) collective-permute-start(bf16[64,2048]{1,0:T(8,128)(2,1)S(1)} %get-tuple-element.68), channel_id=1, source_target_pairs={{0,8},{4,12},{8,16},{12,20},{16,24},{20,28},{24,0},{28,4},{32,40},... | collective-permute-start | bytes 786440 | tf_op jit(solution)/shard_map/ppermute | solution.py:25
  50.6 9.2 %collective-permute-start.29 = (bf16[64,2048]{1,0:T(8,128)(2,1)S(1)}, bf16[64,2048]{1,0:T(8,128)(2,1)S(1)}, u32[]{:S(2)}, u32[]{:S(2)}) collective-permute-start(bf16[64,2048]{1,0:T(8,128)(2,1)S(1)} %get-tuple-element.68), channel_id=1, source_target_pairs={{0,24},{4,28},{8,0},{12,4},{16,8},{20,12},{24,16},{28,20},{32,56},... | collective-permute-start | bytes 786440 | tf_op jit(solution)/shard_map/ppermute | solution.py:25
  53.3 17.3 %collective-permute-start.19 = (bf16[512,768]{1,0:T(8,128)(2,1)S(1)}, bf16[512,768]{1,0:T(8,128)(2,1)S(1)}, u32[]{:S(2)}, u32[]{:S(2)}) collective-permute-start(bf16[512,768]{1,0:T(8,128)(2,1)S(1)} %get-tuple-element.41), channel_id=1, source_target_pairs={{0,1},{1,2},{2,3},{3,0},{4,5},{5,6},{6,7},{7,4},{8,9},{9,10},{10,1... | collective-permute-start | bytes 2359304 | tf_op jit(solution)/shard_map/ppermute | solution.py:37
  53.5 19.8 %collective-permute-start.20 = (bf16[512,768]{1,0:T(8,128)(2,1)S(1)}, bf16[512,768]{1,0:T(8,128)(2,1)S(1)}, u32[]{:S(2)}, u32[]{:S(2)}) collective-permute-start(bf16[512,768]{1,0:T(8,128)(2,1)S(1)} %get-tuple-element.41), channel_id=1, source_target_pairs={{0,3},{1,0},{2,1},{3,2},{4,7},{5,4},{6,5},{7,6},{8,11},{9,8},{10,9... | collective-permute-start | bytes 2359304 | tf_op jit(solution)/shard_map/ppermute | solution.py:37
  57.0 6.5 %collective-permute-start.36 = (bf16[64,2048]{1,0:T(8,128)(2,1)S(1)}, bf16[64,2048]{1,0:T(8,128)(2,1)S(1)}, u32[]{:S(2)}, u32[]{:S(2)}) collective-permute-start(bf16[64,2048]{1,0:T(8,128)(2,1)S(1)} %get-tuple-element.65), channel_id=1, source_target_pairs={{0,32},{4,36},{8,40},{12,44},{16,48},{20,52},{24,56},{28,60},{32,6... | collective-permute-start | bytes 786440 | tf_op jit(solution)/shard_map/ppermute | solution.py:29
  57.1 7.9 %collective-permute-start.37 = (bf16[64,2048]{1,0:T(8,128)(2,1)S(1)}, bf16[64,2048]{1,0:T(8,128)(2,1)S(1)}, u32[]{:S(2)}, u32[]{:S(2)}) collective-permute-start(bf16[64,2048]{1,0:T(8,128)(2,1)S(1)} %get-tuple-element.65), channel_id=1, source_target_pairs={{0,96},{4,100},{8,104},{12,108},{16,112},{20,116},{24,120},{28,124... | collective-permute-start | bytes 786440 | tf_op jit(solution)/shard_map/ppermute | solution.py:29
  60.5 6.1 %collective-permute-start.30 = (bf16[32,2048]{1,0:T(8,128)(2,1)S(1)}, bf16[32,2048]{1,0:T(8,128)(2,1)S(1)}, u32[]{:S(2)}, u32[]{:S(2)}) collective-permute-start(bf16[32,2048]{1,0:T(8,128)(2,1)S(1)} %slice.159), channel_id=1, source_target_pairs={{0,8},{4,12},{8,16},{12,20},{16,24},{20,28},{24,0},{28,4},{32,40},... | collective-permute-start | bytes 393224 | tf_op jit(solution)/shard_map/ppermute | solution.py:25
  63.5 6.5 %collective-permute-start.31 = (bf16[32,2048]{1,0:T(8,128)(2,1)S(1)}, bf16[32,2048]{1,0:T(8,128)(2,1)S(1)}, u32[]{:S(2)}, u32[]{:S(2)}) collective-permute-start(bf16[32,2048]{1,0:T(8,128)(2,1)S(1)} %slice.160), channel_id=1, source_target_pairs={{0,24},{4,28},{8,0},{12,4},{16,8},{20,12},{24,16},{28,20},{32,56},... | collective-permute-start | bytes 393224 | tf_op jit(solution)/shard_map/ppermute | solution.py:25
  65.8 7.6 %collective-permute-start.38 = (bf16[32,2048]{1,0:T(8,128)(2,1)S(1)}, bf16[32,2048]{1,0:T(8,128)(2,1)S(1)}, u32[]{:S(2)}, u32[]{:S(2)}) collective-permute-start(bf16[32,2048]{1,0:T(8,128)(2,1)S(1)} %slice.164), channel_id=1, source_target_pairs={{0,32},{4,36},{8,40},{12,44},{16,48},{20,52},{24,56},{28,60},{32,6... | collective-permute-start | bytes 393224 | tf_op jit(solution)/shard_map/ppermute | solution.py:29
  66.6 10.2 %collective-permute-start.39 = (bf16[32,2048]{1,0:T(8,128)(2,1)S(1)}, bf16[32,2048]{1,0:T(8,128)(2,1)S(1)}, u32[]{:S(2)}, u32[]{:S(2)}) collective-permute-start(bf16[32,2048]{1,0:T(8,128)(2,1)S(1)} %slice.165), channel_id=1, source_target_pairs={{0,96},{4,100},{8,104},{12,108},{16,112},{20,116},{24,120},{28,124... | collective-permute-start | bytes 393224 | tf_op jit(solution)/shard_map/ppermute | solution.py:29
  70.6 29.6 %collective-permute-start.32 = (bf16[256,2048]{1,0:T(8,128)(2,1)}, bf16[256,2048]{1,0:T(8,128)(2,1)}, u32[]{:S(2)}, u32[]{:S(2)}) collective-permute-start(bf16[256,2048]{1,0:T(8,128)(2,1)} %constant_dynamic-update-slice_fusion.19), channel_id=1, source_target_pairs={{0,32},{4,36},{8,40},{12,44},{16,48},{20,52},{24,56},{28,60},{32,6... | collective-permute-start | bytes 3145736 | tf_op jit(solution)/shard_map/ppermute | solution.py:29
  70.6 29.7 %collective-permute-start.33 = (bf16[256,2048]{1,0:T(8,128)(2,1)}, bf16[256,2048]{1,0:T(8,128)(2,1)}, u32[]{:S(2)}, u32[]{:S(2)}) collective-permute-start(bf16[256,2048]{1,0:T(8,128)(2,1)} %constant_dynamic-update-slice_fusion.19), channel_id=1, source_target_pairs={{0,96},{4,100},{8,104},{12,108},{16,112},{20,116},{24,120},{28,124... | collective-permute-start | bytes 3145736 | tf_op jit(solution)/shard_map/ppermute | solution.py:29
  73.3 8.2 %collective-permute-start.21 = (bf16[256,768]{1,0:T(8,128)(2,1)S(1)}, bf16[256,768]{1,0:T(8,128)(2,1)S(1)}, u32[]{:S(2)}, u32[]{:S(2)}) collective-permute-start(bf16[256,768]{1,0:T(8,128)(2,1)S(1)} %slice.151), channel_id=1, source_target_pairs={{0,1},{1,2},{2,3},{3,0},{4,5},{5,6},{6,7},{7,4},{8,9},{9,10},{10,1... | collective-permute-start | bytes 1179656 | tf_op jit(solution)/shard_map/ppermute | solution.py:37
  74.1 7.9 %collective-permute-start.22 = (bf16[256,768]{1,0:T(8,128)(2,1)S(1)}, bf16[256,768]{1,0:T(8,128)(2,1)S(1)}, u32[]{:S(2)}, u32[]{:S(2)}) collective-permute-start(bf16[256,768]{1,0:T(8,128)(2,1)S(1)} %slice.152), channel_id=1, source_target_pairs={{0,3},{1,0},{2,1},{3,2},{4,7},{5,4},{6,5},{7,6},{8,11},{9,8},{10,9... | collective-permute-start | bytes 1179656 | tf_op jit(solution)/shard_map/ppermute | solution.py:37
  77.5 25.2 %collective-permute-start.40 = (bf16[256,2048]{1,0:T(8,128)(2,1)}, bf16[256,2048]{1,0:T(8,128)(2,1)}, u32[]{:S(2)}, u32[]{:S(2)}) collective-permute-start(bf16[256,2048]{1,0:T(8,128)(2,1)} %constant_dynamic-update-slice_fusion.24), channel_id=1, source_target_pairs={{0,8},{4,12},{8,16},{12,20},{16,24},{20,28},{24,0},{28,4},{32,40},... | collective-permute-start | bytes 3145736 | tf_op jit(solution)/shard_map/ppermute | solution.py:25
  81.5 24.0 %collective-permute-start.41 = (bf16[256,2048]{1,0:T(8,128)(2,1)}, bf16[256,2048]{1,0:T(8,128)(2,1)}, u32[]{:S(2)}, u32[]{:S(2)}) collective-permute-start(bf16[256,2048]{1,0:T(8,128)(2,1)} %constant_dynamic-update-slice_fusion.24), channel_id=1, source_target_pairs={{0,24},{4,28},{8,0},{12,4},{16,8},{20,12},{24,16},{28,20},{32,56},... | collective-permute-start | bytes 3145736 | tf_op jit(solution)/shard_map/ppermute | solution.py:25
  82.0 1.7 copy-start
  84.7 31.1 %copy-start.4 = (f32[768,256]{1,0:T(8,128)}, f32[768,256]{1,0:T(8,128)S(1)}, u32[]{:S(2)}) copy-start(f32[768,256]{1,0:T(8,128)S(1)} %fusion.5) | copy-start | bytes 2359300
  85.0 28.2 %collective-permute-start.23 = (f32[768,256]{0,1:T(8,128)S(1)}, f32[768,256]{0,1:T(8,128)S(1)}, u32[]{:S(2)}, u32[]{:S(2)}) collective-permute-start(f32[768,256]{0,1:T(8,128)S(1)} %copy.14), channel_id=1, source_target_pairs={{0,4},{4,0},{8,12},{12,8},{16,20},{20,16},{24,28},{28,24},{32,36},... | collective-permute-start | bytes 2359304 | tf_op jit(solution)/shard_map/ppermute | solution.py:33
  100.2 8.6 %copy-start.1 = (bf16[2048,768]{1,0:T(8,128)(2,1)S(1)}, bf16[2048,768]{1,0:T(8,128)(2,1)}, u32[]{:S(2)}) copy-start(bf16[2048,768]{1,0:T(8,128)(2,1)} %copy-done) | copy-start | bytes 9437188
  100.2 34.7 %collective-permute-start.18 = (bf16[512,512]{1,0:T(8,128)(2,1)}, bf16[512,512]{1,0:T(8,128)(2,1)S(1)}, u32[]{:S(2)}, u32[]{:S(2)}) collective-permute-start(bf16[512,512]{1,0:T(8,128)(2,1)} %pad_maximum_fusion), channel_id=1, source_target_pairs={{0,4},{4,0},{8,12},{12,8},{16,20},{20,16},{24,28},{28,24},{32,36},... | collective-permute-start | bytes 1572872 | tf_op jit(solution)/shard_map/ppermute | solution.py:33
  101.6 14.9 %collective-permute-start.34 = (bf16[128,2048]{1,0:T(8,128)(2,1)S(1)}, bf16[128,2048]{1,0:T(8,128)(2,1)S(1)}, u32[]{:S(2)}, u32[]{:S(2)}) collective-permute-start(bf16[128,2048]{1,0:T(8,128)(2,1)S(1)} %slice.161), channel_id=1, source_target_pairs={{0,32},{4,36},{8,40},{12,44},{16,48},{20,52},{24,56},{28,60},{32,6... | collective-permute-start | bytes 1572872 | tf_op jit(solution)/shard_map/ppermute | solution.py:29
  102.7 14.3 %collective-permute-start.35 = (bf16[128,2048]{1,0:T(8,128)(2,1)S(1)}, bf16[128,2048]{1,0:T(8,128)(2,1)S(1)}, u32[]{:S(2)}, u32[]{:S(2)}) collective-permute-start(bf16[128,2048]{1,0:T(8,128)(2,1)S(1)} %slice.162), channel_id=1, source_target_pairs={{0,96},{4,100},{8,104},{12,108},{16,112},{20,116},{24,120},{28,124... | collective-permute-start | bytes 1572872 | tf_op jit(solution)/shard_map/ppermute | solution.py:29
  106.6 17.7 %collective-permute-start.42 = (bf16[128,2048]{1,0:T(8,128)(2,1)S(1)}, bf16[128,2048]{1,0:T(8,128)(2,1)S(1)}, u32[]{:S(2)}, u32[]{:S(2)}) collective-permute-start(bf16[128,2048]{1,0:T(8,128)(2,1)S(1)} %slice.166), channel_id=1, source_target_pairs={{0,8},{4,12},{8,16},{12,20},{16,24},{20,28},{24,0},{28,4},{32,40},... | collective-permute-start | bytes 1572872 | tf_op jit(solution)/shard_map/ppermute | solution.py:25
  113.2 3.2 %copy-start.5 = (f32[768,256]{0,1:T(8,128)}, f32[768,256]{0,1:T(8,128)S(1)}, u32[]{:S(2)}) copy-start(f32[768,256]{0,1:T(8,128)S(1)} %collective-permute-done.23) | copy-start | bytes 2359300
  113.2 12.0 %collective-permute-start.43 = (bf16[128,2048]{1,0:T(8,128)(2,1)S(1)}, bf16[128,2048]{1,0:T(8,128)(2,1)S(1)}, u32[]{:S(2)}, u32[]{:S(2)}) collective-permute-start(bf16[128,2048]{1,0:T(8,128)(2,1)S(1)} %slice.167), channel_id=1, source_target_pairs={{0,24},{4,28},{8,0},{12,4},{16,8},{20,12},{24,16},{28,20},{32,56},... | collective-permute-start | bytes 1572872 | tf_op jit(solution)/shard_map/ppermute | solution.py:25
  128.4 32.8 %all-to-all-start = ((bf16[8,4,64,512]{3,2,1,0:T(8,128)(2,1)}), bf16[8,4,64,512]{3,2,1,0:T(8,128)(2,1)S(1)}, u32[]{:S(2)}, u32[]{:S(2)}) async-start(bf16[8,4,64,512]{3,2,1,0:T(8,128)(2,1)} %bitcast.21), calls=%async_computation | async-start | bytes 4194304 | tf_op jit(solution)/shard_map/all_to_all | solution.py:290
  135.0 4.6 %copy-start.8 = (f32[64,512]{1,0:T(8,128)S(1)}, f32[64,512]{1,0:T(8,128)}, u32[]{:S(2)}) copy-start(f32[64,512]{1,0:T(8,128)} %param.11) | copy-start | bytes 393220
  137.3 2.0 %copy-start.6 = (bf16[2048,256]{1,0:T(8,128)(2,1)S(1)}, bf16[2048,256]{1,0:T(8,128)(2,1)}, u32[]{:S(2)}) copy-start(bf16[2048,256]{1,0:T(8,128)(2,1)} %param.9) | copy-start | bytes 3145732
  161.2 1.3 copy-start.3
where the time goes:
time: 168 us; the launch traced here: 167 us
  starting transfers between devices  71.4 us (43%)
  waiting for transfers between devices  34.8 us (21%)
  matrix products  21.7 us (13%)
  local copies, waits for them, and re-layouts  16.6 us (10%)
  other arithmetic  10.9 us (6%)
  Pallas kernels  10.5 us (6%)
    ppermute x16, starting transfers between devices, along_z(): return lax.ppermute(x, 'row', row_perm(step, 0, 0))  21 us
    all_to_all x1, waiting for transfers between devices, body(): lax.all_to_all(picked.reshape(8, slots, quarter, 2 * rank), ('row', 'col'...  20 us
    dot_general x14, matrix products, dot(): return jnp.dot(a, b, preferred_element_type=F32)  19.5 us
    ppermute x16, starting transfers between devices, along_y(): return lax.ppermute(x, 'row', row_perm(0, step, 0))  19 us
    ppermute x5, starting transfers between devices, other_core(): return lax.ppermute(x, 'row', row_perm(0, 0, 1))  14.8 us
    ppermute x7, starting transfers between devices, along_x(): return lax.ppermute(x, 'col', [(i, (i + step) % 4) for i in range(4)])  9.96 us
    ppermute x7, waiting for transfers between devices, along_x(): return lax.ppermute(x, 'col', [(i, (i + step) % 4) for i in range(4)])  7.75 us
    unnamed x42, local copies, waits for them, and re-layouts  7.64 us
  transfers between devices with their start and end apart: 45, of which 11 were waited for; matrix products, arithmetic and copies ran while one was open for 26% of the time, Pallas kernels for 2%

commit v1 on v0

v1 whole, which is shorter than its diff:
```python
import jax
import jax.numpy as jnp
from jax import lax
from jax.experimental import pallas as pl
from jax.experimental.pallas import tpu as pltpu
from jax.sharding import PartitionSpec as P

BF = jnp.bfloat16
F32 = jnp.float32


def row_at(z, y, core):
    return ((z % 4) * 4 + (y % 4)) * 2 + core


def other_core(x):
    pairs = [(row_at(z, y, k), row_at(z, y, 1 - k)) for z in range(4) for y in range(4) for k in range(2)]
    return lax.ppermute(x, "row", pairs)


def along_x(x, step):
    pairs = []
    for row in range(32):
        for c in range(4):
            d = step if row % 2 == 0 else -step
            pairs.append((row * 4 + c, row * 4 + (c + d) % 4))
    return lax.ppermute(x, ("row", "col"), pairs)


def hop(x, level, step):
    pairs = []
    for z in range(4):
        for y in range(4):
            for k in range(2):
                dz = step if k != level else 0
                dy = step if k == level else 0
                pairs.append((row_at(z, y, k), row_at(z + dz, y + dy, k)))
    return lax.ppermute(x, "row", pairs)


def slot_of(distance):
    return jnp.where(distance % 2 == 0, distance // 2 * 3, jnp.where(distance == 3, 1, 2))


DISTANCE = (0, 3, 1, 2)
VMEM = pl.BlockSpec(memory_space=pltpu.VMEM)
SMEM = pl.BlockSpec(memory_space=pltpu.SMEM)
ANY = pl.BlockSpec(memory_space=pl.ANY)
HBM = pl.BlockSpec(memory_space=pltpu.HBM)


def unit(size):
    rows = lax.broadcasted_iota(jnp.int32, (size, size), 0)
    cols = lax.broadcasted_iota(jnp.int32, (size, size), 1)
    return jnp.where(rows == cols, 1.0, 0.0).astype(BF)


def flip(x):
    return lax.dot_general(
        unit(x.shape[1]), x, (((1,), (1,)), ((), ())), preferred_element_type=F32
    )


def copy_all(pairs, sems, base=0):
    copies = [pltpu.make_async_copy(src, dst, sems.at[base + i]) for i, (src, dst) in enumerate(pairs)]
    for copy in copies:
        copy.start()
    return copies


def solve_kernel(where, *refs):
    pieces, (right0, right1, right2), (out, *thin), (whole, turned) = (
        refs[:4],
        refs[4:7],
        refs[7:12],
        refs[12:],
    )
    piece = out.shape[0]
    width = whole.shape[1] // 16
    on_zero = where[3] == 0
    for slow in range(4):
        for fast in range(4):
            dz = jnp.where(on_zero, DISTANCE[slow], DISTANCE[fast])
            dy = jnp.where(on_zero, DISTANCE[fast], DISTANCE[slow])
            chip = lax.rem(where[0] + dz, 4) * 4 + lax.rem(where[1] + dy, 4)
            start = pl.multiple_of(chip * width, width)
            whole[:, pl.ds(start, width)] = pieces[slow][fast * piece : (fast + 1) * piece, :]
    rank = right0.shape[1]
    for n, right in enumerate((right0, right1, right2)):
        out[:, n * rank : (n + 1) * rank] = jnp.dot(
            whole[...], right[...], preferred_element_type=F32
        ).astype(BF)
    turned[...] = flip(out[:, : 2 * rank]).astype(BF)
    quarter = rank // 4
    half = quarter // 2
    for step in range(4):
        q = lax.rem(where[2] + jnp.where(on_zero, step, 4 - step), 4)
        for h in range(2):
            for a in range(2):
                start = pl.multiple_of(a * rank + q * quarter + h * half, half)
                at = (2 * h + a) * half
                thin[step][at : at + half, :] = turned[pl.ds(start, half), :]


def solve(where, pieces, rights):
    piece = pieces[0].shape[0] // 4
    tile_size, rank = rights[0].shape
    return pl.pallas_call(
        solve_kernel,
        out_shape=[jax.ShapeDtypeStruct((piece, 3 * rank), BF)]
        + [jax.ShapeDtypeStruct((rank // 2, piece), BF)] * 4,
        in_specs=[SMEM] + [VMEM] * 7,
        out_specs=[VMEM] * 5,
        scratch_shapes=[
            pltpu.VMEM((piece, tile_size), BF),
            pltpu.VMEM((2 * rank, piece), BF),
        ],
        compiler_params=pltpu.CompilerParams(vmem_limit_bytes=16 * 2**20),
        cost_estimate=pl.CostEstimate(
            flops=2 * piece * tile_size * 3 * rank, bytes_accessed=0, transcendentals=0
        ),
        name="solve",
    )(where, *pieces, *rights)


def multiply_kernel(*refs):
    count = len(refs) - 4
    whole, pieces, (out, held, sems) = refs[0], refs[1 : 1 + count], refs[1 + count :]
    rows = pieces[0].shape[0]
    copies = copy_all(
        [(p, held.at[pl.ds(i * rows, rows)]) for i, p in enumerate(pieces)], sems
    )
    for copy in copies:
        copy.wait()
    out[...] = jnp.dot(held[...], whole[...], preferred_element_type=F32)


def multiply(whole, pieces):
    depth, width = whole.shape
    rows = pieces[0].shape[0]
    count = len(pieces)
    return pl.pallas_call(
        multiply_kernel,
        out_shape=jax.ShapeDtypeStruct((count * rows, width), F32),
        in_specs=[VMEM] + [ANY] * count,
        out_specs=VMEM,
        scratch_shapes=[
            pltpu.VMEM((count * rows, depth), BF),
            pltpu.SemaphoreType.DMA((count,)),
        ],
        compiler_params=pltpu.CompilerParams(vmem_limit_bytes=16 * 2**20),
        cost_estimate=pl.CostEstimate(
            flops=2 * count * rows * depth * width, bytes_accessed=0, transcendentals=0
        ),
        name="multiply",
    )(whole, *pieces)


def pick_kernel(
    places, mats, whole, piece0, piece1, early0, early1, out, late0, late1, heads, staged, sems
):
    done = early0.shape[0]
    copies = copy_all(
        [(early0, late0.at[pl.ds(0, done)]), (early1, late1.at[pl.ds(0, done)])], sems, 2
    )
    late0[done:, :] = jnp.dot(piece0[...], whole[...], preferred_element_type=F32)
    late1[done:, :] = jnp.dot(piece1[...], whole[...], preferred_element_type=F32)
    for copy in copies:
        copy.wait()
    products = (late0, late1)
    rank = mats.shape[1]
    half = rank // 8
    count = places.shape[1]
    leaving = []
    for a in range(2):
        at = [pl.ds(pl.multiple_of(places[a, i] * half, half), half) for i in range(count)]
        for i in range(count):
            for h in range(2):
                rows = slice((2 * i + h) * half, (2 * i + h + 1) * half)
                heads[rows, :] = products[h][at[i], 2 * rank :].astype(BF)
        low = jnp.dot(heads[...], mats[a], preferred_element_type=F32)
        for i in range(count):
            for h in range(2):
                mine = low[(2 * i + h) * half : (2 * i + h + 1) * half, :]
                direct = products[h][at[i], a * rank : (a + 1) * rank]
                rows = slice(h * half, (h + 1) * half)
                staged[a, i, rows, :rank] = (mine[:, :rank] + direct).astype(BF)
                staged[a, i, rows, rank:] = mine[:, rank:].astype(BF)
        leaving += copy_all([(staged.at[a], out.at[a])], sems, a)
    for copy in leaving:
        copy.wait()


def pick(places, mats, whole, piece0, piece1, early0, early1):
    count = places.shape[1]
    rank = mats.shape[1]
    shape = (2, count, rank // 4, 2 * rank)
    full = (early0.shape[0] + piece0.shape[0], early0.shape[1])
    return pl.pallas_call(
        pick_kernel,
        out_shape=jax.ShapeDtypeStruct(shape, BF),
        in_specs=[SMEM] + [VMEM] * 6,
        out_specs=HBM,
        scratch_shapes=[
            pltpu.VMEM(full, F32),
            pltpu.VMEM(full, F32),
            pltpu.VMEM((count * rank // 4, rank), BF),
            pltpu.VMEM(shape, BF),
            pltpu.SemaphoreType.DMA((4,)),
        ],
        compiler_params=pltpu.CompilerParams(vmem_limit_bytes=28 * 2**20),
        cost_estimate=pl.CostEstimate(
            flops=2**30, bytes_accessed=0, transcendentals=0
        ),
        name="pick",
    )(places, mats, whole, piece0, piece1, early0, early1)


def couple_kernel(*refs):
    parts, whole, out = refs[:4], refs[4], refs[5]
    rank = out.shape[1]
    size = parts[0].shape[0]
    for i, part in enumerate(parts):
        whole[i * size : (i + 1) * size, :] = part[...]
        term = lax.dot_general(
            part[...], part[:, 2 * rank :], (((0,), (0,)), ((), ())), preferred_element_type=F32
        )
        out[...] = term if i == 0 else out[...] + term


def couple(parts):
    size, width = parts[0].shape
    return pl.pallas_call(
        couple_kernel,
        out_shape=[
            jax.ShapeDtypeStruct((4 * size, width), BF),
            jax.ShapeDtypeStruct((width, width // 3), F32),
        ],
        in_specs=[VMEM] * 4,
        out_specs=[VMEM] * 2,
        compiler_params=pltpu.CompilerParams(vmem_limit_bytes=16 * 2**20),
        cost_estimate=pl.CostEstimate(
            flops=2 * 4 * size * width * width // 3, bytes_accessed=0, transcendentals=0
        ),
        name="couple",
    )(*parts)


def split(x):
    high = x.astype(BF)
    return high, (x - high.astype(F32)).astype(BF)


def by_rows(a, b):
    return lax.dot_general(a, b, (((1,), (1,)), ((), ())), preferred_element_type=F32)


def finish_kernel(core, small, other, mats, coupling, gram):
    rank = small.shape[1]
    last = slice(2 * rank, 3 * rank)
    on_zero = core[0] == 0
    for a in range(2):
        rows = slice(a * rank, (a + 1) * rank)
        high, low = split(small[rows, :])
        gram_high, gram_low = split(other[last, :])
        weight = by_rows(gram_high, high) + by_rows(gram_high, low) + by_rows(gram_low, high)
        mats[a, :, :rank] = jnp.where(on_zero, weight, 0.0).astype(BF)
        mats[a, :, rank:] = (-flip(other[rows, :].astype(BF))).astype(BF)
    coupling[...] = jnp.where(on_zero, small[:rank, :], other[rank : 2 * rank, :])
    gram[...] = jnp.where(on_zero, small[last, :], other[last, :])


def finish(core, small, other):
    rank = small.shape[1]
    return pl.pallas_call(
        finish_kernel,
        out_shape=[
            jax.ShapeDtypeStruct((2, rank, 2 * rank), BF),
            jax.ShapeDtypeStruct((rank, rank), F32),
            jax.ShapeDtypeStruct((rank, rank), F32),
        ],
        in_specs=[SMEM] + [VMEM] * 2,
        out_specs=[VMEM] * 3,
        compiler_params=pltpu.CompilerParams(vmem_limit_bytes=8 * 2**20),
        cost_estimate=pl.CostEstimate(flops=2**28, bytes_accessed=0, transcendentals=0),
        name="finish",
    )(core, small, other)


def update_kernel(gram, band, piece, before, after):
    gram_high, gram_low = split(gram[...])
    middle = jnp.dot(band[...], gram_high, preferred_element_type=F32) + jnp.dot(
        band[...], gram_low, preferred_element_type=F32
    )
    high, low = split(middle)
    after[...] = before[...] - (by_rows(high, piece[...]) + by_rows(low, piece[...]))


def update(gram, band, piece, before):
    return pl.pallas_call(
        update_kernel,
        out_shape=jax.ShapeDtypeStruct(before.shape, F32),
        in_specs=[VMEM] * 4,
        out_specs=VMEM,
        compiler_params=pltpu.CompilerParams(vmem_limit_bytes=8 * 2**20),
        cost_estimate=pl.CostEstimate(flops=2**26, bytes_accessed=0, transcendentals=0),
        name="update",
    )(gram, band, piece, before)


def settle_kernel(landed, out):
    rank = landed.shape[4] // 2
    for p in range(2):
        x = landed[p, :, pl.program_id(0)].reshape(rank, 2 * rank)
        direct = flip(x[:, :rank])
        crossed = flip(x[:, rank:])
        cols = slice(p * rank, (p + 1) * rank)
        out[0, :rank, cols] = direct if p == 0 else crossed
        out[0, rank:, cols] = crossed if p == 0 else direct


def settle(landed):
    slots, width = landed.shape[2], landed.shape[4]
    return pl.pallas_call(
        settle_kernel,
        grid=(slots,),
        out_shape=jax.ShapeDtypeStruct((slots, width, width), F32),
        in_specs=[VMEM],
        out_specs=pl.BlockSpec((1, width, width), lambda s: (s, 0, 0)),
        compiler_params=pltpu.CompilerParams(vmem_limit_bytes=16 * 2**20),
        cost_estimate=pl.CostEstimate(flops=2**30, bytes_accessed=0, transcendentals=0),
        name="settle",
    )(landed)


def join_kernel(*refs):
    pieces, outs = refs[:4], refs[4:]
    rows = pieces[0].shape[0] // len(outs)
    for n, out in enumerate(outs):
        for i in range(4):
            out[i * rows : (i + 1) * rows, :] = pieces[i][n * rows : (n + 1) * rows, :]


def join(pieces, count):
    rows, cols = pieces[0].shape
    return pl.pallas_call(
        join_kernel,
        out_shape=[jax.ShapeDtypeStruct((4 * rows // count, cols), BF)] * count,
        in_specs=[VMEM] * 4,
        out_specs=[VMEM] * count,
        compiler_params=pltpu.CompilerParams(vmem_limit_bytes=8 * 2**20),
        cost_estimate=pl.CostEstimate(
            flops=0, bytes_accessed=0, transcendentals=0
        ),
        name="join",
    )(*pieces)


def direct(x, level):
    return [x, hop(x, level, 1), hop(x, level, -1), hop(x, level, 2)]


def sides(x, level):
    return hop(x, level, 1), hop(x, level, -1)


def body(panel_v, head_v, head_u, diag_inverse, diag_next, ranks, trail_col):
    tile_size = panel_v.shape[2]
    rank = panel_v.shape[3]
    piece = tile_size // 4
    quarter = rank // 4
    col_id = lax.axis_index("col")
    row_id = lax.axis_index("row")
    core = row_id % 2
    my_y = (row_id // 2) % 4
    my_z = row_id // 8
    on_zero = core == 0

    def pick_core(zero, one):
        return jnp.where(on_zero, zero, one)

    inv_mine = pick_core(diag_inverse[0], diag_inverse[1])
    inv_theirs = other_core(pick_core(diag_inverse[1], diag_inverse[0]))
    inv_pair = jnp.concatenate(
        [pick_core(inv_mine, inv_theirs), pick_core(inv_theirs, inv_mine)], axis=1
    )
    column = join(direct(inv_pair, 0), 1)[0]
    panel_other = other_core(panel_v)
    column, panel_late, ranks, trail_col = lax.optimization_barrier((column, panel_v, ranks, trail_col))
    inverse = direct(column, 1)
    own_core = core.astype(jnp.int32)[None]
    cols = jnp.arange(rank)[None, :]
    tiles = trail_col[0]
    slots = tiles.shape[1]
    numbers = jnp.concatenate([ranks[:, 0], tiles.reshape(-1)])
    numbers_other = other_core(numbers.astype(F32)[None])[0].astype(jnp.int32)

    def masked(panels, limits):
        kept = [jnp.where(cols < limits[p], panels[p, 0], jnp.zeros((), BF)) for p in range(2)]
        return pick_core(*kept)

    mine = masked(panel_late, numbers)
    theirs = masked(panel_other, numbers_other)
    rights = [pick_core(mine, theirs), pick_core(theirs, mine), pick_core(head_v, head_u)]
    where = jnp.stack([my_z, my_y, col_id, core]).astype(jnp.int32)
    solved, *thin_parts = solve(where, inverse, rights)

    thin_before = along_x(thin_parts[1], 1)
    thin_after = along_x(thin_parts[3], -1)
    thin_opposite = along_x(thin_parts[2], 2)
    thin_before, thin_after, sent = lax.optimization_barrier((thin_before, thin_after, solved))
    thin = jnp.concatenate([thin_parts[0], thin_before, thin_after, thin_opposite], axis=1)
    quarters = thin.reshape(2, quarter, tile_size)
    line0, line1 = (join(direct(quarters[h], 0), 1)[0] for h in range(2))
    x_before, x_after, x_opposite = along_x(sent, 1), along_x(sent, -1), along_x(sent, 2)
    line1, x_before, x_after, x_opposite = lax.optimization_barrier(
        (line1, x_before, x_after, x_opposite)
    )
    before0, after0 = lax.optimization_barrier(sides(line0, 1))
    before1, after1 = lax.optimization_barrier(sides(line1, 1))
    gathered0 = [line0, before0, after0, hop(before0, 1, 1)]
    whole, small = couple([solved, x_before, x_after, x_opposite])
    early0 = multiply(whole, gathered0[:3])
    after1, small, early0 = lax.optimization_barrier((after1, small, early0))
    gathered1 = [line1, before1, after1, hop(after1, 1, -1)]
    small_other = other_core(small)
    mats, coupling, gram_h = finish(own_core, small, small_other)

    late, _ = lax.optimization_barrier((solved, gathered0[1]))
    passed = other_core(
        jnp.concatenate(
            [
                pick_core(late[:, rank : 2 * rank], late[:, :rank]),
                late[:, 2 * rank :],
            ],
            axis=1,
        )
    )
    own = pick_core(late[:, :rank], late[:, rank : 2 * rank])
    factor_first = pick_core(own, passed[:, :rank])
    factor_second = pick_core(passed[:, :rank], own)
    head_image = pick_core(passed[:, rank:], late[:, 2 * rank :])

    other_tiles = numbers_other[2:].reshape(tiles.shape)
    j = jnp.stack([pick_core(tiles, other_tiles), pick_core(other_tiles, tiles)]).reshape(2, -1)
    sy = slot_of(((j // 2) % 4 - my_y) % 4)
    sz = slot_of((j // 8 - my_z) % 4)
    places = (pick_core(sz, sy) * 4 + pick_core(sy, sz)) * 2 + j % 2
    early1 = multiply(whole, gathered1[:3])
    picked = pick(places, mats, whole, gathered0[3], gathered1[3], early0, early1)
    upper, _ = lax.optimization_barrier((head_u, picked))
    band = tile_size // 32
    upper_band = lax.dynamic_slice_in_dim(upper, row_id * band, band, 0)
    upper_piece = lax.dynamic_slice_in_dim(upper, col_id * piece, piece, 0)
    next_diagonal = update(gram_h, upper_band, upper_piece, diag_next)
    chip_groups = [[(2 * chip + m) * 4 + c for m in range(2) for c in range(4)] for chip in range(16)]
    landed = lax.all_to_all(
        picked.reshape(8, slots, quarter, 2 * rank),
        ("row", "col"),
        0,
        0,
        axis_index_groups=chip_groups,
        tiled=True,
    )
    cores = settle(landed.reshape(2, 4, slots, quarter, 2 * rank))
    trail_cores = cores.reshape(1, 1, slots, 2 * rank, 2 * rank)
    return (
        factor_first[None],
        factor_second[None],
        coupling[None],
        head_image,
        next_diagonal,
        trail_cores,
    )


def solution(mesh):
    return jax.shard_map(
        body,
        mesh=mesh,
        in_specs=(
            P(None, "row", None, None),
            P(),
            P(),
            P(None, "col", "row"),
            P("row", "col"),
            P(None, "row"),
            P("row", None, None),
        ),
        out_specs=(
            P("row", "col", None),
            P("row", "col", None),
            P("row", None, None),
            P("col", None),
            P("row", "col"),
            P("row", "col", None, None, None),
        ),
        check_vma=False,
    )
```

time: 168 us -> 159 us (0.946)
  waiting for transfers between devices: 34.8 us -> 64.6 us
  starting transfers between devices: 71.4 us -> 46.5 us
  matrix products: 21.7 us -> 0 us
  Pallas kernels: 10.5 us -> 25.2 us
  local copies, waits for them, and re-layouts: 16.6 us -> 13.1 us
  other arithmetic: 10.9 us -> 8.39 us
    ppermute x44 -> x29, waiting for transfers between devices: 14.8 us -> 46.3 us  [the longest x18 24.1 us: hop(): return lax.ppermute(x, 'row', pairs)]
    ppermute x44 -> x29, starting transfers between devices: 64.8 us -> 41.8 us  [the longest x18 27.6 us: hop(): return lax.ppermute(x, 'row', pairs)]
    dot_general x17 -> x0, matrix products: 21.7 us -> none  [the longest x14 19.5 us: dot(): return jnp.dot(a, b, preferred_element_type=F32)]
    pallas_call x1 -> x9, Pallas kernels: 2.58 us -> 18.3 us  [the longest x2 8.05 us: multiply(): pl.pallas_call(multiply_kernel, out_shape=jax.ShapeDtypeStruct((count * r...]
    slice x19 -> x5, local copies, waits for them, and re-layouts: 5.56 us -> 2.17 us  [the longest x2 1.16 us: masked(): limits[p]]
    lt x0 -> x2, other arithmetic: none -> 2.59 us  [masked(): cols < limits[p]]
    select_n x9 -> x7, other arithmetic: 6.64 us -> 4.64 us  [pick_core(): return jnp.where(on_zero, zero, one)]
    all_to_all x1, starting transfers between devices: 6.58 us -> 4.74 us  [body(): lax.all_to_all(picked.reshape(8, slots, quarter, 2 * rank), ('row', 'col'...]
  transfers between devices with their start and end apart: 45 -> 30, of which waited for: 11 -> 18; matrix products, arithmetic and copies ran while one was open for 26% -> 8% of each run, Pallas kernels for 2% -> 9%
where the time goes in v1:
time: 159 us
  waiting for transfers between devices  64.6 us (41%)
  starting transfers between devices  46.5 us (29%)
  Pallas kernels  25.2 us (16%)
  local copies, waits for them, and re-layouts  13.1 us (8%)
  other arithmetic  8.39 us (5%)
    ppermute x18, starting transfers between devices, hop(): return lax.ppermute(x, 'row', pairs)  27.6 us
    ppermute x18, waiting for transfers between devices, hop(): return lax.ppermute(x, 'row', pairs)  24.1 us
    all_to_all x1, waiting for transfers between devices, body(): lax.all_to_all(picked.reshape(8, slots, quarter, 2 * rank), ('row', 'col'...  18.3 us
    ppermute x6, waiting for transfers between devices, along_x(): return lax.ppermute(x, ('row', 'col'), pairs)  17.4 us
    unnamed x37, local copies, waits for them, and re-layouts  8.87 us
    pallas_call x2, Pallas kernels, multiply(): pl.pallas_call(multiply_kernel, out_shape=jax.ShapeDtypeStruct((count * r...  8.05 us
    ppermute x5, starting transfers between devices, other_core(): return lax.ppermute(x, 'row', pairs)  7.37 us
    ppermute x6, starting transfers between devices, along_x(): return lax.ppermute(x, ('row', 'col'), pairs)  6.8 us
  transfers between devices with their start and end apart: 30, of which 18 were waited for; matrix products, arithmetic and copies ran while one was open for 8% of the time, Pallas kernels for 9%

profile of v1, /device:TPU:1, one launch (start us, length us, event | category | flops | bytes accessed | tf_op | source)
XLA Modules:
  0.0 158.8 jit_solution(3866017916882259309)
XLA Ops:
  0.6 1.5 collective-permute-start.8
  2.1 0.9 fusion.10
  3.5 2.6 %collective-permute-done = bf16[512,64]{1,0:T(8,128)(2,1)S(1)} collective-permute-done((bf16[512,64]{1,0:T(8,128)(2,1)S(1)}, bf16[512,64]{1,0:T(8,128)(2,1)S(1)}, u32[]{:S(2)}, u32[]{:S(2)}) %collective-permute-start) | collective-permute-done | bytes 65568 | tf_op jit(solution)/shard_map/ppermute | solution.py:18
  6.3 1.8 %collective-permute-start.1 = (bf16[512,128]{1,0:T(8,128)(2,1)S(1)}, bf16[512,128]{1,0:T(8,128)(2,1)S(1)}, u32[]{:S(2)}, u32[]{:S(2)}) collective-permute-start(bf16[512,128]{1,0:T(8,128)(2,1)S(1)} %pad_maximum_fusion.1.refs_0_), channel_id=1, source_target_pairs={{0,8},{4,36},{8,16},{12,44},{16,24},{20,52},{24,0},{28,60},{32,40}... | collective-permute-start | bytes 393224 | tf_op jit(solution)/shard_map/ppermute | solution.py:38
  8.1 2.2 %collective-permute-start.2 = (bf16[512,128]{1,0:T(8,128)(2,1)S(1)}, bf16[512,128]{1,0:T(8,128)(2,1)S(1)}, u32[]{:S(2)}, u32[]{:S(2)}) collective-permute-start(bf16[512,128]{1,0:T(8,128)(2,1)S(1)} %pad_maximum_fusion.1.refs_0_), channel_id=1, source_target_pairs={{0,24},{4,100},{8,0},{12,108},{16,8},{20,116},{24,16},{28,124},{32... | collective-permute-start | bytes 393224 | tf_op jit(solution)/shard_map/ppermute | solution.py:38
  10.3 1.2 collective-permute-start.3
  11.8 0.8 collective-permute-done.1.refs_1_
  12.6 3.3 %collective-permute-done.3.refs_3_ = bf16[512,128]{1,0:T(8,128)(2,1)S(1)} collective-permute-done((bf16[512,128]{1,0:T(8,128)(2,1)S(1)}, bf16[512,128]{1,0:T(8,128)(2,1)S(1)}, u32[]{:S(2)}, u32[]{:S(2)}) %collective-permute-start.3) | collective-permute-done | bytes 131104 | tf_op jit(solution)/shard_map/ppermute | solution.py:38
  15.9 1.1 collective-permute-start.4
  17.0 1.7 %collective-permute-start.5 = (bf16[2048,128]{1,0:T(8,128)(2,1)S(1)}, bf16[2048,128]{1,0:T(8,128)(2,1)}, u32[]{:S(2)}, u32[]{:S(2)}) collective-permute-start(bf16[2048,128]{1,0:T(8,128)(2,1)S(1)} %join.3.refs_0_), channel_id=1, source_target_pairs={{0,96},{4,28},{8,104},{12,4},{16,112},{20,12},{24,120},{28,20},{32... | collective-permute-start | bytes 1572872 | tf_op jit(solution)/shard_map/ppermute | solution.py:38
  18.7 1.4 collective-permute-start.6
  20.3 2.5 %collective-permute-start.7 = (f32[1,18]{1,0:T(1,128)S(1)}, f32[1,18]{1,0:T(1,128)S(1)}, u32[]{:S(2)}, u32[]{:S(2)}) collective-permute-start(f32[1,18]{1,0:T(1,128)S(1)} %add_convert_fusion), channel_id=1, source_target_pairs={{0,4},{4,0},{8,12},{12,8},{16,20},{20,16},{24,28},{28,24},{32,36},... | collective-permute-start | bytes 224 | tf_op jit(solution)/shard_map/ppermute | solution.py:18
  22.7 0.6 fusion.12
  23.3 1.3 iota_compare_fusion.2
  24.6 0.6 fusion.11
  25.2 1.3 iota_compare_fusion
  26.5 2.5 %broadcast_select_fusion.1 = (bf16[2048,256]{1,0:T(8,128)(2,1)S(1)}, bf16[2048,256]{1,0:T(8,128)(2,1)S(1)}) fusion(pred[]{:T(512)S(6)} %eq.25, bf16[2,1,2048,256]{3,2,1,0:T(8,128)(2,1)} %param.7, pred[256]{0:T(512)(128)(4,1)S(1)} %get-tuple-element.87, pred[256]{0:T(512)(128)(4,1)S(1)} %get-tuple-element.88, ...), kind=kLoop, calls=%fused_computation.9 | loop fusion | flops 4194304 | bytes 6292481 | tf_op jit(solution)/shard_map/jit(_where)/select_n | solution.py:380
  29.0 0.8 copy-done.10
  29.8 0.6 collective-permute-done.5.refs_2_
  30.4 1.8 %collective-permute-done.6.refs_3_ = bf16[2048,128]{1,0:T(8,128)(2,1)} collective-permute-done((bf16[2048,128]{1,0:T(8,128)(2,1)S(1)}, bf16[2048,128]{1,0:T(8,128)(2,1)}, u32[]{:S(2)}, u32[]{:S(2)}) %collective-permute-start.6) | collective-permute-done | bytes 524320 | tf_op jit(solution)/shard_map/ppermute | solution.py:38
  32.2 1.0 copy-done.11
  33.3 3.9 %solve.1 = (bf16[512,768]{1,0:T(8,128)(2,1)S(1)}, bf16[128,512]{1,0:T(8,128)(2,1)S(1)}, bf16[128,512]{1,0:T(8,128)(2,1)S(1)}, bf16[128,512]{1,0:T(8,128)(2,1)S(1)}, bf16[128,512]{1,0:T(8,128)(2,1)S(1)}) custom-call(s32[4]{0:T(128)S(1)} %pad_add_fusion.1.where, bf16[2048,128]{1,0:T(8,128)(2,1)S(1)} %join.3.refs_0_, bf16[2048,128]{1,0:T(8,128)(2,1)S(1)} %copy-done.11, ...), custom_call_target="tpu_custom_call" | custom-call | flops 1610612736 | tf_op jit(solution)/shard_map/solve/pallas_call | solution.py:108
  37.2 2.5 %collective-permute-start.9 = (bf16[128,512]{1,0:T(8,128)(2,1)S(1)}, bf16[128,512]{1,0:T(8,128)(2,1)S(1)}, u32[]{:S(2)}, u32[]{:S(2)}) collective-permute-start(bf16[128,512]{1,0:T(8,128)(2,1)S(1)} %get-tuple-element.42), channel_id=1, source_target_pairs={{0,1},{1,2},{2,3},{3,0},{4,7},{5,4},{6,5},{7,6},{8,9},{9,10},{10,1... | collective-permute-start | bytes 393224 | tf_op jit(solution)/shard_map/ppermute | solution.py:27
  39.7 1.7 %collective-permute-start.11 = (bf16[128,512]{1,0:T(8,128)(2,1)S(1)}, bf16[128,512]{1,0:T(8,128)(2,1)S(1)}, u32[]{:S(2)}, u32[]{:S(2)}) collective-permute-start(bf16[128,512]{1,0:T(8,128)(2,1)S(1)} %get-tuple-element.46), channel_id=1, source_target_pairs={{0,2},{1,3},{2,0},{3,1},{4,6},{5,7},{6,4},{7,5},{8,10},{9,11},{10,... | collective-permute-start | bytes 393224 | tf_op jit(solution)/shard_map/ppermute | solution.py:27
  41.7 5.7 %collective-permute-done.10 = bf16[128,512]{1,0:T(8,128)(2,1)S(1)} collective-permute-done((bf16[128,512]{1,0:T(8,128)(2,1)S(1)}, bf16[128,512]{1,0:T(8,128)(2,1)S(1)}, u32[]{:S(2)}, u32[]{:S(2)}) %collective-permute-start.10) | collective-permute-done | bytes 131104 | tf_op jit(solution)/shard_map/ppermute | solution.py:27
  47.8 2.4 %collective-permute-start.13 = (bf16[64,2048]{1,0:T(8,128)(2,1)S(1)}, bf16[64,2048]{1,0:T(8,128)(2,1)S(1)}, u32[]{:S(2)}, u32[]{:S(2)}) collective-permute-start(bf16[64,2048]{1,0:T(8,128)(2,1)S(1)} %get-tuple-element.74.refs_0_), channel_id=1, source_target_pairs={{0,24},{4,100},{8,0},{12,108},{16,8},{20,116},{24,16},{28,124},{32... | collective-permute-start | bytes 786440 | tf_op jit(solution)/shard_map/ppermute | solution.py:38
  50.2 1.3 collective-permute-start.21
  51.7 1.1 collective-permute-start.23
  52.7 1.2 collective-permute-done.12.refs_1_
  54.2 0.8 collective-permute-start.18
  55.0 5.8 %collective-permute-done.14.refs_3_ = bf16[64,2048]{1,0:T(8,128)(2,1)S(1)} collective-permute-done((bf16[64,2048]{1,0:T(8,128)(2,1)S(1)}, bf16[64,2048]{1,0:T(8,128)(2,1)S(1)}, u32[]{:S(2)}, u32[]{:S(2)}) %collective-permute-start.14) | collective-permute-done | bytes 262176 | tf_op jit(solution)/shard_map/ppermute | solution.py:38
  60.8 0.4 collective-permute-start.19
  61.2 2.6 %collective-permute-done.18.refs_1_ = bf16[64,2048]{1,0:T(8,128)(2,1)S(1)} collective-permute-done((bf16[64,2048]{1,0:T(8,128)(2,1)S(1)}, bf16[64,2048]{1,0:T(8,128)(2,1)S(1)}, u32[]{:S(2)}, u32[]{:S(2)}) %collective-permute-start.18) | collective-permute-done | bytes 262176 | tf_op jit(solution)/shard_map/ppermute | solution.py:38
  64.1 2.2 %collective-permute-done.19.refs_2_ = bf16[64,2048]{1,0:T(8,128)(2,1)S(1)} collective-permute-done((bf16[64,2048]{1,0:T(8,128)(2,1)S(1)}, bf16[64,2048]{1,0:T(8,128)(2,1)S(1)}, u32[]{:S(2)}, u32[]{:S(2)}) %collective-permute-start.19) | collective-permute-done | bytes 262176 | tf_op jit(solution)/shard_map/ppermute | solution.py:38
  66.3 2.6 %collective-permute-start.15 = (bf16[256,2048]{1,0:T(8,128)(2,1)S(1)}, bf16[256,2048]{1,0:T(8,128)(2,1)}, u32[]{:S(2)}, u32[]{:S(2)}) collective-permute-start(bf16[256,2048]{1,0:T(8,128)(2,1)S(1)} %join.4.refs_1_), channel_id=1, source_target_pairs={{0,32},{4,12},{8,40},{12,20},{16,48},{20,28},{24,56},{28,4},{32,64... | collective-permute-start | bytes 3145736 | tf_op jit(solution)/shard_map/ppermute | solution.py:38
  68.9 1.6 %collective-permute-done.20.refs_3_ = bf16[64,2048]{1,0:T(8,128)(2,1)S(1)} collective-permute-done((bf16[64,2048]{1,0:T(8,128)(2,1)S(1)}, bf16[64,2048]{1,0:T(8,128)(2,1)S(1)}, u32[]{:S(2)}, u32[]{:S(2)}) %collective-permute-start.20) | collective-permute-done | bytes 262176 | tf_op jit(solution)/shard_map/ppermute | solution.py:38
  70.5 1.8 %collective-permute-start.16 = (bf16[256,2048]{1,0:T(8,128)(2,1)S(1)}, bf16[256,2048]{1,0:T(8,128)(2,1)S(1)}, u32[]{:S(2)}, u32[]{:S(2)}) collective-permute-start(bf16[256,2048]{1,0:T(8,128)(2,1)S(1)} %join.4.refs_1_), channel_id=1, source_target_pairs={{0,96},{4,28},{8,104},{12,4},{16,112},{20,12},{24,120},{28,20},{32... | collective-permute-start | bytes 3145736 | tf_op jit(solution)/shard_map/ppermute | solution.py:38
  72.4 1.0 collective-permute-done.22.refs_2_
  73.4 10.5 %collective-permute-done.23.refs_3_ = bf16[512,768]{1,0:T(8,128)(2,1)S(1)} collective-permute-done((bf16[512,768]{1,0:T(8,128)(2,1)S(1)}, bf16[512,768]{1,0:T(8,128)(2,1)S(1)}, u32[]{:S(2)}, u32[]{:S(2)}) %collective-permute-start.23) | collective-permute-done | bytes 786464 | tf_op jit(solution)/shard_map/ppermute | solution.py:27
  83.9 6.7 %collective-permute-start.24 = (bf16[256,2048]{1,0:T(8,128)(2,1)S(1)}, bf16[256,2048]{1,0:T(8,128)(2,1)S(1)}, u32[]{:S(2)}, u32[]{:S(2)}) collective-permute-start(bf16[256,2048]{1,0:T(8,128)(2,1)S(1)} %join.5.refs_1_), channel_id=1, source_target_pairs={{0,32},{4,12},{8,40},{12,20},{16,48},{20,28},{24,56},{28,4},{32,64... | collective-permute-start | bytes 3145736 | tf_op jit(solution)/shard_map/ppermute | solution.py:38
  90.6 2.0 %couple.1 = (bf16[2048,768]{1,0:T(8,128)(2,1)S(1)}, f32[768,256]{1,0:T(8,128)}) custom-call(bf16[512,768]{1,0:T(8,128)(2,1)S(1)} %get-tuple-element.49.refs_0_, bf16[512,768]{1,0:T(8,128)(2,1)S(1)} %collective-permute-done.21.refs_1_, bf16[512,768]{1,0:T(8,128)(2,1)S(1)} %collective-permute-done.22.refs_2_, bf16[512,768]{1,0:T(8,128)(2,1)S(1)} %collective-permute-done.23.refs_3_), custom_call_target="tpu_custom_call" | custom-call | flops 805306368 | tf_op jit(solution)/shard_map/couple/pallas_call | solution.py:233
  92.7 1.5 collective-permute-start.27
  94.2 3.9 %multiply.2.early0 = f32[768,768]{1,0:T(8,128)S(1)} custom-call(bf16[2048,768]{1,0:T(8,128)(2,1)S(1)} %get-tuple-element.56.refs_0_.whole, bf16[256,2048]{1,0:T(8,128)(2,1)S(1)} %join.4.refs_1_, bf16[256,2048]{1,0:T(8,128)(2,1)} %collective-permute-done.15.refs_2_, bf16[256,2048]{1,0:T(8,128)(2,1)S(1)} %collective-permute-done.16.refs_3_), custom_call_target="tpu_custom_call" | custom-call | flops 2415919104 | tf_op jit(solution)/shard_map/multiply/pallas_call | solution.py:142
  98.2 1.4 copy-done.3
  99.5 3.5 %collective-permute-done.24.refs_2_ = bf16[256,2048]{1,0:T(8,128)(2,1)S(1)} collective-permute-done((bf16[256,2048]{1,0:T(8,128)(2,1)S(1)}, bf16[256,2048]{1,0:T(8,128)(2,1)S(1)}, u32[]{:S(2)}, u32[]{:S(2)}) %collective-permute-start.24) | collective-permute-done | bytes 1048608 | tf_op jit(solution)/shard_map/ppermute | solution.py:38
  103.0 1.0 copy-done.8
  104.0 0.7 collective-permute-done.25.refs_3_
  104.7 1.1 collective-permute-start.28
  105.8 3.1 %collective-permute-start.26 = (f32[768,256]{1,0:T(8,128)}, f32[768,256]{1,0:T(8,128)}, u32[]{:S(2)}, u32[]{:S(2)}) collective-permute-start(f32[768,256]{1,0:T(8,128)} %get-tuple-element.58.small), channel_id=1, source_target_pairs={{0,4},{4,0},{8,12},{12,8},{16,20},{20,16},{24,28},{28,24},{32,36},... | collective-permute-start | bytes 2359304 | tf_op jit(solution)/shard_map/ppermute | solution.py:18
  109.3 1.9 %copy-done.1 = bf16[2048,768]{1,0:T(8,128)(2,1)S(1)} copy-done((bf16[2048,768]{1,0:T(8,128)(2,1)S(1)}, bf16[2048,768]{1,0:T(8,128)(2,1)}, u32[]{:S(2)}) %copy-start.1) | copy-done | bytes 3145752
  111.2 1.2 copy-done.6
  112.5 1.2 copy-done.9
  113.7 4.1 %multiply.3.early1 = f32[768,768]{1,0:T(8,128)S(1)} custom-call(bf16[2048,768]{1,0:T(8,128)(2,1)S(1)} %copy-done.1, bf16[256,2048]{1,0:T(8,128)(2,1)S(1)} %copy-done.6, bf16[256,2048]{1,0:T(8,128)(2,1)S(1)} %copy-done.9, bf16[256,2048]{1,0:T(8,128)(2,1)} %collective-permute-done.25.refs_3_), custom_call_target="tpu_custom_call" | custom-call | flops 2415919104 | tf_op jit(solution)/shard_map/multiply/pallas_call | solution.py:142
  117.8 2.5 %finish.1 = (bf16[2,256,512]{2,1,0:T(8,128)(2,1)S(1)}, f32[256,256]{1,0:T(8,128)}, f32[256,256]{1,0:T(8,128)S(1)}) custom-call(s32[1]{0:T(128)} %bitcast.3.core, f32[768,256]{1,0:T(8,128)} %get-tuple-element.58.small, f32[768,256]{1,0:T(8,128)} %collective-permute-done.26.other), custom_call_target="tpu_custom_call" | custom-call | flops 268435456 | tf_op jit(solution)/shard_map/finish/pallas_call | solution.py:275
  120.4 4.5 %pick.1 = bf16[2,16,64,512]{3,2,1,0:T(8,128)(2,1)} custom-call(s32[2,16]{1,0:T(2,128)S(1)} %fusion.5.places, bf16[2,256,512]{2,1,0:T(8,128)(2,1)S(1)} %get-tuple-element.61.mats, bf16[2048,768]{1,0:T(8,128)(2,1)S(1)} %copy-done.2, bf16[256,2048]{1,0:T(8,128)(2,1)S(1)} %collective-permute-done.27.piece0, ...), custom_call_target="tpu_custom_call" | custom-call | flops 1073741824 | tf_op jit(solution)/shard_map/pick/pallas_call | solution.py:199
  124.9 4.7 %all-to-all-start = ((bf16[8,4,64,512]{3,2,1,0:T(8,128)(2,1)}), bf16[8,4,64,512]{3,2,1,0:T(8,128)(2,1)S(1)}, u32[]{:S(2)}, u32[]{:S(2)}) async-start(bf16[8,4,64,512]{3,2,1,0:T(8,128)(2,1)} %bitcast.18), calls=%async_computation | async-start | bytes 4194304 | tf_op jit(solution)/shard_map/all_to_all | solution.py:457
  129.7 0.8 pad_maximum_fusion
  130.6 2.2 %collective-permute-done.17 = bf16[512,512]{1,0:T(8,128)(2,1)} collective-permute-done((bf16[512,512]{1,0:T(8,128)(2,1)}, bf16[512,512]{1,0:T(8,128)(2,1)}, u32[]{:S(2)}, u32[]{:S(2)}) %collective-permute-start.17) | collective-permute-done | bytes 524320 | tf_op jit(solution)/shard_map/ppermute | solution.py:18
  132.8 1.9 %slice_select_fusion = (bf16[512,256]{1,0:T(8,128)(2,1)}, bf16[1,512,256]{2,1,0:T(8,128)(2,1)}, bf16[1,512,256]{2,1,0:T(8,128)(2,1)}) fusion(bf16[512,512]{1,0:T(8,128)(2,1)} %collective-permute-done.17, pred[]{:T(512)S(6)} %eq.25, bf16[512,768]{1,0:T(8,128)(2,1)S(1)} %get-tuple-element.49.refs_0_), kind=kLoop, calls=%fused_computation.12 | loop fusion | flops 524288 | bytes 2097153 | tf_op jit(solution)/shard_map/jit(_where)/select_n | solution.py:380
  134.7 0.8 constant_dynamic-slice_fusion.1.band
  135.5 1.0 constant_dynamic-slice_fusion.piece
  136.5 1.0 update.1
  137.5 18.3 %all-to-all-done = bf16[8,4,64,512]{3,2,1,0:T(8,128)(2,1)S(1)} async-done(((bf16[8,4,64,512]{3,2,1,0:T(8,128)(2,1)}), bf16[8,4,64,512]{3,2,1,0:T(8,128)(2,1)S(1)}, u32[]{:S(2)}, u32[]{:S(2)}) %all-to-all-start) | async-done | bytes 2097184 | tf_op jit(solution)/shard_map/all_to_all | solution.py:457
  155.9 3.0 %settle.1 = f32[4,512,512]{2,1,0:T(8,128)} custom-call(bf16[2,4,4,64,512]{4,3,2,1,0:T(8,128)(2,1)S(1)} %bitcast.58), custom_call_target="tpu_custom_call" | custom-call | flops 1073741824 | tf_op jit(solution)/shard_map/settle/pallas_call | solution.py:324
  (71 shorter events, 3.0 us)
Async XLA Ops:
  0.6 10.9 %copy-start.12 = (bf16[2048,256]{1,0:T(8,128)(2,1)S(1)}, bf16[2048,256]{1,0:T(8,128)(2,1)}, u32[]{:S(2)}) copy-start(bf16[2048,256]{1,0:T(8,128)(2,1)} %param.9) | copy-start | bytes 3145732
  0.6 25.9 %collective-permute-start.8 = (bf16[2,1,2048,256]{3,2,1,0:T(8,128)(2,1)}, bf16[2,1,2048,256]{3,2,1,0:T(8,128)(2,1)}, u32[]{:S(2)}, u32[]{:S(2)}) collective-permute-start(bf16[2,1,2048,256]{3,2,1,0:T(8,128)(2,1)} %param.7), channel_id=1, source_target_pairs={{0,4},{4,0},{8,12},{12,8},{16,20},{20,16},{24,28},{28,24},{32,36},... | collective-permute-start | bytes 6291464 | tf_op jit(solution)/shard_map/ppermute | solution.py:18
  3.3 8.2 %copy-start.13 = (bf16[2048,256]{1,0:T(8,128)(2,1)S(1)}, bf16[2048,256]{1,0:T(8,128)(2,1)}, u32[]{:S(2)}) copy-start(bf16[2048,256]{1,0:T(8,128)(2,1)} %param.8) | copy-start | bytes 3145732
  3.3 2.8 %collective-permute-start = (bf16[512,64]{1,0:T(8,128)(2,1)S(1)}, bf16[512,64]{1,0:T(8,128)(2,1)S(1)}, u32[]{:S(2)}, u32[]{:S(2)}) collective-permute-start(bf16[512,64]{1,0:T(8,128)(2,1)S(1)} %select_bitcast_fusion.2), channel_id=1, source_target_pairs={{0,4},{4,0},{8,12},{12,8},{16,20},{20,16},{24,28},{28,24},{32,36},... | collective-permute-start | bytes 196616 | tf_op jit(solution)/shard_map/ppermute | solution.py:18
  6.3 13.8 %copy-start.14 = (s32[1,4,4]{2,1,0:T(4,128)S(1)}, s32[1,4,4]{2,1,0:T(4,128)}, u32[]{:S(2)}) copy-start(s32[1,4,4]{2,1,0:T(4,128)} %param.13) | copy-start | bytes 196
  6.3 13.9 %copy-start.15 = (s32[2,1]{0,1:T(1,128)S(1)}, s32[2,1]{0,1:T(1,128)}, u32[]{:S(2)}) copy-start(s32[2,1]{0,1:T(1,128)} %param.12) | copy-start | bytes 28
  6.3 6.3 %collective-permute-start.1 = (bf16[512,128]{1,0:T(8,128)(2,1)S(1)}, bf16[512,128]{1,0:T(8,128)(2,1)S(1)}, u32[]{:S(2)}, u32[]{:S(2)}) collective-permute-start(bf16[512,128]{1,0:T(8,128)(2,1)S(1)} %pad_maximum_fusion.1.refs_0_), channel_id=1, source_target_pairs={{0,8},{4,36},{8,16},{12,44},{16,24},{20,52},{24,0},{28,60},{32,40}... | collective-permute-start | bytes 393224 | tf_op jit(solution)/shard_map/ppermute | solution.py:38
  8.1 4.5 %collective-permute-start.2 = (bf16[512,128]{1,0:T(8,128)(2,1)S(1)}, bf16[512,128]{1,0:T(8,128)(2,1)S(1)}, u32[]{:S(2)}, u32[]{:S(2)}) collective-permute-start(bf16[512,128]{1,0:T(8,128)(2,1)S(1)} %pad_maximum_fusion.1.refs_0_), channel_id=1, source_target_pairs={{0,24},{4,100},{8,0},{12,108},{16,8},{20,116},{24,16},{28,124},{32... | collective-permute-start | bytes 393224 | tf_op jit(solution)/shard_map/ppermute | solution.py:38
  10.3 5.6 %collective-permute-start.3 = (bf16[512,128]{1,0:T(8,128)(2,1)S(1)}, bf16[512,128]{1,0:T(8,128)(2,1)S(1)}, u32[]{:S(2)}, u32[]{:S(2)}) collective-permute-start(bf16[512,128]{1,0:T(8,128)(2,1)S(1)} %pad_maximum_fusion.1.refs_0_), channel_id=1, source_target_pairs={{0,16},{4,68},{8,24},{12,76},{16,0},{20,84},{24,8},{28,92},{32,48}... | collective-permute-start | bytes 393224 | tf_op jit(solution)/shard_map/ppermute | solution.py:38
  15.9 13.0 %collective-permute-start.4 = (bf16[2048,128]{1,0:T(8,128)(2,1)S(1)}, bf16[2048,128]{1,0:T(8,128)(2,1)S(1)}, u32[]{:S(2)}, u32[]{:S(2)}) collective-permute-start(bf16[2048,128]{1,0:T(8,128)(2,1)S(1)} %join.3.refs_0_), channel_id=1, source_target_pairs={{0,32},{4,12},{8,40},{12,20},{16,48},{20,28},{24,56},{28,4},{32,64... | collective-permute-start | bytes 1572872 | tf_op jit(solution)/shard_map/ppermute | solution.py:38
  17.0 13.4 %collective-permute-start.5 = (bf16[2048,128]{1,0:T(8,128)(2,1)S(1)}, bf16[2048,128]{1,0:T(8,128)(2,1)}, u32[]{:S(2)}, u32[]{:S(2)}) collective-permute-start(bf16[2048,128]{1,0:T(8,128)(2,1)S(1)} %join.3.refs_0_), channel_id=1, source_target_pairs={{0,96},{4,28},{8,104},{12,4},{16,112},{20,12},{24,120},{28,20},{32... | collective-permute-start | bytes 1572872 | tf_op jit(solution)/shard_map/ppermute | solution.py:38
  18.7 13.5 %collective-permute-start.6 = (bf16[2048,128]{1,0:T(8,128)(2,1)S(1)}, bf16[2048,128]{1,0:T(8,128)(2,1)}, u32[]{:S(2)}, u32[]{:S(2)}) collective-permute-start(bf16[2048,128]{1,0:T(8,128)(2,1)S(1)} %join.3.refs_0_), channel_id=1, source_target_pairs={{0,64},{4,20},{8,72},{12,28},{16,80},{20,4},{24,88},{28,12},{32,96... | collective-permute-start | bytes 1572872 | tf_op jit(solution)/shard_map/ppermute | solution.py:38
  20.3 4.3 %collective-permute-start.7 = (f32[1,18]{1,0:T(1,128)S(1)}, f32[1,18]{1,0:T(1,128)S(1)}, u32[]{:S(2)}, u32[]{:S(2)}) collective-permute-start(f32[1,18]{1,0:T(1,128)S(1)} %add_convert_fusion), channel_id=1, source_target_pairs={{0,4},{4,0},{8,12},{12,8},{16,20},{20,16},{24,28},{28,24},{32,36},... | collective-permute-start | bytes 224 | tf_op jit(solution)/shard_map/ppermute | solution.py:18
  29.0 0.8 copy-start.10
  32.2 1.0 copy-start.11
  37.2 4.5 %collective-permute-start.9 = (bf16[128,512]{1,0:T(8,128)(2,1)S(1)}, bf16[128,512]{1,0:T(8,128)(2,1)S(1)}, u32[]{:S(2)}, u32[]{:S(2)}) collective-permute-start(bf16[128,512]{1,0:T(8,128)(2,1)S(1)} %get-tuple-element.42), channel_id=1, source_target_pairs={{0,1},{1,2},{2,3},{3,0},{4,7},{5,4},{6,5},{7,6},{8,9},{9,10},{10,1... | collective-permute-start | bytes 393224 | tf_op jit(solution)/shard_map/ppermute | solution.py:27
  39.7 7.6 %collective-permute-start.10 = (bf16[128,512]{1,0:T(8,128)(2,1)S(1)}, bf16[128,512]{1,0:T(8,128)(2,1)S(1)}, u32[]{:S(2)}, u32[]{:S(2)}) collective-permute-start(bf16[128,512]{1,0:T(8,128)(2,1)S(1)} %get-tuple-element.43), channel_id=1, source_target_pairs={{0,3},{1,0},{2,1},{3,2},{4,5},{5,6},{6,7},{7,4},{8,11},{9,8},{10,9... | collective-permute-start | bytes 393224 | tf_op jit(solution)/shard_map/ppermute | solution.py:27
  39.7 7.6 %collective-permute-start.11 = (bf16[128,512]{1,0:T(8,128)(2,1)S(1)}, bf16[128,512]{1,0:T(8,128)(2,1)S(1)}, u32[]{:S(2)}, u32[]{:S(2)}) collective-permute-start(bf16[128,512]{1,0:T(8,128)(2,1)S(1)} %get-tuple-element.46), channel_id=1, source_target_pairs={{0,2},{1,3},{2,0},{3,1},{4,6},{5,7},{6,4},{7,5},{8,10},{9,11},{10,... | collective-permute-start | bytes 393224 | tf_op jit(solution)/shard_map/ppermute | solution.py:27
  47.5 6.5 %collective-permute-start.12 = (bf16[64,2048]{1,0:T(8,128)(2,1)S(1)}, bf16[64,2048]{1,0:T(8,128)(2,1)S(1)}, u32[]{:S(2)}, u32[]{:S(2)}) collective-permute-start(bf16[64,2048]{1,0:T(8,128)(2,1)S(1)} %get-tuple-element.74.refs_0_), channel_id=1, source_target_pairs={{0,8},{4,36},{8,16},{12,44},{16,24},{20,52},{24,0},{28,60},{32,40}... | collective-permute-start | bytes 786440 | tf_op jit(solution)/shard_map/ppermute | solution.py:38
  47.8 6.4 %collective-permute-start.13 = (bf16[64,2048]{1,0:T(8,128)(2,1)S(1)}, bf16[64,2048]{1,0:T(8,128)(2,1)S(1)}, u32[]{:S(2)}, u32[]{:S(2)}) collective-permute-start(bf16[64,2048]{1,0:T(8,128)(2,1)S(1)} %get-tuple-element.74.refs_0_), channel_id=1, source_target_pairs={{0,24},{4,100},{8,0},{12,108},{16,8},{20,116},{24,16},{28,124},{32... | collective-permute-start | bytes 786440 | tf_op jit(solution)/shard_map/ppermute | solution.py:38
  50.2 22.2 %collective-permute-start.21 = (bf16[512,768]{1,0:T(8,128)(2,1)S(1)}, bf16[512,768]{1,0:T(8,128)(2,1)S(1)}, u32[]{:S(2)}, u32[]{:S(2)}) collective-permute-start(bf16[512,768]{1,0:T(8,128)(2,1)S(1)} %get-tuple-element.49.refs_0_), channel_id=1, source_target_pairs={{0,1},{1,2},{2,3},{3,0},{4,7},{5,4},{6,5},{7,6},{8,9},{9,10},{10,1... | collective-permute-start | bytes 2359304 | tf_op jit(solution)/shard_map/ppermute | solution.py:27
  51.6 21.8 %collective-permute-start.22 = (bf16[512,768]{1,0:T(8,128)(2,1)S(1)}, bf16[512,768]{1,0:T(8,128)(2,1)S(1)}, u32[]{:S(2)}, u32[]{:S(2)}) collective-permute-start(bf16[512,768]{1,0:T(8,128)(2,1)S(1)} %get-tuple-element.49.refs_0_), channel_id=1, source_target_pairs={{0,3},{1,0},{2,1},{3,2},{4,5},{5,6},{6,7},{7,4},{8,11},{9,8},{10,9... | collective-permute-start | bytes 2359304 | tf_op jit(solution)/shard_map/ppermute | solution.py:27
  51.7 32.3 %collective-permute-start.23 = (bf16[512,768]{1,0:T(8,128)(2,1)S(1)}, bf16[512,768]{1,0:T(8,128)(2,1)S(1)}, u32[]{:S(2)}, u32[]{:S(2)}) collective-permute-start(bf16[512,768]{1,0:T(8,128)(2,1)S(1)} %get-tuple-element.49.refs_0_), channel_id=1, source_target_pairs={{0,2},{1,3},{2,0},{3,1},{4,6},{5,7},{6,4},{7,5},{8,10},{9,11},{10,... | collective-permute-start | bytes 2359304 | tf_op jit(solution)/shard_map/ppermute | solution.py:27
  54.0 6.8 %collective-permute-start.14 = (bf16[64,2048]{1,0:T(8,128)(2,1)S(1)}, bf16[64,2048]{1,0:T(8,128)(2,1)S(1)}, u32[]{:S(2)}, u32[]{:S(2)}) collective-permute-start(bf16[64,2048]{1,0:T(8,128)(2,1)S(1)} %get-tuple-element.74.refs_0_), channel_id=1, source_target_pairs={{0,16},{4,68},{8,24},{12,76},{16,0},{20,84},{24,8},{28,92},{32,48}... | collective-permute-start | bytes 786440 | tf_op jit(solution)/shard_map/ppermute | solution.py:38
  54.2 9.6 %collective-permute-start.18 = (bf16[64,2048]{1,0:T(8,128)(2,1)S(1)}, bf16[64,2048]{1,0:T(8,128)(2,1)S(1)}, u32[]{:S(2)}, u32[]{:S(2)}) collective-permute-start(bf16[64,2048]{1,0:T(8,128)(2,1)S(1)} %get-tuple-element.73.refs_0_), channel_id=1, source_target_pairs={{0,8},{4,36},{8,16},{12,44},{16,24},{20,52},{24,0},{28,60},{32,40}... | collective-permute-start | bytes 786440 | tf_op jit(solution)/shard_map/ppermute | solution.py:38
  60.8 5.5 %collective-permute-start.19 = (bf16[64,2048]{1,0:T(8,128)(2,1)S(1)}, bf16[64,2048]{1,0:T(8,128)(2,1)S(1)}, u32[]{:S(2)}, u32[]{:S(2)}) collective-permute-start(bf16[64,2048]{1,0:T(8,128)(2,1)S(1)} %get-tuple-element.73.refs_0_), channel_id=1, source_target_pairs={{0,24},{4,100},{8,0},{12,108},{16,8},{20,116},{24,16},{28,124},{32... | collective-permute-start | bytes 786440 | tf_op jit(solution)/shard_map/ppermute | solution.py:38
  63.8 6.7 %collective-permute-start.20 = (bf16[64,2048]{1,0:T(8,128)(2,1)S(1)}, bf16[64,2048]{1,0:T(8,128)(2,1)S(1)}, u32[]{:S(2)}, u32[]{:S(2)}) collective-permute-start(bf16[64,2048]{1,0:T(8,128)(2,1)S(1)} %get-tuple-element.73.refs_0_), channel_id=1, source_target_pairs={{0,16},{4,68},{8,24},{12,76},{16,0},{20,84},{24,8},{28,92},{32,48}... | collective-permute-start | bytes 786440 | tf_op jit(solution)/shard_map/ppermute | solution.py:38
  66.3 26.3 %collective-permute-start.15 = (bf16[256,2048]{1,0:T(8,128)(2,1)S(1)}, bf16[256,2048]{1,0:T(8,128)(2,1)}, u32[]{:S(2)}, u32[]{:S(2)}) collective-permute-start(bf16[256,2048]{1,0:T(8,128)(2,1)S(1)} %join.4.refs_1_), channel_id=1, source_target_pairs={{0,32},{4,12},{8,40},{12,20},{16,48},{20,28},{24,56},{28,4},{32,64... | collective-permute-start | bytes 3145736 | tf_op jit(solution)/shard_map/ppermute | solution.py:38
  70.5 22.1 %collective-permute-start.16 = (bf16[256,2048]{1,0:T(8,128)(2,1)S(1)}, bf16[256,2048]{1,0:T(8,128)(2,1)S(1)}, u32[]{:S(2)}, u32[]{:S(2)}) collective-permute-start(bf16[256,2048]{1,0:T(8,128)(2,1)S(1)} %join.4.refs_1_), channel_id=1, source_target_pairs={{0,96},{4,28},{8,104},{12,4},{16,112},{20,12},{24,120},{28,20},{32... | collective-permute-start | bytes 3145736 | tf_op jit(solution)/shard_map/ppermute | solution.py:38
  72.4 25.7 %copy-start.5 = (bf16[256,2048]{1,0:T(8,128)(2,1)}, bf16[256,2048]{1,0:T(8,128)(2,1)S(1)}, u32[]{:S(2)}) copy-start(bf16[256,2048]{1,0:T(8,128)(2,1)S(1)} %join.5.refs_1_) | copy-start | bytes 3145732
  83.9 19.1 %collective-permute-start.24 = (bf16[256,2048]{1,0:T(8,128)(2,1)S(1)}, bf16[256,2048]{1,0:T(8,128)(2,1)S(1)}, u32[]{:S(2)}, u32[]{:S(2)}) collective-permute-start(bf16[256,2048]{1,0:T(8,128)(2,1)S(1)} %join.5.refs_1_), channel_id=1, source_target_pairs={{0,32},{4,12},{8,40},{12,20},{16,48},{20,28},{24,56},{28,4},{32,64... | collective-permute-start | bytes 3145736 | tf_op jit(solution)/shard_map/ppermute | solution.py:38
  90.6 14.0 %collective-permute-start.25 = (bf16[256,2048]{1,0:T(8,128)(2,1)S(1)}, bf16[256,2048]{1,0:T(8,128)(2,1)}, u32[]{:S(2)}, u32[]{:S(2)}) collective-permute-start(bf16[256,2048]{1,0:T(8,128)(2,1)S(1)} %join.5.refs_1_), channel_id=1, source_target_pairs={{0,96},{4,28},{8,104},{12,4},{16,112},{20,12},{24,120},{28,20},{32... | collective-permute-start | bytes 3145736 | tf_op jit(solution)/shard_map/ppermute | solution.py:38
  92.7 5.5 %copy-start = (bf16[2048,768]{1,0:T(8,128)(2,1)}, bf16[2048,768]{1,0:T(8,128)(2,1)S(1)}, u32[]{:S(2)}) copy-start(bf16[2048,768]{1,0:T(8,128)(2,1)S(1)} %get-tuple-element.56.refs_0_.whole) | copy-start | bytes 9437188
  92.7 27.7 %collective-permute-start.27 = (bf16[256,2048]{1,0:T(8,128)(2,1)}, bf16[256,2048]{1,0:T(8,128)(2,1)S(1)}, u32[]{:S(2)}, u32[]{:S(2)}) collective-permute-start(bf16[256,2048]{1,0:T(8,128)(2,1)} %collective-permute-done.15.refs_2_), channel_id=1, source_target_pairs={{0,32},{4,12},{8,40},{12,20},{16,48},{20,28},{24,56},{28,4},{32,64... | collective-permute-start | bytes 3145736 | tf_op jit(solution)/shard_map/ppermute | solution.py:38
  98.1 1.4 copy-start.3
  103.0 1.0 copy-start.8
  104.7 15.7 %collective-permute-start.28 = (bf16[256,2048]{1,0:T(8,128)(2,1)}, bf16[256,2048]{1,0:T(8,128)(2,1)S(1)}, u32[]{:S(2)}, u32[]{:S(2)}) collective-permute-start(bf16[256,2048]{1,0:T(8,128)(2,1)} %collective-permute-done.25.refs_3_), channel_id=1, source_target_pairs={{0,96},{4,28},{8,104},{12,4},{16,112},{20,12},{24,120},{28,20},{32... | collective-permute-start | bytes 3145736 | tf_op jit(solution)/shard_map/ppermute | solution.py:38
  105.8 12.0 %collective-permute-start.26 = (f32[768,256]{1,0:T(8,128)}, f32[768,256]{1,0:T(8,128)}, u32[]{:S(2)}, u32[]{:S(2)}) collective-permute-start(f32[768,256]{1,0:T(8,128)} %get-tuple-element.58.small), channel_id=1, source_target_pairs={{0,4},{4,0},{8,12},{12,8},{16,20},{20,16},{24,28},{28,24},{32,36},... | collective-permute-start | bytes 2359304 | tf_op jit(solution)/shard_map/ppermute | solution.py:18
  109.3 1.9 %copy-start.1 = (bf16[2048,768]{1,0:T(8,128)(2,1)S(1)}, bf16[2048,768]{1,0:T(8,128)(2,1)}, u32[]{:S(2)}) copy-start(bf16[2048,768]{1,0:T(8,128)(2,1)} %copy-done) | copy-start | bytes 9437188
  111.2 1.2 copy-start.6
  112.5 1.2 copy-start.9
  113.7 6.7 %copy-start.2 = (bf16[2048,768]{1,0:T(8,128)(2,1)S(1)}, bf16[2048,768]{1,0:T(8,128)(2,1)}, u32[]{:S(2)}) copy-start(bf16[2048,768]{1,0:T(8,128)(2,1)} %copy-done) | copy-start | bytes 9437188
  113.7 6.7 %copy-start.4 = (f32[768,768]{1,0:T(8,128)S(1)}, f32[768,768]{1,0:T(8,128)}, u32[]{:S(2)}) copy-start(f32[768,768]{1,0:T(8,128)} %copy-done.3) | copy-start | bytes 7077892
  124.9 31.0 %all-to-all-start = ((bf16[8,4,64,512]{3,2,1,0:T(8,128)(2,1)}), bf16[8,4,64,512]{3,2,1,0:T(8,128)(2,1)S(1)}, u32[]{:S(2)}, u32[]{:S(2)}) async-start(bf16[8,4,64,512]{3,2,1,0:T(8,128)(2,1)} %bitcast.18), calls=%async_computation | async-start | bytes 4194304 | tf_op jit(solution)/shard_map/all_to_all | solution.py:457
  129.7 6.8 %copy-start.7 = (f32[64,512]{1,0:T(8,128)S(1)}, f32[64,512]{1,0:T(8,128)}, u32[]{:S(2)}) copy-start(f32[64,512]{1,0:T(8,128)} %before.1) | copy-start | bytes 393220
  130.5 2.3 %collective-permute-start.17 = (bf16[512,512]{1,0:T(8,128)(2,1)}, bf16[512,512]{1,0:T(8,128)(2,1)}, u32[]{:S(2)}, u32[]{:S(2)}) collective-permute-start(bf16[512,512]{1,0:T(8,128)(2,1)} %pad_maximum_fusion), channel_id=1, source_target_pairs={{0,4},{4,0},{8,12},{12,8},{16,20},{20,16},{24,28},{28,24},{32,36},... | collective-permute-start | bytes 1572872 | tf_op jit(solution)/shard_map/ppermute | solution.py:18

commit v2 on v1

--- a/solution.py
+++ b/solution.py
@@ -410,8 +410,7 @@
     thin_opposite = along_x(thin_parts[2], 2)
     thin_before, thin_after, sent = lax.optimization_barrier((thin_before, thin_after, solved))
     thin = jnp.concatenate([thin_parts[0], thin_before, thin_after, thin_opposite], axis=1)
-    quarters = thin.reshape(2, quarter, tile_size)
-    line0, line1 = (join(direct(quarters[h], 0), 1)[0] for h in range(2))
+    line0, line1 = join(direct(thin, 0), 2)
     x_before, x_after, x_opposite = along_x(sent, 1), along_x(sent, -1), along_x(sent, 2)
     line1, x_before, x_after, x_opposite = lax.optimization_barrier(
         (line1, x_before, x_after, x_opposite)

time: 159 us -> 157 us (0.987)
  starting transfers between devices: 46.5 us -> 43.4 us
    ppermute x18 -> x15, starting transfers between devices: 27.6 us -> 22.1 us  [hop(): return lax.ppermute(x, 'row', pairs)]
    ppermute x5, starting transfers between devices: 7.37 us -> 9.87 us  [other_core(): return lax.ppermute(x, 'row', pairs)]
    ppermute x18 -> x15, waiting for transfers between devices: 24.1 us -> 24.4 us  [hop(): return lax.ppermute(x, 'row', pairs)]
  transfers between devices with their start and end apart: 30 -> 27, of which waited for: 18 -> 16; matrix products, arithmetic and copies ran while one was open for 8% -> 8% of each run, Pallas kernels for 9% -> 9%
where the time goes in v2:
time: 157 us; the launch traced here: 156 us
  waiting for transfers between devices  65.2 us (42%)
  starting transfers between devices  43.4 us (28%)
  Pallas kernels  25.2 us (16%)
  local copies, waits for them, and re-layouts  13.1 us (8%)
  other arithmetic  8.38 us (5%)
    ppermute x15, waiting for transfers between devices, hop(): return lax.ppermute(x, 'row', pairs)  24.4 us
    ppermute x15, starting transfers between devices, hop(): return lax.ppermute(x, 'row', pairs)  22.1 us
    all_to_all x1, waiting for transfers between devices, body(): lax.all_to_all(picked.reshape(8, slots, quarter, 2 * rank), ('row', 'col'...  18.3 us
    ppermute x6, waiting for transfers between devices, along_x(): return lax.ppermute(x, ('row', 'col'), pairs)  17.6 us
    ppermute x5, starting transfers between devices, other_core(): return lax.ppermute(x, 'row', pairs)  9.87 us
    unnamed x37, local copies, waits for them, and re-layouts  8.88 us
    pallas_call x2, Pallas kernels, multiply(): pl.pallas_call(multiply_kernel, out_shape=jax.ShapeDtypeStruct((count * r...  8.05 us
    ppermute x6, starting transfers between devices, along_x(): return lax.ppermute(x, ('row', 'col'), pairs)  6.68 us
  transfers between devices with their start and end apart: 27, of which 16 were waited for; matrix products, arithmetic and copies ran while one was open for 8% of the time, Pallas kernels for 9%

profile of v2, /device:TPU:1, one launch (start us, length us, event | category | flops | bytes accessed | tf_op | source)
XLA Modules:
  0.0 156.2 jit_solution(2444402641872733017)
XLA Ops:
  0.6 1.5 collective-permute-start.8
  2.1 0.9 fusion.9
  3.5 2.6 %collective-permute-done = bf16[512,64]{1,0:T(8,128)(2,1)S(1)} collective-permute-done((bf16[512,64]{1,0:T(8,128)(2,1)S(1)}, bf16[512,64]{1,0:T(8,128)(2,1)S(1)}, u32[]{:S(2)}, u32[]{:S(2)}) %collective-permute-start) | collective-permute-done | bytes 65568 | tf_op jit(solution)/shard_map/ppermute | solution.py:18
  6.3 1.8 %collective-permute-start.1 = (bf16[512,128]{1,0:T(8,128)(2,1)S(1)}, bf16[512,128]{1,0:T(8,128)(2,1)S(1)}, u32[]{:S(2)}, u32[]{:S(2)}) collective-permute-start(bf16[512,128]{1,0:T(8,128)(2,1)S(1)} %pad_maximum_fusion.1.refs_0_), channel_id=1, source_target_pairs={{0,8},{4,36},{8,16},{12,44},{16,24},{20,52},{24,0},{28,60},{32,40}... | collective-permute-start | bytes 393224 | tf_op jit(solution)/shard_map/ppermute | solution.py:38
  8.1 2.2 %collective-permute-start.2 = (bf16[512,128]{1,0:T(8,128)(2,1)S(1)}, bf16[512,128]{1,0:T(8,128)(2,1)S(1)}, u32[]{:S(2)}, u32[]{:S(2)}) collective-permute-start(bf16[512,128]{1,0:T(8,128)(2,1)S(1)} %pad_maximum_fusion.1.refs_0_), channel_id=1, source_target_pairs={{0,24},{4,100},{8,0},{12,108},{16,8},{20,116},{24,16},{28,124},{32... | collective-permute-start | bytes 393224 | tf_op jit(solution)/shard_map/ppermute | solution.py:38
  10.3 1.2 collective-permute-start.3
  11.8 0.8 collective-permute-done.1.refs_1_
  12.6 3.3 %collective-permute-done.3.refs_3_ = bf16[512,128]{1,0:T(8,128)(2,1)S(1)} collective-permute-done((bf16[512,128]{1,0:T(8,128)(2,1)S(1)}, bf16[512,128]{1,0:T(8,128)(2,1)S(1)}, u32[]{:S(2)}, u32[]{:S(2)}) %collective-permute-start.3) | collective-permute-done | bytes 131104 | tf_op jit(solution)/shard_map/ppermute | solution.py:38
  15.9 1.1 collective-permute-start.4
  17.0 1.7 %collective-permute-start.5 = (bf16[2048,128]{1,0:T(8,128)(2,1)S(1)}, bf16[2048,128]{1,0:T(8,128)(2,1)}, u32[]{:S(2)}, u32[]{:S(2)}) collective-permute-start(bf16[2048,128]{1,0:T(8,128)(2,1)S(1)} %join.2.refs_0_), channel_id=1, source_target_pairs={{0,96},{4,28},{8,104},{12,4},{16,112},{20,12},{24,120},{28,20},{32... | collective-permute-start | bytes 1572872 | tf_op jit(solution)/shard_map/ppermute | solution.py:38
  18.7 1.4 collective-permute-start.6
  20.3 2.5 %collective-permute-start.7 = (f32[1,18]{1,0:T(1,128)S(1)}, f32[1,18]{1,0:T(1,128)S(1)}, u32[]{:S(2)}, u32[]{:S(2)}) collective-permute-start(f32[1,18]{1,0:T(1,128)S(1)} %add_convert_fusion), channel_id=1, source_target_pairs={{0,4},{4,0},{8,12},{12,8},{16,20},{20,16},{24,28},{28,24},{32,36},... | collective-permute-start | bytes 224 | tf_op jit(solution)/shard_map/ppermute | solution.py:18
  22.7 0.6 fusion.11
  23.3 1.3 iota_compare_fusion.2
  24.6 0.6 fusion.10
  25.2 1.3 iota_compare_fusion
  26.5 2.5 %broadcast_select_fusion.1 = (bf16[2048,256]{1,0:T(8,128)(2,1)S(1)}, bf16[2048,256]{1,0:T(8,128)(2,1)S(1)}) fusion(pred[]{:T(512)S(6)} %eq.25, bf16[2,1,2048,256]{3,2,1,0:T(8,128)(2,1)} %param.7, pred[256]{0:T(512)(128)(4,1)S(1)} %get-tuple-element.89, pred[256]{0:T(512)(128)(4,1)S(1)} %get-tuple-element.90, ...), kind=kLoop, calls=%fused_computation.9 | loop fusion | flops 4194304 | bytes 6292481 | tf_op jit(solution)/shard_map/jit(_where)/select_n | solution.py:380
  29.0 0.8 copy-done.10
  29.8 0.6 collective-permute-done.5.refs_2_
  30.4 1.8 %collective-permute-done.6.refs_3_ = bf16[2048,128]{1,0:T(8,128)(2,1)} collective-permute-done((bf16[2048,128]{1,0:T(8,128)(2,1)S(1)}, bf16[2048,128]{1,0:T(8,128)(2,1)}, u32[]{:S(2)}, u32[]{:S(2)}) %collective-permute-start.6) | collective-permute-done | bytes 524320 | tf_op jit(solution)/shard_map/ppermute | solution.py:38
  32.2 1.0 copy-done.11
  33.3 3.9 %solve.1 = (bf16[512,768]{1,0:T(8,128)(2,1)S(1)}, bf16[128,512]{1,0:T(8,128)(2,1)S(1)}, bf16[128,512]{1,0:T(8,128)(2,1)S(1)}, bf16[128,512]{1,0:T(8,128)(2,1)S(1)}, bf16[128,512]{1,0:T(8,128)(2,1)S(1)}) custom-call(s32[4]{0:T(128)S(1)} %pad_add_fusion.1.where, bf16[2048,128]{1,0:T(8,128)(2,1)S(1)} %join.2.refs_0_, bf16[2048,128]{1,0:T(8,128)(2,1)S(1)} %copy-done.11, ...), custom_call_target="tpu_custom_call" | custom-call | flops 1610612736 | tf_op jit(solution)/shard_map/solve/pallas_call | solution.py:108
  37.2 2.5 %collective-permute-start.9 = (bf16[128,512]{1,0:T(8,128)(2,1)S(1)}, bf16[128,512]{1,0:T(8,128)(2,1)S(1)}, u32[]{:S(2)}, u32[]{:S(2)}) collective-permute-start(bf16[128,512]{1,0:T(8,128)(2,1)S(1)} %get-tuple-element.44), channel_id=1, source_target_pairs={{0,1},{1,2},{2,3},{3,0},{4,7},{5,4},{6,5},{7,6},{8,9},{9,10},{10,1... | collective-permute-start | bytes 393224 | tf_op jit(solution)/shard_map/ppermute | solution.py:27
  39.7 1.7 %collective-permute-start.11 = (bf16[128,512]{1,0:T(8,128)(2,1)S(1)}, bf16[128,512]{1,0:T(8,128)(2,1)S(1)}, u32[]{:S(2)}, u32[]{:S(2)}) collective-permute-start(bf16[128,512]{1,0:T(8,128)(2,1)S(1)} %get-tuple-element.48), channel_id=1, source_target_pairs={{0,2},{1,3},{2,0},{3,1},{4,6},{5,7},{6,4},{7,5},{8,10},{9,11},{10,... | collective-permute-start | bytes 393224 | tf_op jit(solution)/shard_map/ppermute | solution.py:27
  41.5 0.2 collective-permute-done.9
  41.7 5.7 %collective-permute-done.10 = bf16[128,512]{1,0:T(8,128)(2,1)S(1)} collective-permute-done((bf16[128,512]{1,0:T(8,128)(2,1)S(1)}, bf16[128,512]{1,0:T(8,128)(2,1)S(1)}, u32[]{:S(2)}, u32[]{:S(2)}) %collective-permute-start.10) | collective-permute-done | bytes 131104 | tf_op jit(solution)/shard_map/ppermute | solution.py:27
  47.4 0.4 collective-permute-start.12
  47.8 1.1 collective-permute-start.18
  48.9 0.3 collective-permute-start.19
  49.2 0.9 collective-permute-start.20
  50.2 2.5 %collective-permute-start.13 = (bf16[128,2048]{1,0:T(8,128)(2,1)S(1)}, bf16[128,2048]{1,0:T(8,128)(2,1)S(1)}, u32[]{:S(2)}, u32[]{:S(2)}) collective-permute-start(bf16[128,2048]{1,0:T(8,128)(2,1)S(1)} %constant_dynamic-update-slice_fusion.refs_0_), channel_id=1, source_target_pairs={{0,24},{4,100},{8,0},{12,108},{16,8},{20,116},{24,16},{28,124},{32... | collective-permute-start | bytes 1572872 | tf_op jit(solution)/shard_map/ppermute | solution.py:38
  52.7 4.3 %collective-permute-done.12.refs_1_ = bf16[128,2048]{1,0:T(8,128)(2,1)S(1)} collective-permute-done((bf16[128,2048]{1,0:T(8,128)(2,1)S(1)}, bf16[128,2048]{1,0:T(8,128)(2,1)S(1)}, u32[]{:S(2)}, u32[]{:S(2)}) %collective-permute-start.12) | collective-permute-done | bytes 524320 | tf_op jit(solution)/shard_map/ppermute | solution.py:38
  57.0 0.3 collective-permute-start.14
  57.3 7.2 %collective-permute-done.13.refs_2_ = bf16[128,2048]{1,0:T(8,128)(2,1)S(1)} collective-permute-done((bf16[128,2048]{1,0:T(8,128)(2,1)S(1)}, bf16[128,2048]{1,0:T(8,128)(2,1)S(1)}, u32[]{:S(2)}, u32[]{:S(2)}) %collective-permute-start.13) | collective-permute-done | bytes 524320 | tf_op jit(solution)/shard_map/ppermute | solution.py:38
  64.4 2.4 %collective-permute-done.14.refs_3_ = bf16[128,2048]{1,0:T(8,128)(2,1)S(1)} collective-permute-done((bf16[128,2048]{1,0:T(8,128)(2,1)S(1)}, bf16[128,2048]{1,0:T(8,128)(2,1)S(1)}, u32[]{:S(2)}, u32[]{:S(2)}) %collective-permute-start.14) | collective-permute-done | bytes 524320 | tf_op jit(solution)/shard_map/ppermute | solution.py:38
  67.0 2.4 %collective-permute-start.15 = (bf16[256,2048]{1,0:T(8,128)(2,1)S(1)}, bf16[256,2048]{1,0:T(8,128)(2,1)}, u32[]{:S(2)}, u32[]{:S(2)}) collective-permute-start(bf16[256,2048]{1,0:T(8,128)(2,1)S(1)} %get-tuple-element.49.refs_1_), channel_id=1, source_target_pairs={{0,32},{4,12},{8,40},{12,20},{16,48},{20,28},{24,56},{28,4},{32,64... | collective-permute-start | bytes 3145736 | tf_op jit(solution)/shard_map/ppermute | solution.py:38
  69.4 0.4 collective-permute-start.16
  69.8 0.3 collective-permute-done.19.refs_2_
  70.1 11.4 %collective-permute-done.20.refs_3_ = bf16[512,768]{1,0:T(8,128)(2,1)S(1)} collective-permute-done((bf16[512,768]{1,0:T(8,128)(2,1)S(1)}, bf16[512,768]{1,0:T(8,128)(2,1)S(1)}, u32[]{:S(2)}, u32[]{:S(2)}) %collective-permute-start.20) | collective-permute-done | bytes 786464 | tf_op jit(solution)/shard_map/ppermute | solution.py:27
  81.5 4.0 %collective-permute-start.21 = (bf16[256,2048]{1,0:T(8,128)(2,1)S(1)}, bf16[256,2048]{1,0:T(8,128)(2,1)S(1)}, u32[]{:S(2)}, u32[]{:S(2)}) collective-permute-start(bf16[256,2048]{1,0:T(8,128)(2,1)S(1)} %get-tuple-element.54.refs_1_), channel_id=1, source_target_pairs={{0,32},{4,12},{8,40},{12,20},{16,48},{20,28},{24,56},{28,4},{32,64... | collective-permute-start | bytes 3145736 | tf_op jit(solution)/shard_map/ppermute | solution.py:38
  85.5 2.0 %couple.1 = (bf16[2048,768]{1,0:T(8,128)(2,1)S(1)}, f32[768,256]{1,0:T(8,128)}) custom-call(bf16[512,768]{1,0:T(8,128)(2,1)S(1)} %get-tuple-element.53.refs_0_, bf16[512,768]{1,0:T(8,128)(2,1)S(1)} %collective-permute-done.18.refs_1_, bf16[512,768]{1,0:T(8,128)(2,1)S(1)} %collective-permute-done.19.refs_2_, bf16[512,768]{1,0:T(8,128)(2,1)S(1)} %collective-permute-done.20.refs_3_), custom_call_target="tpu_custom_call" | custom-call | flops 805306368 | tf_op jit(solution)/shard_map/couple/pallas_call | solution.py:233
  87.5 1.7 %collective-permute-start.24 = (bf16[256,2048]{1,0:T(8,128)(2,1)}, bf16[256,2048]{1,0:T(8,128)(2,1)S(1)}, u32[]{:S(2)}, u32[]{:S(2)}) collective-permute-start(bf16[256,2048]{1,0:T(8,128)(2,1)} %collective-permute-done.15.refs_2_), channel_id=1, source_target_pairs={{0,32},{4,12},{8,40},{12,20},{16,48},{20,28},{24,56},{28,4},{32,64... | collective-permute-start | bytes 3145736 | tf_op jit(solution)/shard_map/ppermute | solution.py:38
  89.2 3.9 %multiply.2.early0 = f32[768,768]{1,0:T(8,128)S(1)} custom-call(bf16[2048,768]{1,0:T(8,128)(2,1)S(1)} %get-tuple-element.60.refs_0_.whole, bf16[256,2048]{1,0:T(8,128)(2,1)S(1)} %get-tuple-element.49.refs_1_, bf16[256,2048]{1,0:T(8,128)(2,1)} %collective-permute-done.15.refs_2_, bf16[256,2048]{1,0:T(8,128)(2,1)S(1)} %collective-permute-done.16.refs_3_), custom_call_target="tpu_custom_call" | custom-call | flops 2415919104 | tf_op jit(solution)/shard_map/multiply/pallas_call | solution.py:142
  93.2 1.4 copy-done.3
  94.6 2.7 %collective-permute-done.21.refs_2_ = bf16[256,2048]{1,0:T(8,128)(2,1)S(1)} collective-permute-done((bf16[256,2048]{1,0:T(8,128)(2,1)S(1)}, bf16[256,2048]{1,0:T(8,128)(2,1)S(1)}, u32[]{:S(2)}, u32[]{:S(2)}) %collective-permute-start.21) | collective-permute-done | bytes 1048608 | tf_op jit(solution)/shard_map/ppermute | solution.py:38
  97.2 1.0 copy-done.8
  98.2 1.3 collective-permute-done.22.refs_3_
  99.5 1.1 collective-permute-start.25
  100.7 5.6 %collective-permute-start.23 = (f32[768,256]{1,0:T(8,128)}, f32[768,256]{1,0:T(8,128)}, u32[]{:S(2)}, u32[]{:S(2)}) collective-permute-start(f32[768,256]{1,0:T(8,128)} %get-tuple-element.62.small), channel_id=1, source_target_pairs={{0,4},{4,0},{8,12},{12,8},{16,20},{20,16},{24,28},{28,24},{32,36},... | collective-permute-start | bytes 2359304 | tf_op jit(solution)/shard_map/ppermute | solution.py:18
  106.7 1.9 %copy-done.1 = bf16[2048,768]{1,0:T(8,128)(2,1)S(1)} copy-done((bf16[2048,768]{1,0:T(8,128)(2,1)S(1)}, bf16[2048,768]{1,0:T(8,128)(2,1)}, u32[]{:S(2)}) %copy-start.1) | copy-done | bytes 3145752
  108.6 1.2 copy-done.7
  109.8 1.2 copy-done.9
  111.0 4.1 %multiply.3.early1 = f32[768,768]{1,0:T(8,128)S(1)} custom-call(bf16[2048,768]{1,0:T(8,128)(2,1)S(1)} %copy-done.1, bf16[256,2048]{1,0:T(8,128)(2,1)S(1)} %copy-done.7, bf16[256,2048]{1,0:T(8,128)(2,1)S(1)} %copy-done.9, bf16[256,2048]{1,0:T(8,128)(2,1)} %collective-permute-done.22.refs_3_), custom_call_target="tpu_custom_call" | custom-call | flops 2415919104 | tf_op jit(solution)/shard_map/multiply/pallas_call | solution.py:142
  115.2 2.5 %finish.1 = (bf16[2,256,512]{2,1,0:T(8,128)(2,1)S(1)}, f32[256,256]{1,0:T(8,128)}, f32[256,256]{1,0:T(8,128)S(1)}) custom-call(s32[1]{0:T(128)} %bitcast.3.core, f32[768,256]{1,0:T(8,128)} %get-tuple-element.62.small, f32[768,256]{1,0:T(8,128)} %collective-permute-done.23.other), custom_call_target="tpu_custom_call" | custom-call | flops 268435456 | tf_op jit(solution)/shard_map/finish/pallas_call | solution.py:275
  117.8 4.5 %pick.1 = bf16[2,16,64,512]{3,2,1,0:T(8,128)(2,1)} custom-call(s32[2,16]{1,0:T(2,128)S(1)} %fusion.5.places, bf16[2,256,512]{2,1,0:T(8,128)(2,1)S(1)} %get-tuple-element.65.mats, bf16[2048,768]{1,0:T(8,128)(2,1)S(1)} %copy-done.2, bf16[256,2048]{1,0:T(8,128)(2,1)S(1)} %collective-permute-done.24.piece0, ...), custom_call_target="tpu_custom_call" | custom-call | flops 1073741824 | tf_op jit(solution)/shard_map/pick/pallas_call | solution.py:199
  122.2 4.7 %all-to-all-start = ((bf16[8,4,64,512]{3,2,1,0:T(8,128)(2,1)}), bf16[8,4,64,512]{3,2,1,0:T(8,128)(2,1)S(1)}, u32[]{:S(2)}, u32[]{:S(2)}) async-start(bf16[8,4,64,512]{3,2,1,0:T(8,128)(2,1)} %bitcast.18), calls=%async_computation | async-start | bytes 4194304 | tf_op jit(solution)/shard_map/all_to_all | solution.py:456
  127.0 0.8 pad_maximum_fusion
  128.0 2.2 %collective-permute-done.17 = bf16[512,512]{1,0:T(8,128)(2,1)} collective-permute-done((bf16[512,512]{1,0:T(8,128)(2,1)}, bf16[512,512]{1,0:T(8,128)(2,1)}, u32[]{:S(2)}, u32[]{:S(2)}) %collective-permute-start.17) | collective-permute-done | bytes 524320 | tf_op jit(solution)/shard_map/ppermute | solution.py:18
  130.1 1.9 %slice_select_fusion = (bf16[512,256]{1,0:T(8,128)(2,1)}, bf16[1,512,256]{2,1,0:T(8,128)(2,1)}, bf16[1,512,256]{2,1,0:T(8,128)(2,1)}) fusion(bf16[512,512]{1,0:T(8,128)(2,1)} %collective-permute-done.17, pred[]{:T(512)S(6)} %eq.25, bf16[512,768]{1,0:T(8,128)(2,1)S(1)} %get-tuple-element.53.refs_0_), kind=kLoop, calls=%fused_computation.12 | loop fusion | flops 524288 | bytes 2097153 | tf_op jit(solution)/shard_map/jit(_where)/select_n | solution.py:380
  132.1 0.8 constant_dynamic-slice_fusion.1.band
  132.8 1.0 constant_dynamic-slice_fusion.piece
  133.8 1.0 update.1
  134.9 18.3 %all-to-all-done = bf16[8,4,64,512]{3,2,1,0:T(8,128)(2,1)S(1)} async-done(((bf16[8,4,64,512]{3,2,1,0:T(8,128)(2,1)}), bf16[8,4,64,512]{3,2,1,0:T(8,128)(2,1)S(1)}, u32[]{:S(2)}, u32[]{:S(2)}) %all-to-all-start) | async-done | bytes 2097184 | tf_op jit(solution)/shard_map/all_to_all | solution.py:456
  153.2 3.0 %settle.1 = f32[4,512,512]{2,1,0:T(8,128)} custom-call(bf16[2,4,4,64,512]{4,3,2,1,0:T(8,128)(2,1)S(1)} %bitcast.58), custom_call_target="tpu_custom_call" | custom-call | flops 1073741824 | tf_op jit(solution)/shard_map/settle/pallas_call | solution.py:324
  (63 shorter events, 1.8 us)
Async XLA Ops:
  0.6 10.9 %copy-start.12 = (bf16[2048,256]{1,0:T(8,128)(2,1)S(1)}, bf16[2048,256]{1,0:T(8,128)(2,1)}, u32[]{:S(2)}) copy-start(bf16[2048,256]{1,0:T(8,128)(2,1)} %param.9) | copy-start | bytes 3145732
  0.6 25.9 %collective-permute-start.8 = (bf16[2,1,2048,256]{3,2,1,0:T(8,128)(2,1)}, bf16[2,1,2048,256]{3,2,1,0:T(8,128)(2,1)}, u32[]{:S(2)}, u32[]{:S(2)}) collective-permute-start(bf16[2,1,2048,256]{3,2,1,0:T(8,128)(2,1)} %param.7), channel_id=1, source_target_pairs={{0,4},{4,0},{8,12},{12,8},{16,20},{20,16},{24,28},{28,24},{32,36},... | collective-permute-start | bytes 6291464 | tf_op jit(solution)/shard_map/ppermute | solution.py:18
  3.3 8.2 %copy-start.13 = (bf16[2048,256]{1,0:T(8,128)(2,1)S(1)}, bf16[2048,256]{1,0:T(8,128)(2,1)}, u32[]{:S(2)}) copy-start(bf16[2048,256]{1,0:T(8,128)(2,1)} %param.8) | copy-start | bytes 3145732
  3.3 2.8 %collective-permute-start = (bf16[512,64]{1,0:T(8,128)(2,1)S(1)}, bf16[512,64]{1,0:T(8,128)(2,1)S(1)}, u32[]{:S(2)}, u32[]{:S(2)}) collective-permute-start(bf16[512,64]{1,0:T(8,128)(2,1)S(1)} %select_bitcast_fusion.2), channel_id=1, source_target_pairs={{0,4},{4,0},{8,12},{12,8},{16,20},{20,16},{24,28},{28,24},{32,36},... | collective-permute-start | bytes 196616 | tf_op jit(solution)/shard_map/ppermute | solution.py:18
  6.3 13.8 %copy-start.14 = (s32[1,4,4]{2,1,0:T(4,128)S(1)}, s32[1,4,4]{2,1,0:T(4,128)}, u32[]{:S(2)}) copy-start(s32[1,4,4]{2,1,0:T(4,128)} %param.13) | copy-start | bytes 196
  6.3 13.9 %copy-start.15 = (s32[2,1]{0,1:T(1,128)S(1)}, s32[2,1]{0,1:T(1,128)}, u32[]{:S(2)}) copy-start(s32[2,1]{0,1:T(1,128)} %param.12) | copy-start | bytes 28
  6.3 6.3 %collective-permute-start.1 = (bf16[512,128]{1,0:T(8,128)(2,1)S(1)}, bf16[512,128]{1,0:T(8,128)(2,1)S(1)}, u32[]{:S(2)}, u32[]{:S(2)}) collective-permute-start(bf16[512,128]{1,0:T(8,128)(2,1)S(1)} %pad_maximum_fusion.1.refs_0_), channel_id=1, source_target_pairs={{0,8},{4,36},{8,16},{12,44},{16,24},{20,52},{24,0},{28,60},{32,40}... | collective-permute-start | bytes 393224 | tf_op jit(solution)/shard_map/ppermute | solution.py:38
  8.1 4.5 %collective-permute-start.2 = (bf16[512,128]{1,0:T(8,128)(2,1)S(1)}, bf16[512,128]{1,0:T(8,128)(2,1)S(1)}, u32[]{:S(2)}, u32[]{:S(2)}) collective-permute-start(bf16[512,128]{1,0:T(8,128)(2,1)S(1)} %pad_maximum_fusion.1.refs_0_), channel_id=1, source_target_pairs={{0,24},{4,100},{8,0},{12,108},{16,8},{20,116},{24,16},{28,124},{32... | collective-permute-start | bytes 393224 | tf_op jit(solution)/shard_map/ppermute | solution.py:38
  10.3 5.6 %collective-permute-start.3 = (bf16[512,128]{1,0:T(8,128)(2,1)S(1)}, bf16[512,128]{1,0:T(8,128)(2,1)S(1)}, u32[]{:S(2)}, u32[]{:S(2)}) collective-permute-start(bf16[512,128]{1,0:T(8,128)(2,1)S(1)} %pad_maximum_fusion.1.refs_0_), channel_id=1, source_target_pairs={{0,16},{4,68},{8,24},{12,76},{16,0},{20,84},{24,8},{28,92},{32,48}... | collective-permute-start | bytes 393224 | tf_op jit(solution)/shard_map/ppermute | solution.py:38
  15.9 13.0 %collective-permute-start.4 = (bf16[2048,128]{1,0:T(8,128)(2,1)S(1)}, bf16[2048,128]{1,0:T(8,128)(2,1)S(1)}, u32[]{:S(2)}, u32[]{:S(2)}) collective-permute-start(bf16[2048,128]{1,0:T(8,128)(2,1)S(1)} %join.2.refs_0_), channel_id=1, source_target_pairs={{0,32},{4,12},{8,40},{12,20},{16,48},{20,28},{24,56},{28,4},{32,64... | collective-permute-start | bytes 1572872 | tf_op jit(solution)/shard_map/ppermute | solution.py:38
  17.0 13.4 %collective-permute-start.5 = (bf16[2048,128]{1,0:T(8,128)(2,1)S(1)}, bf16[2048,128]{1,0:T(8,128)(2,1)}, u32[]{:S(2)}, u32[]{:S(2)}) collective-permute-start(bf16[2048,128]{1,0:T(8,128)(2,1)S(1)} %join.2.refs_0_), channel_id=1, source_target_pairs={{0,96},{4,28},{8,104},{12,4},{16,112},{20,12},{24,120},{28,20},{32... | collective-permute-start | bytes 1572872 | tf_op jit(solution)/shard_map/ppermute | solution.py:38
  18.7 13.5 %collective-permute-start.6 = (bf16[2048,128]{1,0:T(8,128)(2,1)S(1)}, bf16[2048,128]{1,0:T(8,128)(2,1)}, u32[]{:S(2)}, u32[]{:S(2)}) collective-permute-start(bf16[2048,128]{1,0:T(8,128)(2,1)S(1)} %join.2.refs_0_), channel_id=1, source_target_pairs={{0,64},{4,20},{8,72},{12,28},{16,80},{20,4},{24,88},{28,12},{32,96... | collective-permute-start | bytes 1572872 | tf_op jit(solution)/shard_map/ppermute | solution.py:38
  20.3 4.3 %collective-permute-start.7 = (f32[1,18]{1,0:T(1,128)S(1)}, f32[1,18]{1,0:T(1,128)S(1)}, u32[]{:S(2)}, u32[]{:S(2)}) collective-permute-start(f32[1,18]{1,0:T(1,128)S(1)} %add_convert_fusion), channel_id=1, source_target_pairs={{0,4},{4,0},{8,12},{12,8},{16,20},{20,16},{24,28},{28,24},{32,36},... | collective-permute-start | bytes 224 | tf_op jit(solution)/shard_map/ppermute | solution.py:18
  29.0 0.8 copy-start.10
  32.2 1.0 copy-start.11
  37.2 4.5 %collective-permute-start.9 = (bf16[128,512]{1,0:T(8,128)(2,1)S(1)}, bf16[128,512]{1,0:T(8,128)(2,1)S(1)}, u32[]{:S(2)}, u32[]{:S(2)}) collective-permute-start(bf16[128,512]{1,0:T(8,128)(2,1)S(1)} %get-tuple-element.44), channel_id=1, source_target_pairs={{0,1},{1,2},{2,3},{3,0},{4,7},{5,4},{6,5},{7,6},{8,9},{9,10},{10,1... | collective-permute-start | bytes 393224 | tf_op jit(solution)/shard_map/ppermute | solution.py:27
  39.7 7.6 %collective-permute-start.10 = (bf16[128,512]{1,0:T(8,128)(2,1)S(1)}, bf16[128,512]{1,0:T(8,128)(2,1)S(1)}, u32[]{:S(2)}, u32[]{:S(2)}) collective-permute-start(bf16[128,512]{1,0:T(8,128)(2,1)S(1)} %get-tuple-element.45), channel_id=1, source_target_pairs={{0,3},{1,0},{2,1},{3,2},{4,5},{5,6},{6,7},{7,4},{8,11},{9,8},{10,9... | collective-permute-start | bytes 393224 | tf_op jit(solution)/shard_map/ppermute | solution.py:27
  39.7 7.6 %collective-permute-start.11 = (bf16[128,512]{1,0:T(8,128)(2,1)S(1)}, bf16[128,512]{1,0:T(8,128)(2,1)S(1)}, u32[]{:S(2)}, u32[]{:S(2)}) collective-permute-start(bf16[128,512]{1,0:T(8,128)(2,1)S(1)} %get-tuple-element.48), channel_id=1, source_target_pairs={{0,2},{1,3},{2,0},{3,1},{4,6},{5,7},{6,4},{7,5},{8,10},{9,11},{10,... | collective-permute-start | bytes 393224 | tf_op jit(solution)/shard_map/ppermute | solution.py:27
  47.4 9.6 %collective-permute-start.12 = (bf16[128,2048]{1,0:T(8,128)(2,1)S(1)}, bf16[128,2048]{1,0:T(8,128)(2,1)S(1)}, u32[]{:S(2)}, u32[]{:S(2)}) collective-permute-start(bf16[128,2048]{1,0:T(8,128)(2,1)S(1)} %constant_dynamic-update-slice_fusion.refs_0_), channel_id=1, source_target_pairs={{0,8},{4,36},{8,16},{12,44},{16,24},{20,52},{24,0},{28,60},{32,40}... | collective-permute-start | bytes 1572872 | tf_op jit(solution)/shard_map/ppermute | solution.py:38
  47.8 22.0 %collective-permute-start.18 = (bf16[512,768]{1,0:T(8,128)(2,1)S(1)}, bf16[512,768]{1,0:T(8,128)(2,1)S(1)}, u32[]{:S(2)}, u32[]{:S(2)}) collective-permute-start(bf16[512,768]{1,0:T(8,128)(2,1)S(1)} %get-tuple-element.53.refs_0_), channel_id=1, source_target_pairs={{0,1},{1,2},{2,3},{3,0},{4,7},{5,4},{6,5},{7,6},{8,9},{9,10},{10,1... | collective-permute-start | bytes 2359304 | tf_op jit(solution)/shard_map/ppermute | solution.py:27
  48.9 21.2 %collective-permute-start.19 = (bf16[512,768]{1,0:T(8,128)(2,1)S(1)}, bf16[512,768]{1,0:T(8,128)(2,1)S(1)}, u32[]{:S(2)}, u32[]{:S(2)}) collective-permute-start(bf16[512,768]{1,0:T(8,128)(2,1)S(1)} %get-tuple-element.53.refs_0_), channel_id=1, source_target_pairs={{0,3},{1,0},{2,1},{3,2},{4,5},{5,6},{6,7},{7,4},{8,11},{9,8},{10,9... | collective-permute-start | bytes 2359304 | tf_op jit(solution)/shard_map/ppermute | solution.py:27
  49.2 32.3 %collective-permute-start.20 = (bf16[512,768]{1,0:T(8,128)(2,1)S(1)}, bf16[512,768]{1,0:T(8,128)(2,1)S(1)}, u32[]{:S(2)}, u32[]{:S(2)}) collective-permute-start(bf16[512,768]{1,0:T(8,128)(2,1)S(1)} %get-tuple-element.53.refs_0_), channel_id=1, source_target_pairs={{0,2},{1,3},{2,0},{3,1},{4,6},{5,7},{6,4},{7,5},{8,10},{9,11},{10,... | collective-permute-start | bytes 2359304 | tf_op jit(solution)/shard_map/ppermute | solution.py:27
  50.2 14.3 %collective-permute-start.13 = (bf16[128,2048]{1,0:T(8,128)(2,1)S(1)}, bf16[128,2048]{1,0:T(8,128)(2,1)S(1)}, u32[]{:S(2)}, u32[]{:S(2)}) collective-permute-start(bf16[128,2048]{1,0:T(8,128)(2,1)S(1)} %constant_dynamic-update-slice_fusion.refs_0_), channel_id=1, source_target_pairs={{0,24},{4,100},{8,0},{12,108},{16,8},{20,116},{24,16},{28,124},{32... | collective-permute-start | bytes 1572872 | tf_op jit(solution)/shard_map/ppermute | solution.py:38
  57.0 9.8 %collective-permute-start.14 = (bf16[128,2048]{1,0:T(8,128)(2,1)S(1)}, bf16[128,2048]{1,0:T(8,128)(2,1)S(1)}, u32[]{:S(2)}, u32[]{:S(2)}) collective-permute-start(bf16[128,2048]{1,0:T(8,128)(2,1)S(1)} %constant_dynamic-update-slice_fusion.refs_0_), channel_id=1, source_target_pairs={{0,16},{4,68},{8,24},{12,76},{16,0},{20,84},{24,8},{28,92},{32,48}... | collective-permute-start | bytes 1572872 | tf_op jit(solution)/shard_map/ppermute | solution.py:38
  67.0 26.2 %copy-start.6 = (bf16[256,2048]{1,0:T(8,128)(2,1)}, bf16[256,2048]{1,0:T(8,128)(2,1)S(1)}, u32[]{:S(2)}) copy-start(bf16[256,2048]{1,0:T(8,128)(2,1)S(1)} %get-tuple-element.54.refs_1_) | copy-start | bytes 3145732
  67.0 20.5 %collective-permute-start.15 = (bf16[256,2048]{1,0:T(8,128)(2,1)S(1)}, bf16[256,2048]{1,0:T(8,128)(2,1)}, u32[]{:S(2)}, u32[]{:S(2)}) collective-permute-start(bf16[256,2048]{1,0:T(8,128)(2,1)S(1)} %get-tuple-element.49.refs_1_), channel_id=1, source_target_pairs={{0,32},{4,12},{8,40},{12,20},{16,48},{20,28},{24,56},{28,4},{32,64... | collective-permute-start | bytes 3145736 | tf_op jit(solution)/shard_map/ppermute | solution.py:38
  69.4 18.1 %collective-permute-start.16 = (bf16[256,2048]{1,0:T(8,128)(2,1)S(1)}, bf16[256,2048]{1,0:T(8,128)(2,1)S(1)}, u32[]{:S(2)}, u32[]{:S(2)}) collective-permute-start(bf16[256,2048]{1,0:T(8,128)(2,1)S(1)} %get-tuple-element.49.refs_1_), channel_id=1, source_target_pairs={{0,96},{4,28},{8,104},{12,4},{16,112},{20,12},{24,120},{28,20},{32... | collective-permute-start | bytes 3145736 | tf_op jit(solution)/shard_map/ppermute | solution.py:38
  81.5 15.8 %collective-permute-start.21 = (bf16[256,2048]{1,0:T(8,128)(2,1)S(1)}, bf16[256,2048]{1,0:T(8,128)(2,1)S(1)}, u32[]{:S(2)}, u32[]{:S(2)}) collective-permute-start(bf16[256,2048]{1,0:T(8,128)(2,1)S(1)} %get-tuple-element.54.refs_1_), channel_id=1, source_target_pairs={{0,32},{4,12},{8,40},{12,20},{16,48},{20,28},{24,56},{28,4},{32,64... | collective-permute-start | bytes 3145736 | tf_op jit(solution)/shard_map/ppermute | solution.py:38
  85.5 14.0 %collective-permute-start.22 = (bf16[256,2048]{1,0:T(8,128)(2,1)S(1)}, bf16[256,2048]{1,0:T(8,128)(2,1)}, u32[]{:S(2)}, u32[]{:S(2)}) collective-permute-start(bf16[256,2048]{1,0:T(8,128)(2,1)S(1)} %get-tuple-element.54.refs_1_), channel_id=1, source_target_pairs={{0,96},{4,28},{8,104},{12,4},{16,112},{20,12},{24,120},{28,20},{32... | collective-permute-start | bytes 3145736 | tf_op jit(solution)/shard_map/ppermute | solution.py:38
  87.5 5.7 %copy-start = (bf16[2048,768]{1,0:T(8,128)(2,1)}, bf16[2048,768]{1,0:T(8,128)(2,1)S(1)}, u32[]{:S(2)}) copy-start(bf16[2048,768]{1,0:T(8,128)(2,1)S(1)} %get-tuple-element.60.refs_0_.whole) | copy-start | bytes 9437188
  87.5 30.2 %collective-permute-start.24 = (bf16[256,2048]{1,0:T(8,128)(2,1)}, bf16[256,2048]{1,0:T(8,128)(2,1)S(1)}, u32[]{:S(2)}, u32[]{:S(2)}) collective-permute-start(bf16[256,2048]{1,0:T(8,128)(2,1)} %collective-permute-done.15.refs_2_), channel_id=1, source_target_pairs={{0,32},{4,12},{8,40},{12,20},{16,48},{20,28},{24,56},{28,4},{32,64... | collective-permute-start | bytes 3145736 | tf_op jit(solution)/shard_map/ppermute | solution.py:38
  93.2 1.4 copy-start.3
  97.2 1.0 copy-start.8
  99.5 18.2 %collective-permute-start.25 = (bf16[256,2048]{1,0:T(8,128)(2,1)}, bf16[256,2048]{1,0:T(8,128)(2,1)S(1)}, u32[]{:S(2)}, u32[]{:S(2)}) collective-permute-start(bf16[256,2048]{1,0:T(8,128)(2,1)} %collective-permute-done.22.refs_3_), channel_id=1, source_target_pairs={{0,96},{4,28},{8,104},{12,4},{16,112},{20,12},{24,120},{28,20},{32... | collective-permute-start | bytes 3145736 | tf_op jit(solution)/shard_map/ppermute | solution.py:38
  100.7 14.5 %collective-permute-start.23 = (f32[768,256]{1,0:T(8,128)}, f32[768,256]{1,0:T(8,128)}, u32[]{:S(2)}, u32[]{:S(2)}) collective-permute-start(f32[768,256]{1,0:T(8,128)} %get-tuple-element.62.small), channel_id=1, source_target_pairs={{0,4},{4,0},{8,12},{12,8},{16,20},{20,16},{24,28},{28,24},{32,36},... | collective-permute-start | bytes 2359304 | tf_op jit(solution)/shard_map/ppermute | solution.py:18
  106.7 1.9 %copy-start.1 = (bf16[2048,768]{1,0:T(8,128)(2,1)S(1)}, bf16[2048,768]{1,0:T(8,128)(2,1)}, u32[]{:S(2)}) copy-start(bf16[2048,768]{1,0:T(8,128)(2,1)} %copy-done) | copy-start | bytes 9437188
  108.6 1.2 copy-start.7
  109.8 1.2 copy-start.9
  111.0 6.7 %copy-start.2 = (bf16[2048,768]{1,0:T(8,128)(2,1)S(1)}, bf16[2048,768]{1,0:T(8,128)(2,1)}, u32[]{:S(2)}) copy-start(bf16[2048,768]{1,0:T(8,128)(2,1)} %copy-done) | copy-start | bytes 9437188
  111.0 6.7 %copy-start.4 = (f32[768,768]{1,0:T(8,128)S(1)}, f32[768,768]{1,0:T(8,128)}, u32[]{:S(2)}) copy-start(f32[768,768]{1,0:T(8,128)} %copy-done.3) | copy-start | bytes 7077892
  122.2 31.0 %all-to-all-start = ((bf16[8,4,64,512]{3,2,1,0:T(8,128)(2,1)}), bf16[8,4,64,512]{3,2,1,0:T(8,128)(2,1)S(1)}, u32[]{:S(2)}, u32[]{:S(2)}) async-start(bf16[8,4,64,512]{3,2,1,0:T(8,128)(2,1)} %bitcast.18), calls=%async_computation | async-start | bytes 4194304 | tf_op jit(solution)/shard_map/all_to_all | solution.py:456
  127.0 6.8 %copy-start.5 = (f32[64,512]{1,0:T(8,128)S(1)}, f32[64,512]{1,0:T(8,128)}, u32[]{:S(2)}) copy-start(f32[64,512]{1,0:T(8,128)} %before.1) | copy-start | bytes 393220
  127.9 2.3 %collective-permute-start.17 = (bf16[512,512]{1,0:T(8,128)(2,1)}, bf16[512,512]{1,0:T(8,128)(2,1)}, u32[]{:S(2)}, u32[]{:S(2)}) collective-permute-start(bf16[512,512]{1,0:T(8,128)(2,1)} %pad_maximum_fusion), channel_id=1, source_target_pairs={{0,4},{4,0},{8,12},{12,8},{16,20},{20,16},{24,28},{28,24},{32,36},... | collective-permute-start | bytes 1572872 | tf_op jit(solution)/shard_map/ppermute | solution.py:18

commit v3 on v2

--- a/solution.py
+++ b/solution.py
@@ -159,9 +159,16 @@
 def pick_kernel(
     places, mats, whole, piece0, piece1, early0, early1, out, late0, late1, heads, staged, sems
 ):
-    done = early0.shape[0]
+    rows = piece0.shape[0]
+    done = late0.shape[0] - rows
     copies = copy_all(
-        [(early0, late0.at[pl.ds(0, done)]), (early1, late1.at[pl.ds(0, done)])], sems, 2
+        [
+            (early0.at[pl.ds(0, done)], late0.at[pl.ds(0, done)]),
+            (early0.at[pl.ds(done, rows)], late1.at[pl.ds(0, rows)]),
+            (early1, late1.at[pl.ds(rows, done - rows)]),
+        ],
+        sems,
+        2,
     )
     late0[done:, :] = jnp.dot(piece0[...], whole[...], preferred_element_type=F32)
     late1[done:, :] = jnp.dot(piece1[...], whole[...], preferred_element_type=F32)
@@ -195,7 +202,7 @@
     count = places.shape[1]
     rank = mats.shape[1]
     shape = (2, count, rank // 4, 2 * rank)
-    full = (early0.shape[0] + piece0.shape[0], early0.shape[1])
+    full = (4 * piece0.shape[0], early0.shape[1])
     return pl.pallas_call(
         pick_kernel,
         out_shape=jax.ShapeDtypeStruct(shape, BF),
@@ -206,7 +213,7 @@
             pltpu.VMEM(full, F32),
             pltpu.VMEM((count * rank // 4, rank), BF),
             pltpu.VMEM(shape, BF),
-            pltpu.SemaphoreType.DMA((4,)),
+            pltpu.SemaphoreType.DMA((5,)),
         ],
         compiler_params=pltpu.CompilerParams(vmem_limit_bytes=28 * 2**20),
         cost_estimate=pl.CostEstimate(
@@ -419,7 +426,7 @@
     before1, after1 = lax.optimization_barrier(sides(line1, 1))
     gathered0 = [line0, before0, after0, hop(before0, 1, 1)]
     whole, small = couple([solved, x_before, x_after, x_opposite])
-    early0 = multiply(whole, gathered0[:3])
+    early0 = multiply(whole, gathered0[:3] + [line1])
     after1, small, early0 = lax.optimization_barrier((after1, small, early0))
     gathered1 = [line1, before1, after1, hop(after1, 1, -1)]
     small_other = other_core(small)
@@ -445,7 +452,7 @@
     sy = slot_of(((j // 2) % 4 - my_y) % 4)
     sz = slot_of((j // 8 - my_z) % 4)
     places = (pick_core(sz, sy) * 4 + pick_core(sy, sz)) * 2 + j % 2
-    early1 = multiply(whole, gathered1[:3])
+    early1 = multiply(whole, gathered1[1:3])
     picked = pick(places, mats, whole, gathered0[3], gathered1[3], early0, early1)
     upper, _ = lax.optimization_barrier((head_u, picked))
     band = tile_size // 32

time: 157 us -> 160 us (1.019)
  starting transfers between devices: 43.4 us -> 47.2 us
  local copies, waits for them, and re-layouts: 13.1 us -> 9.71 us
  waiting for transfers between devices: 65.2 us -> 68.5 us
    ppermute x6, waiting for transfers between devices: 17.6 us -> 25.9 us  [along_x(): return lax.ppermute(x, ('row', 'col'), pairs)]
    ppermute x15, waiting for transfers between devices: 24.4 us -> 19.5 us  [hop(): return lax.ppermute(x, 'row', pairs)]
    all_to_all x1, starting transfers between devices: 4.73 us -> 8.98 us  [body(): lax.all_to_all(picked.reshape(8, slots, quarter, 2 * rank), ('row', 'col'...]
    unnamed x37 -> x29, local copies, waits for them, and re-layouts: 8.88 us -> 5.51 us
  transfers between devices with their start and end apart: 27 -> 27, of which waited for: 16 -> 17; matrix products, arithmetic and copies ran while one was open for 8% -> 8% of each run, Pallas kernels for 9% -> 9%
where the time goes in v3:
time: 160 us; the launch traced here: 159 us
  waiting for transfers between devices  68.5 us (43%)
  starting transfers between devices  47.2 us (30%)
  Pallas kernels  24.7 us (15%)
  local copies, waits for them, and re-layouts  9.71 us (6%)
  other arithmetic  8.39 us (5%)
    ppermute x6, waiting for transfers between devices, along_x(): return lax.ppermute(x, ('row', 'col'), pairs)  25.9 us
    ppermute x15, starting transfers between devices, hop(): return lax.ppermute(x, 'row', pairs)  21.8 us
    ppermute x15, waiting for transfers between devices, hop(): return lax.ppermute(x, 'row', pairs)  19.5 us
    all_to_all x1, waiting for transfers between devices, body(): lax.all_to_all(picked.reshape(8, slots, quarter, 2 * rank), ('row', 'col'...  18.3 us
    ppermute x5, starting transfers between devices, other_core(): return lax.ppermute(x, 'row', pairs)  10.1 us
    all_to_all x1, starting transfers between devices, body(): lax.all_to_all(picked.reshape(8, slots, quarter, 2 * rank), ('row', 'col'...  8.98 us
    pallas_call x2, Pallas kernels, multiply(): pl.pallas_call(multiply_kernel, out_shape=jax.ShapeDtypeStruct((count * r...  7.99 us
    ppermute x6, starting transfers between devices, along_x(): return lax.ppermute(x, ('row', 'col'), pairs)  6.3 us
  transfers between devices with their start and end apart: 27, of which 17 were waited for; matrix products, arithmetic and copies ran while one was open for 8% of the time, Pallas kernels for 9%

profile of v3, /device:TPU:1, one launch (start us, length us, event | category | flops | bytes accessed | tf_op | source)
XLA Modules:
  0.0 159.4 jit_solution(3758646259031046488)
XLA Ops:
  0.6 1.5 collective-permute-start.8
  2.1 0.9 fusion.9
  3.3 0.2 collective-permute-start
  3.5 2.6 %collective-permute-done = bf16[512,64]{1,0:T(8,128)(2,1)S(1)} collective-permute-done((bf16[512,64]{1,0:T(8,128)(2,1)S(1)}, bf16[512,64]{1,0:T(8,128)(2,1)S(1)}, u32[]{:S(2)}, u32[]{:S(2)}) %collective-permute-start) | collective-permute-done | bytes 65568 | tf_op jit(solution)/shard_map/ppermute | solution.py:18
  6.3 1.8 %collective-permute-start.1 = (bf16[512,128]{1,0:T(8,128)(2,1)S(1)}, bf16[512,128]{1,0:T(8,128)(2,1)S(1)}, u32[]{:S(2)}, u32[]{:S(2)}) collective-permute-start(bf16[512,128]{1,0:T(8,128)(2,1)S(1)} %pad_maximum_fusion.1.refs_0_), channel_id=1, source_target_pairs={{0,8},{4,36},{8,16},{12,44},{16,24},{20,52},{24,0},{28,60},{32,40}... | collective-permute-start | bytes 393224 | tf_op jit(solution)/shard_map/ppermute | solution.py:38
  8.1 2.2 %collective-permute-start.2 = (bf16[512,128]{1,0:T(8,128)(2,1)S(1)}, bf16[512,128]{1,0:T(8,128)(2,1)S(1)}, u32[]{:S(2)}, u32[]{:S(2)}) collective-permute-start(bf16[512,128]{1,0:T(8,128)(2,1)S(1)} %pad_maximum_fusion.1.refs_0_), channel_id=1, source_target_pairs={{0,24},{4,100},{8,0},{12,108},{16,8},{20,116},{24,16},{28,124},{32... | collective-permute-start | bytes 393224 | tf_op jit(solution)/shard_map/ppermute | solution.py:38
  10.3 1.2 collective-permute-start.3
  11.5 0.1 broadcast_select_fusion.refs_6_
  11.8 0.8 collective-permute-done.1.refs_1_
  12.6 3.3 %collective-permute-done.3.refs_3_ = bf16[512,128]{1,0:T(8,128)(2,1)S(1)} collective-permute-done((bf16[512,128]{1,0:T(8,128)(2,1)S(1)}, bf16[512,128]{1,0:T(8,128)(2,1)S(1)}, u32[]{:S(2)}, u32[]{:S(2)}) %collective-permute-start.3) | collective-permute-done | bytes 131104 | tf_op jit(solution)/shard_map/ppermute | solution.py:38
  15.9 1.1 collective-permute-start.4
  17.0 1.7 %collective-permute-start.5 = (bf16[2048,128]{1,0:T(8,128)(2,1)S(1)}, bf16[2048,128]{1,0:T(8,128)(2,1)S(1)}, u32[]{:S(2)}, u32[]{:S(2)}) collective-permute-start(bf16[2048,128]{1,0:T(8,128)(2,1)S(1)} %join.2.refs_0_), channel_id=1, source_target_pairs={{0,96},{4,28},{8,104},{12,4},{16,112},{20,12},{24,120},{28,20},{32... | collective-permute-start | bytes 1572872 | tf_op jit(solution)/shard_map/ppermute | solution.py:38
  18.7 1.4 collective-permute-start.6
  20.3 2.5 %collective-permute-start.7 = (f32[1,18]{1,0:T(1,128)S(1)}, f32[1,18]{1,0:T(1,128)S(1)}, u32[]{:S(2)}, u32[]{:S(2)}) collective-permute-start(f32[1,18]{1,0:T(1,128)S(1)} %add_convert_fusion), channel_id=1, source_target_pairs={{0,4},{4,0},{8,12},{12,8},{16,20},{20,16},{24,28},{28,24},{32,36},... | collective-permute-start | bytes 224 | tf_op jit(solution)/shard_map/ppermute | solution.py:18
  22.7 0.6 fusion.11
  23.3 1.3 iota_compare_fusion.2
  24.6 0.6 fusion.10
  25.2 1.3 iota_compare_fusion
  26.5 2.5 %broadcast_select_fusion.1 = (bf16[2048,256]{1,0:T(8,128)(2,1)S(1)}, bf16[2048,256]{1,0:T(8,128)(2,1)S(1)}) fusion(pred[]{:T(512)S(6)} %eq.25, bf16[2,1,2048,256]{3,2,1,0:T(8,128)(2,1)} %param.7, pred[256]{0:T(512)(128)(4,1)S(1)} %get-tuple-element.89, pred[256]{0:T(512)(128)(4,1)S(1)} %get-tuple-element.90, ...), kind=kLoop, calls=%fused_computation.9 | loop fusion | flops 4194304 | bytes 6292481 | tf_op jit(solution)/shard_map/jit(_where)/select_n | solution.py:387
  29.0 1.4 collective-permute-done.5.refs_2_
  30.4 1.7 %collective-permute-done.6.refs_3_ = bf16[2048,128]{1,0:T(8,128)(2,1)S(1)} collective-permute-done((bf16[2048,128]{1,0:T(8,128)(2,1)S(1)}, bf16[2048,128]{1,0:T(8,128)(2,1)S(1)}, u32[]{:S(2)}, u32[]{:S(2)}) %collective-permute-start.6) | collective-permute-done | bytes 524320 | tf_op jit(solution)/shard_map/ppermute | solution.py:38
  32.1 3.3 %solve.1 = (bf16[512,768]{1,0:T(8,128)(2,1)S(1)}, bf16[128,512]{1,0:T(8,128)(2,1)S(1)}, bf16[128,512]{1,0:T(8,128)(2,1)S(1)}, bf16[128,512]{1,0:T(8,128)(2,1)S(1)}, bf16[128,512]{1,0:T(8,128)(2,1)S(1)}) custom-call(s32[4]{0:T(128)S(1)} %pad_add_fusion.1.where, bf16[2048,128]{1,0:T(8,128)(2,1)S(1)} %join.2.refs_0_, ...), custom_call_target="tpu_custom_call" | custom-call | flops 1610612736 | tf_op jit(solution)/shard_map/solve/pallas_call | solution.py:108
  35.4 2.6 %collective-permute-start.9 = (bf16[128,512]{1,0:T(8,128)(2,1)S(1)}, bf16[128,512]{1,0:T(8,128)(2,1)S(1)}, u32[]{:S(2)}, u32[]{:S(2)}) collective-permute-start(bf16[128,512]{1,0:T(8,128)(2,1)S(1)} %get-tuple-element.44), channel_id=1, source_target_pairs={{0,1},{1,2},{2,3},{3,0},{4,7},{5,4},{6,5},{7,6},{8,9},{9,10},{10,1... | collective-permute-start | bytes 393224 | tf_op jit(solution)/shard_map/ppermute | solution.py:27
  37.9 1.7 %collective-permute-start.11 = (bf16[128,512]{1,0:T(8,128)(2,1)S(1)}, bf16[128,512]{1,0:T(8,128)(2,1)S(1)}, u32[]{:S(2)}, u32[]{:S(2)}) collective-permute-start(bf16[128,512]{1,0:T(8,128)(2,1)S(1)} %get-tuple-element.48), channel_id=1, source_target_pairs={{0,2},{1,3},{2,0},{3,1},{4,6},{5,7},{6,4},{7,5},{8,10},{9,11},{10,... | collective-permute-start | bytes 393224 | tf_op jit(solution)/shard_map/ppermute | solution.py:27
  39.7 0.2 collective-permute-done.9
  39.9 5.7 %collective-permute-done.10 = bf16[128,512]{1,0:T(8,128)(2,1)S(1)} collective-permute-done((bf16[128,512]{1,0:T(8,128)(2,1)S(1)}, bf16[128,512]{1,0:T(8,128)(2,1)S(1)}, u32[]{:S(2)}, u32[]{:S(2)}) %collective-permute-start.10) | collective-permute-done | bytes 131104 | tf_op jit(solution)/shard_map/ppermute | solution.py:27
  45.6 0.4 collective-permute-start.12
  46.0 2.4 %collective-permute-start.13 = (bf16[128,2048]{1,0:T(8,128)(2,1)S(1)}, bf16[128,2048]{1,0:T(8,128)(2,1)S(1)}, u32[]{:S(2)}, u32[]{:S(2)}) collective-permute-start(bf16[128,2048]{1,0:T(8,128)(2,1)S(1)} %constant_dynamic-update-slice_fusion.refs_0_), channel_id=1, source_target_pairs={{0,24},{4,100},{8,0},{12,108},{16,8},{20,116},{24,16},{28,124},{32... | collective-permute-start | bytes 1572872 | tf_op jit(solution)/shard_map/ppermute | solution.py:38
  48.3 1.3 collective-permute-start.14
  49.7 0.7 collective-permute-start.18
  50.4 0.8 collective-permute-start.19
  51.2 4.0 %collective-permute-done.12.refs_1_ = bf16[128,2048]{1,0:T(8,128)(2,1)S(1)} collective-permute-done((bf16[128,2048]{1,0:T(8,128)(2,1)S(1)}, bf16[128,2048]{1,0:T(8,128)(2,1)S(1)}, u32[]{:S(2)}, u32[]{:S(2)}) %collective-permute-start.12) | collective-permute-done | bytes 524320 | tf_op jit(solution)/shard_map/ppermute | solution.py:38
  55.2 0.5 collective-permute-start.20
  55.7 4.3 %collective-permute-done.13.refs_2_ = bf16[128,2048]{1,0:T(8,128)(2,1)S(1)} collective-permute-done((bf16[128,2048]{1,0:T(8,128)(2,1)S(1)}, bf16[128,2048]{1,0:T(8,128)(2,1)S(1)}, u32[]{:S(2)}, u32[]{:S(2)}) %collective-permute-start.13) | collective-permute-done | bytes 524320 | tf_op jit(solution)/shard_map/ppermute | solution.py:38
  60.1 0.9 collective-permute-done.14.refs_3_
  61.2 2.5 %collective-permute-start.15 = (bf16[256,2048]{1,0:T(8,128)(2,1)S(1)}, bf16[256,2048]{1,0:T(8,128)(2,1)}, u32[]{:S(2)}, u32[]{:S(2)}) collective-permute-start(bf16[256,2048]{1,0:T(8,128)(2,1)S(1)} %get-tuple-element.49.refs_1_), channel_id=1, source_target_pairs={{0,32},{4,12},{8,40},{12,20},{16,48},{20,28},{24,56},{28,4},{32,64... | collective-permute-start | bytes 3145736 | tf_op jit(solution)/shard_map/ppermute | solution.py:38
  63.6 0.3 collective-permute-start.16
  63.9 2.2 %collective-permute-done.18.refs_1_ = bf16[512,768]{1,0:T(8,128)(2,1)S(1)} collective-permute-done((bf16[512,768]{1,0:T(8,128)(2,1)S(1)}, bf16[512,768]{1,0:T(8,128)(2,1)S(1)}, u32[]{:S(2)}, u32[]{:S(2)}) %collective-permute-start.18) | collective-permute-done | bytes 786464 | tf_op jit(solution)/shard_map/ppermute | solution.py:27
  66.1 5.7 %collective-permute-done.19.refs_2_ = bf16[512,768]{1,0:T(8,128)(2,1)S(1)} collective-permute-done((bf16[512,768]{1,0:T(8,128)(2,1)S(1)}, bf16[512,768]{1,0:T(8,128)(2,1)S(1)}, u32[]{:S(2)}, u32[]{:S(2)}) %collective-permute-start.19) | collective-permute-done | bytes 786464 | tf_op jit(solution)/shard_map/ppermute | solution.py:27
  71.7 12.2 %collective-permute-done.20.refs_3_ = bf16[512,768]{1,0:T(8,128)(2,1)S(1)} collective-permute-done((bf16[512,768]{1,0:T(8,128)(2,1)S(1)}, bf16[512,768]{1,0:T(8,128)(2,1)S(1)}, u32[]{:S(2)}, u32[]{:S(2)}) %collective-permute-start.20) | collective-permute-done | bytes 786464 | tf_op jit(solution)/shard_map/ppermute | solution.py:27
  84.0 2.8 %collective-permute-start.21 = (bf16[256,2048]{1,0:T(8,128)(2,1)S(1)}, bf16[256,2048]{1,0:T(8,128)(2,1)S(1)}, u32[]{:S(2)}, u32[]{:S(2)}) collective-permute-start(bf16[256,2048]{1,0:T(8,128)(2,1)S(1)} %get-tuple-element.54.refs_4_), channel_id=1, source_target_pairs={{0,32},{4,12},{8,40},{12,20},{16,48},{20,28},{24,56},{28,4},{32,64... | collective-permute-start | bytes 3145736 | tf_op jit(solution)/shard_map/ppermute | solution.py:38
  86.7 2.0 %couple.1 = (bf16[2048,768]{1,0:T(8,128)(2,1)S(1)}, f32[768,256]{1,0:T(8,128)}) custom-call(bf16[512,768]{1,0:T(8,128)(2,1)S(1)} %get-tuple-element.53.refs_0_, bf16[512,768]{1,0:T(8,128)(2,1)S(1)} %collective-permute-done.18.refs_1_, bf16[512,768]{1,0:T(8,128)(2,1)S(1)} %collective-permute-done.19.refs_2_, bf16[512,768]{1,0:T(8,128)(2,1)S(1)} %collective-permute-done.20.refs_3_), custom_call_target="tpu_custom_call" | custom-call | flops 805306368 | tf_op jit(solution)/shard_map/couple/pallas_call | solution.py:240
  88.7 1.7 %collective-permute-start.24 = (bf16[256,2048]{1,0:T(8,128)(2,1)}, bf16[256,2048]{1,0:T(8,128)(2,1)}, u32[]{:S(2)}, u32[]{:S(2)}) collective-permute-start(bf16[256,2048]{1,0:T(8,128)(2,1)} %collective-permute-done.15.refs_2_), channel_id=1, source_target_pairs={{0,32},{4,12},{8,40},{12,20},{16,48},{20,28},{24,56},{28,4},{32,64... | collective-permute-start | bytes 3145736 | tf_op jit(solution)/shard_map/ppermute | solution.py:38
  90.4 4.7 %multiply.2.early0 = f32[1024,768]{1,0:T(8,128)S(1)} custom-call(bf16[2048,768]{1,0:T(8,128)(2,1)S(1)} %get-tuple-element.60.refs_0_.whole, bf16[256,2048]{1,0:T(8,128)(2,1)S(1)} %get-tuple-element.49.refs_1_, bf16[256,2048]{1,0:T(8,128)(2,1)} %collective-permute-done.15.refs_2_, bf16[256,2048]{1,0:T(8,128)(2,1)S(1)} %collective-permute-done.16.refs_3_, ...), custom_call_target="tpu_custom_call" | custom-call | flops 3221225472 | tf_op jit(solution)/shard_map/multiply/pallas_call | solution.py:142
  95.2 1.7 %copy-done.3 = f32[1024,768]{1,0:T(8,128)} copy-done((f32[1024,768]{1,0:T(8,128)}, f32[1024,768]{1,0:T(8,128)S(1)}, u32[]{:S(2)}) %copy-start.3) | copy-done | bytes 3145752
  96.9 2.2 %collective-permute-done.21.refs_1_ = bf16[256,2048]{1,0:T(8,128)(2,1)S(1)} collective-permute-done((bf16[256,2048]{1,0:T(8,128)(2,1)S(1)}, bf16[256,2048]{1,0:T(8,128)(2,1)S(1)}, u32[]{:S(2)}, u32[]{:S(2)}) %collective-permute-start.21) | collective-permute-done | bytes 1048608 | tf_op jit(solution)/shard_map/ppermute | solution.py:38
  99.1 1.0 copy-done.5
  100.1 0.7 collective-permute-done.22.refs_2_
  100.8 1.1 collective-permute-start.25
  101.9 5.9 %collective-permute-start.23 = (f32[768,256]{1,0:T(8,128)}, f32[768,256]{1,0:T(8,128)}, u32[]{:S(2)}, u32[]{:S(2)}) collective-permute-start(f32[768,256]{1,0:T(8,128)} %get-tuple-element.62.small), channel_id=1, source_target_pairs={{0,4},{4,0},{8,12},{12,8},{16,20},{20,16},{24,28},{28,24},{32,36},... | collective-permute-start | bytes 2359304 | tf_op jit(solution)/shard_map/ppermute | solution.py:18
  108.1 1.2 copy-done.6
  109.4 3.3 %multiply.3.early1 = f32[512,768]{1,0:T(8,128)S(1)} custom-call(bf16[2048,768]{1,0:T(8,128)(2,1)S(1)} %get-tuple-element.60.refs_0_.whole, bf16[256,2048]{1,0:T(8,128)(2,1)S(1)} %copy-done.6, bf16[256,2048]{1,0:T(8,128)(2,1)} %collective-permute-done.22.refs_2_), custom_call_target="tpu_custom_call" | custom-call | flops 1610612736 | tf_op jit(solution)/shard_map/multiply/pallas_call | solution.py:142
  112.6 2.5 %finish.1 = (bf16[2,256,512]{2,1,0:T(8,128)(2,1)S(1)}, f32[256,256]{1,0:T(8,128)}, f32[256,256]{1,0:T(8,128)S(1)}) custom-call(s32[1]{0:T(128)} %bitcast.3.core, f32[768,256]{1,0:T(8,128)} %get-tuple-element.62.small, f32[768,256]{1,0:T(8,128)} %collective-permute-done.23.other), custom_call_target="tpu_custom_call" | custom-call | flops 268435456 | tf_op jit(solution)/shard_map/finish/pallas_call | solution.py:282
  115.2 4.7 %pick.1 = bf16[2,16,64,512]{3,2,1,0:T(8,128)(2,1)S(1)} custom-call(s32[2,16]{1,0:T(2,128)S(1)} %fusion.5.places, bf16[2,256,512]{2,1,0:T(8,128)(2,1)S(1)} %get-tuple-element.65.mats, bf16[2048,768]{1,0:T(8,128)(2,1)S(1)} %get-tuple-element.60.refs_0_.whole, bf16[256,2048]{1,0:T(8,128)(2,1)} %collective-permute-done.24.piece0, ...), custom_call_target="tpu_custom_call" | custom-call | flops 1073741824 | tf_op jit(solution)/shard_map/pick/pallas_call | solution.py:206
  120.0 1.3 copy-done
  121.3 9.0 %all-to-all-start = ((bf16[8,4,64,512]{3,2,1,0:T(8,128)(2,1)}), bf16[8,4,64,512]{3,2,1,0:T(8,128)(2,1)S(1)}, u32[]{:S(2)}, u32[]{:S(2)}) async-start(bf16[8,4,64,512]{3,2,1,0:T(8,128)(2,1)} %bitcast.58), calls=%async_computation | async-start | bytes 4194304 | tf_op jit(solution)/shard_map/all_to_all | solution.py:463
  130.3 0.8 pad_maximum_fusion
  131.2 2.2 %collective-permute-done.17 = bf16[512,512]{1,0:T(8,128)(2,1)} collective-permute-done((bf16[512,512]{1,0:T(8,128)(2,1)}, bf16[512,512]{1,0:T(8,128)(2,1)}, u32[]{:S(2)}, u32[]{:S(2)}) %collective-permute-start.17) | collective-permute-done | bytes 524320 | tf_op jit(solution)/shard_map/ppermute | solution.py:18
  133.4 1.9 %slice_select_fusion = (bf16[512,256]{1,0:T(8,128)(2,1)}, bf16[1,512,256]{2,1,0:T(8,128)(2,1)}, bf16[1,512,256]{2,1,0:T(8,128)(2,1)}) fusion(bf16[512,512]{1,0:T(8,128)(2,1)} %collective-permute-done.17, pred[]{:T(512)S(6)} %eq.25, bf16[512,768]{1,0:T(8,128)(2,1)S(1)} %copy-done.2), kind=kLoop, calls=%fused_computation.12 | loop fusion | flops 524288 | bytes 2097153 | tf_op jit(solution)/shard_map/jit(_where)/select_n | solution.py:387
  135.3 0.8 constant_dynamic-slice_fusion.1.band
  136.1 1.0 constant_dynamic-slice_fusion.piece
  137.1 1.0 update.1
  138.1 18.3 %all-to-all-done = bf16[8,4,64,512]{3,2,1,0:T(8,128)(2,1)S(1)} async-done(((bf16[8,4,64,512]{3,2,1,0:T(8,128)(2,1)}), bf16[8,4,64,512]{3,2,1,0:T(8,128)(2,1)S(1)}, u32[]{:S(2)}, u32[]{:S(2)}) %all-to-all-start) | async-done | bytes 2097184 | tf_op jit(solution)/shard_map/all_to_all | solution.py:463
  156.5 3.0 %settle.1 = f32[4,512,512]{2,1,0:T(8,128)} custom-call(bf16[2,4,4,64,512]{4,3,2,1,0:T(8,128)(2,1)S(1)} %bitcast.59), custom_call_target="tpu_custom_call" | custom-call | flops 1073741824 | tf_op jit(solution)/shard_map/settle/pallas_call | solution.py:331
  (55 shorter events, 1.5 us)
Async XLA Ops:
  0.6 10.9 %copy-start.8 = (bf16[2048,256]{1,0:T(8,128)(2,1)S(1)}, bf16[2048,256]{1,0:T(8,128)(2,1)}, u32[]{:S(2)}) copy-start(bf16[2048,256]{1,0:T(8,128)(2,1)} %param.9) | copy-start | bytes 3145732
  0.6 25.9 %collective-permute-start.8 = (bf16[2,1,2048,256]{3,2,1,0:T(8,128)(2,1)}, bf16[2,1,2048,256]{3,2,1,0:T(8,128)(2,1)}, u32[]{:S(2)}, u32[]{:S(2)}) collective-permute-start(bf16[2,1,2048,256]{3,2,1,0:T(8,128)(2,1)} %param.7), channel_id=1, source_target_pairs={{0,4},{4,0},{8,12},{12,8},{16,20},{20,16},{24,28},{28,24},{32,36},... | collective-permute-start | bytes 6291464 | tf_op jit(solution)/shard_map/ppermute | solution.py:18
  3.3 8.2 %copy-start.9 = (bf16[2048,256]{1,0:T(8,128)(2,1)S(1)}, bf16[2048,256]{1,0:T(8,128)(2,1)}, u32[]{:S(2)}) copy-start(bf16[2048,256]{1,0:T(8,128)(2,1)} %param.8) | copy-start | bytes 3145732
  3.3 2.8 %collective-permute-start = (bf16[512,64]{1,0:T(8,128)(2,1)S(1)}, bf16[512,64]{1,0:T(8,128)(2,1)S(1)}, u32[]{:S(2)}, u32[]{:S(2)}) collective-permute-start(bf16[512,64]{1,0:T(8,128)(2,1)S(1)} %select_bitcast_fusion.2), channel_id=1, source_target_pairs={{0,4},{4,0},{8,12},{12,8},{16,20},{20,16},{24,28},{28,24},{32,36},... | collective-permute-start | bytes 196616 | tf_op jit(solution)/shard_map/ppermute | solution.py:18
  6.3 13.8 %copy-start.10 = (s32[1,4,4]{2,1,0:T(4,128)S(1)}, s32[1,4,4]{2,1,0:T(4,128)}, u32[]{:S(2)}) copy-start(s32[1,4,4]{2,1,0:T(4,128)} %param.13) | copy-start | bytes 196
  6.3 13.9 %copy-start.11 = (s32[2,1]{0,1:T(1,128)S(1)}, s32[2,1]{0,1:T(1,128)}, u32[]{:S(2)}) copy-start(s32[2,1]{0,1:T(1,128)} %param.12) | copy-start | bytes 28
  6.3 6.3 %collective-permute-start.1 = (bf16[512,128]{1,0:T(8,128)(2,1)S(1)}, bf16[512,128]{1,0:T(8,128)(2,1)S(1)}, u32[]{:S(2)}, u32[]{:S(2)}) collective-permute-start(bf16[512,128]{1,0:T(8,128)(2,1)S(1)} %pad_maximum_fusion.1.refs_0_), channel_id=1, source_target_pairs={{0,8},{4,36},{8,16},{12,44},{16,24},{20,52},{24,0},{28,60},{32,40}... | collective-permute-start | bytes 393224 | tf_op jit(solution)/shard_map/ppermute | solution.py:38
  8.1 4.5 %collective-permute-start.2 = (bf16[512,128]{1,0:T(8,128)(2,1)S(1)}, bf16[512,128]{1,0:T(8,128)(2,1)S(1)}, u32[]{:S(2)}, u32[]{:S(2)}) collective-permute-start(bf16[512,128]{1,0:T(8,128)(2,1)S(1)} %pad_maximum_fusion.1.refs_0_), channel_id=1, source_target_pairs={{0,24},{4,100},{8,0},{12,108},{16,8},{20,116},{24,16},{28,124},{32... | collective-permute-start | bytes 393224 | tf_op jit(solution)/shard_map/ppermute | solution.py:38
  10.3 5.6 %collective-permute-start.3 = (bf16[512,128]{1,0:T(8,128)(2,1)S(1)}, bf16[512,128]{1,0:T(8,128)(2,1)S(1)}, u32[]{:S(2)}, u32[]{:S(2)}) collective-permute-start(bf16[512,128]{1,0:T(8,128)(2,1)S(1)} %pad_maximum_fusion.1.refs_0_), channel_id=1, source_target_pairs={{0,16},{4,68},{8,24},{12,76},{16,0},{20,84},{24,8},{28,92},{32,48}... | collective-permute-start | bytes 393224 | tf_op jit(solution)/shard_map/ppermute | solution.py:38
  15.9 13.0 %collective-permute-start.4 = (bf16[2048,128]{1,0:T(8,128)(2,1)S(1)}, bf16[2048,128]{1,0:T(8,128)(2,1)S(1)}, u32[]{:S(2)}, u32[]{:S(2)}) collective-permute-start(bf16[2048,128]{1,0:T(8,128)(2,1)S(1)} %join.2.refs_0_), channel_id=1, source_target_pairs={{0,32},{4,12},{8,40},{12,20},{16,48},{20,28},{24,56},{28,4},{32,64... | collective-permute-start | bytes 1572872 | tf_op jit(solution)/shard_map/ppermute | solution.py:38
  17.0 13.4 %collective-permute-start.5 = (bf16[2048,128]{1,0:T(8,128)(2,1)S(1)}, bf16[2048,128]{1,0:T(8,128)(2,1)S(1)}, u32[]{:S(2)}, u32[]{:S(2)}) collective-permute-start(bf16[2048,128]{1,0:T(8,128)(2,1)S(1)} %join.2.refs_0_), channel_id=1, source_target_pairs={{0,96},{4,28},{8,104},{12,4},{16,112},{20,12},{24,120},{28,20},{32... | collective-permute-start | bytes 1572872 | tf_op jit(solution)/shard_map/ppermute | solution.py:38
  18.7 13.4 %collective-permute-start.6 = (bf16[2048,128]{1,0:T(8,128)(2,1)S(1)}, bf16[2048,128]{1,0:T(8,128)(2,1)S(1)}, u32[]{:S(2)}, u32[]{:S(2)}) collective-permute-start(bf16[2048,128]{1,0:T(8,128)(2,1)S(1)} %join.2.refs_0_), channel_id=1, source_target_pairs={{0,64},{4,20},{8,72},{12,28},{16,80},{20,4},{24,88},{28,12},{32,96... | collective-permute-start | bytes 1572872 | tf_op jit(solution)/shard_map/ppermute | solution.py:38
  20.3 4.3 %collective-permute-start.7 = (f32[1,18]{1,0:T(1,128)S(1)}, f32[1,18]{1,0:T(1,128)S(1)}, u32[]{:S(2)}, u32[]{:S(2)}) collective-permute-start(f32[1,18]{1,0:T(1,128)S(1)} %add_convert_fusion), channel_id=1, source_target_pairs={{0,4},{4,0},{8,12},{12,8},{16,20},{20,16},{24,28},{28,24},{32,36},... | collective-permute-start | bytes 224 | tf_op jit(solution)/shard_map/ppermute | solution.py:18
  35.4 53.4 %copy-start.1 = (bf16[512,768]{1,0:T(8,128)(2,1)}, bf16[512,768]{1,0:T(8,128)(2,1)S(1)}, u32[]{:S(2)}) copy-start(bf16[512,768]{1,0:T(8,128)(2,1)S(1)} %get-tuple-element.53.refs_0_) | copy-start | bytes 2359300
  35.4 4.5 %collective-permute-start.9 = (bf16[128,512]{1,0:T(8,128)(2,1)S(1)}, bf16[128,512]{1,0:T(8,128)(2,1)S(1)}, u32[]{:S(2)}, u32[]{:S(2)}) collective-permute-start(bf16[128,512]{1,0:T(8,128)(2,1)S(1)} %get-tuple-element.44), channel_id=1, source_target_pairs={{0,1},{1,2},{2,3},{3,0},{4,7},{5,4},{6,5},{7,6},{8,9},{9,10},{10,1... | collective-permute-start | bytes 393224 | tf_op jit(solution)/shard_map/ppermute | solution.py:27
  37.9 7.6 %collective-permute-start.10 = (bf16[128,512]{1,0:T(8,128)(2,1)S(1)}, bf16[128,512]{1,0:T(8,128)(2,1)S(1)}, u32[]{:S(2)}, u32[]{:S(2)}) collective-permute-start(bf16[128,512]{1,0:T(8,128)(2,1)S(1)} %get-tuple-element.45), channel_id=1, source_target_pairs={{0,3},{1,0},{2,1},{3,2},{4,5},{5,6},{6,7},{7,4},{8,11},{9,8},{10,9... | collective-permute-start | bytes 393224 | tf_op jit(solution)/shard_map/ppermute | solution.py:27
  37.9 7.6 %collective-permute-start.11 = (bf16[128,512]{1,0:T(8,128)(2,1)S(1)}, bf16[128,512]{1,0:T(8,128)(2,1)S(1)}, u32[]{:S(2)}, u32[]{:S(2)}) collective-permute-start(bf16[128,512]{1,0:T(8,128)(2,1)S(1)} %get-tuple-element.48), channel_id=1, source_target_pairs={{0,2},{1,3},{2,0},{3,1},{4,6},{5,7},{6,4},{7,5},{8,10},{9,11},{10,... | collective-permute-start | bytes 393224 | tf_op jit(solution)/shard_map/ppermute | solution.py:27
  45.6 9.6 %collective-permute-start.12 = (bf16[128,2048]{1,0:T(8,128)(2,1)S(1)}, bf16[128,2048]{1,0:T(8,128)(2,1)S(1)}, u32[]{:S(2)}, u32[]{:S(2)}) collective-permute-start(bf16[128,2048]{1,0:T(8,128)(2,1)S(1)} %constant_dynamic-update-slice_fusion.refs_0_), channel_id=1, source_target_pairs={{0,8},{4,36},{8,16},{12,44},{16,24},{20,52},{24,0},{28,60},{32,40}... | collective-permute-start | bytes 1572872 | tf_op jit(solution)/shard_map/ppermute | solution.py:38
  46.0 14.1 %collective-permute-start.13 = (bf16[128,2048]{1,0:T(8,128)(2,1)S(1)}, bf16[128,2048]{1,0:T(8,128)(2,1)S(1)}, u32[]{:S(2)}, u32[]{:S(2)}) collective-permute-start(bf16[128,2048]{1,0:T(8,128)(2,1)S(1)} %constant_dynamic-update-slice_fusion.refs_0_), channel_id=1, source_target_pairs={{0,24},{4,100},{8,0},{12,108},{16,8},{20,116},{24,16},{28,124},{32... | collective-permute-start | bytes 1572872 | tf_op jit(solution)/shard_map/ppermute | solution.py:38
  48.3 12.7 %collective-permute-start.14 = (bf16[128,2048]{1,0:T(8,128)(2,1)S(1)}, bf16[128,2048]{1,0:T(8,128)(2,1)S(1)}, u32[]{:S(2)}, u32[]{:S(2)}) collective-permute-start(bf16[128,2048]{1,0:T(8,128)(2,1)S(1)} %constant_dynamic-update-slice_fusion.refs_0_), channel_id=1, source_target_pairs={{0,16},{4,68},{8,24},{12,76},{16,0},{20,84},{24,8},{28,92},{32,48}... | collective-permute-start | bytes 1572872 | tf_op jit(solution)/shard_map/ppermute | solution.py:38
  49.7 16.4 %collective-permute-start.18 = (bf16[512,768]{1,0:T(8,128)(2,1)S(1)}, bf16[512,768]{1,0:T(8,128)(2,1)S(1)}, u32[]{:S(2)}, u32[]{:S(2)}) collective-permute-start(bf16[512,768]{1,0:T(8,128)(2,1)S(1)} %get-tuple-element.53.refs_0_), channel_id=1, source_target_pairs={{0,1},{1,2},{2,3},{3,0},{4,7},{5,4},{6,5},{7,6},{8,9},{9,10},{10,1... | collective-permute-start | bytes 2359304 | tf_op jit(solution)/shard_map/ppermute | solution.py:27
  50.4 21.4 %collective-permute-start.19 = (bf16[512,768]{1,0:T(8,128)(2,1)S(1)}, bf16[512,768]{1,0:T(8,128)(2,1)S(1)}, u32[]{:S(2)}, u32[]{:S(2)}) collective-permute-start(bf16[512,768]{1,0:T(8,128)(2,1)S(1)} %get-tuple-element.53.refs_0_), channel_id=1, source_target_pairs={{0,3},{1,0},{2,1},{3,2},{4,5},{5,6},{6,7},{7,4},{8,11},{9,8},{10,9... | collective-permute-start | bytes 2359304 | tf_op jit(solution)/shard_map/ppermute | solution.py:27
  55.2 28.8 %collective-permute-start.20 = (bf16[512,768]{1,0:T(8,128)(2,1)S(1)}, bf16[512,768]{1,0:T(8,128)(2,1)S(1)}, u32[]{:S(2)}, u32[]{:S(2)}) collective-permute-start(bf16[512,768]{1,0:T(8,128)(2,1)S(1)} %get-tuple-element.53.refs_0_), channel_id=1, source_target_pairs={{0,2},{1,3},{2,0},{3,1},{4,6},{5,7},{6,4},{7,5},{8,10},{9,11},{10,... | collective-permute-start | bytes 2359304 | tf_op jit(solution)/shard_map/ppermute | solution.py:27
  61.2 27.6 %collective-permute-start.15 = (bf16[256,2048]{1,0:T(8,128)(2,1)S(1)}, bf16[256,2048]{1,0:T(8,128)(2,1)}, u32[]{:S(2)}, u32[]{:S(2)}) collective-permute-start(bf16[256,2048]{1,0:T(8,128)(2,1)S(1)} %get-tuple-element.49.refs_1_), channel_id=1, source_target_pairs={{0,32},{4,12},{8,40},{12,20},{16,48},{20,28},{24,56},{28,4},{32,64... | collective-permute-start | bytes 3145736 | tf_op jit(solution)/shard_map/ppermute | solution.py:38
  63.6 25.1 %collective-permute-start.16 = (bf16[256,2048]{1,0:T(8,128)(2,1)S(1)}, bf16[256,2048]{1,0:T(8,128)(2,1)S(1)}, u32[]{:S(2)}, u32[]{:S(2)}) collective-permute-start(bf16[256,2048]{1,0:T(8,128)(2,1)S(1)} %get-tuple-element.49.refs_1_), channel_id=1, source_target_pairs={{0,96},{4,28},{8,104},{12,4},{16,112},{20,12},{24,120},{28,20},{32... | collective-permute-start | bytes 3145736 | tf_op jit(solution)/shard_map/ppermute | solution.py:38
  84.0 15.2 %collective-permute-start.21 = (bf16[256,2048]{1,0:T(8,128)(2,1)S(1)}, bf16[256,2048]{1,0:T(8,128)(2,1)S(1)}, u32[]{:S(2)}, u32[]{:S(2)}) collective-permute-start(bf16[256,2048]{1,0:T(8,128)(2,1)S(1)} %get-tuple-element.54.refs_4_), channel_id=1, source_target_pairs={{0,32},{4,12},{8,40},{12,20},{16,48},{20,28},{24,56},{28,4},{32,64... | collective-permute-start | bytes 3145736 | tf_op jit(solution)/shard_map/ppermute | solution.py:38
  86.7 14.0 %collective-permute-start.22 = (bf16[256,2048]{1,0:T(8,128)(2,1)S(1)}, bf16[256,2048]{1,0:T(8,128)(2,1)}, u32[]{:S(2)}, u32[]{:S(2)}) collective-permute-start(bf16[256,2048]{1,0:T(8,128)(2,1)S(1)} %get-tuple-element.54.refs_4_), channel_id=1, source_target_pairs={{0,96},{4,28},{8,104},{12,4},{16,112},{20,12},{24,120},{28,20},{32... | collective-permute-start | bytes 3145736 | tf_op jit(solution)/shard_map/ppermute | solution.py:38
  88.7 26.5 %collective-permute-start.24 = (bf16[256,2048]{1,0:T(8,128)(2,1)}, bf16[256,2048]{1,0:T(8,128)(2,1)}, u32[]{:S(2)}, u32[]{:S(2)}) collective-permute-start(bf16[256,2048]{1,0:T(8,128)(2,1)} %collective-permute-done.15.refs_2_), channel_id=1, source_target_pairs={{0,32},{4,12},{8,40},{12,20},{16,48},{20,28},{24,56},{28,4},{32,64... | collective-permute-start | bytes 3145736 | tf_op jit(solution)/shard_map/ppermute | solution.py:38
  95.2 1.7 %copy-start.3 = (f32[1024,768]{1,0:T(8,128)}, f32[1024,768]{1,0:T(8,128)S(1)}, u32[]{:S(2)}) copy-start(f32[1024,768]{1,0:T(8,128)S(1)} %multiply.2.early0) | copy-start | bytes 9437188
  99.1 1.0 copy-start.5
  100.8 14.4 %collective-permute-start.25 = (bf16[256,2048]{1,0:T(8,128)(2,1)}, bf16[256,2048]{1,0:T(8,128)(2,1)}, u32[]{:S(2)}, u32[]{:S(2)}) collective-permute-start(bf16[256,2048]{1,0:T(8,128)(2,1)} %collective-permute-done.22.refs_2_), channel_id=1, source_target_pairs={{0,96},{4,28},{8,104},{12,4},{16,112},{20,12},{24,120},{28,20},{32... | collective-permute-start | bytes 3145736 | tf_op jit(solution)/shard_map/ppermute | solution.py:38
  101.9 10.8 %collective-permute-start.23 = (f32[768,256]{1,0:T(8,128)}, f32[768,256]{1,0:T(8,128)}, u32[]{:S(2)}, u32[]{:S(2)}) collective-permute-start(f32[768,256]{1,0:T(8,128)} %get-tuple-element.62.small), channel_id=1, source_target_pairs={{0,4},{4,0},{8,12},{12,8},{16,20},{20,16},{24,28},{28,24},{32,36},... | collective-permute-start | bytes 2359304 | tf_op jit(solution)/shard_map/ppermute | solution.py:18
  108.1 1.2 copy-start.6
  109.4 5.8 %copy-start.4 = (f32[1024,768]{1,0:T(8,128)S(1)}, f32[1024,768]{1,0:T(8,128)}, u32[]{:S(2)}) copy-start(f32[1024,768]{1,0:T(8,128)} %copy-done.3) | copy-start | bytes 9437188
  119.9 1.3 copy-start
  121.3 9.0 %copy-start.2 = (bf16[512,768]{1,0:T(8,128)(2,1)S(1)}, bf16[512,768]{1,0:T(8,128)(2,1)}, u32[]{:S(2)}) copy-start(bf16[512,768]{1,0:T(8,128)(2,1)} %copy-done.1) | copy-start | bytes 2359300
  121.3 35.2 %all-to-all-start = ((bf16[8,4,64,512]{3,2,1,0:T(8,128)(2,1)}), bf16[8,4,64,512]{3,2,1,0:T(8,128)(2,1)S(1)}, u32[]{:S(2)}, u32[]{:S(2)}) async-start(bf16[8,4,64,512]{3,2,1,0:T(8,128)(2,1)} %bitcast.58), calls=%async_computation | async-start | bytes 4194304 | tf_op jit(solution)/shard_map/all_to_all | solution.py:463
  130.3 6.8 %copy-start.7 = (f32[64,512]{1,0:T(8,128)S(1)}, f32[64,512]{1,0:T(8,128)}, u32[]{:S(2)}) copy-start(f32[64,512]{1,0:T(8,128)} %before.1) | copy-start | bytes 393220
  131.1 2.3 %collective-permute-start.17 = (bf16[512,512]{1,0:T(8,128)(2,1)}, bf16[512,512]{1,0:T(8,128)(2,1)}, u32[]{:S(2)}, u32[]{:S(2)}) collective-permute-start(bf16[512,512]{1,0:T(8,128)(2,1)} %pad_maximum_fusion), channel_id=1, source_target_pairs={{0,4},{4,0},{8,12},{12,8},{16,20},{20,16},{24,28},{28,24},{32,36},... | collective-permute-start | bytes 1572872 | tf_op jit(solution)/shard_map/ppermute | solution.py:18

commit v4 on v2

--- a/solution.py
+++ b/solution.py
@@ -420,7 +420,7 @@
     gathered0 = [line0, before0, after0, hop(before0, 1, 1)]
     whole, small = couple([solved, x_before, x_after, x_opposite])
     early0 = multiply(whole, gathered0[:3])
-    after1, small, early0 = lax.optimization_barrier((after1, small, early0))
+    after1, _, _ = lax.optimization_barrier((after1, small, early0))
     gathered1 = [line1, before1, after1, hop(after1, 1, -1)]
     small_other = other_core(small)
     mats, coupling, gram_h = finish(own_core, small, small_other)

time: 157 us -> 158 us (level)
  starting transfers between devices: 43.4 us -> 46.1 us
  waiting for transfers between devices: 65.2 us -> 63.6 us
    ppermute x5, starting transfers between devices: 9.87 us -> 12.9 us  [other_core(): return lax.ppermute(x, 'row', pairs)]
    ppermute x6, waiting for transfers between devices: 17.6 us -> 15.4 us  [along_x(): return lax.ppermute(x, ('row', 'col'), pairs)]
    ppermute x5, waiting for transfers between devices: 4.79 us -> 6.73 us  [other_core(): return lax.ppermute(x, 'row', pairs)]
where the time goes in v4:
time: 158 us; the launch traced here: 157 us
  waiting for transfers between devices  63.6 us (40%)
  starting transfers between devices  46.1 us (29%)
  Pallas kernels  25.2 us (16%)
  local copies, waits for them, and re-layouts  13.1 us (8%)
  other arithmetic  8.38 us (5%)
    ppermute x15, waiting for transfers between devices, hop(): return lax.ppermute(x, 'row', pairs)  23 us
    ppermute x15, starting transfers between devices, hop(): return lax.ppermute(x, 'row', pairs)  20.5 us
    all_to_all x1, waiting for transfers between devices, body(): lax.all_to_all(picked.reshape(8, slots, quarter, 2 * rank), ('row', 'col'...  18.3 us
    ppermute x6, waiting for transfers between devices, along_x(): return lax.ppermute(x, ('row', 'col'), pairs)  15.4 us
    ppermute x5, starting transfers between devices, other_core(): return lax.ppermute(x, 'row', pairs)  12.9 us
    unnamed x37, local copies, waits for them, and re-layouts  8.88 us
    pallas_call x2, Pallas kernels, multiply(): pl.pallas_call(multiply_kernel, out_shape=jax.ShapeDtypeStruct((count * r...  8.05 us
    ppermute x6, starting transfers between devices, along_x(): return lax.ppermute(x, ('row', 'col'), pairs)  7.7 us
  transfers between devices with their start and end apart: 27, of which 16 were waited for; matrix products, arithmetic and copies ran while one was open for 8% of the time, Pallas kernels for 9%

profile of v4, /device:TPU:1, one launch (start us, length us, event | category | flops | bytes accessed | tf_op | source)
XLA Modules:
  0.0 157.3 jit_solution(12090863693154138291)
XLA Ops:
  0.6 1.5 collective-permute-start.8
  2.1 0.9 fusion.9
  3.5 2.6 %collective-permute-done = bf16[512,64]{1,0:T(8,128)(2,1)S(1)} collective-permute-done((bf16[512,64]{1,0:T(8,128)(2,1)S(1)}, bf16[512,64]{1,0:T(8,128)(2,1)S(1)}, u32[]{:S(2)}, u32[]{:S(2)}) %collective-permute-start) | collective-permute-done | bytes 65568 | tf_op jit(solution)/shard_map/ppermute | solution.py:18
  6.3 1.8 %collective-permute-start.1 = (bf16[512,128]{1,0:T(8,128)(2,1)S(1)}, bf16[512,128]{1,0:T(8,128)(2,1)S(1)}, u32[]{:S(2)}, u32[]{:S(2)}) collective-permute-start(bf16[512,128]{1,0:T(8,128)(2,1)S(1)} %pad_maximum_fusion.1.refs_0_), channel_id=1, source_target_pairs={{0,8},{4,36},{8,16},{12,44},{16,24},{20,52},{24,0},{28,60},{32,40}... | collective-permute-start | bytes 393224 | tf_op jit(solution)/shard_map/ppermute | solution.py:38
  8.1 2.2 %collective-permute-start.2 = (bf16[512,128]{1,0:T(8,128)(2,1)S(1)}, bf16[512,128]{1,0:T(8,128)(2,1)S(1)}, u32[]{:S(2)}, u32[]{:S(2)}) collective-permute-start(bf16[512,128]{1,0:T(8,128)(2,1)S(1)} %pad_maximum_fusion.1.refs_0_), channel_id=1, source_target_pairs={{0,24},{4,100},{8,0},{12,108},{16,8},{20,116},{24,16},{28,124},{32... | collective-permute-start | bytes 393224 | tf_op jit(solution)/shard_map/ppermute | solution.py:38
  10.3 1.2 collective-permute-start.3
  11.8 0.8 collective-permute-done.1.refs_1_
  12.6 3.3 %collective-permute-done.3.refs_3_ = bf16[512,128]{1,0:T(8,128)(2,1)S(1)} collective-permute-done((bf16[512,128]{1,0:T(8,128)(2,1)S(1)}, bf16[512,128]{1,0:T(8,128)(2,1)S(1)}, u32[]{:S(2)}, u32[]{:S(2)}) %collective-permute-start.3) | collective-permute-done | bytes 131104 | tf_op jit(solution)/shard_map/ppermute | solution.py:38
  15.9 1.1 collective-permute-start.4
  17.0 1.7 %collective-permute-start.5 = (bf16[2048,128]{1,0:T(8,128)(2,1)S(1)}, bf16[2048,128]{1,0:T(8,128)(2,1)}, u32[]{:S(2)}, u32[]{:S(2)}) collective-permute-start(bf16[2048,128]{1,0:T(8,128)(2,1)S(1)} %join.2.refs_0_), channel_id=1, source_target_pairs={{0,96},{4,28},{8,104},{12,4},{16,112},{20,12},{24,120},{28,20},{32... | collective-permute-start | bytes 1572872 | tf_op jit(solution)/shard_map/ppermute | solution.py:38
  18.7 1.4 collective-permute-start.6
  20.3 2.5 %collective-permute-start.7 = (f32[1,18]{1,0:T(1,128)S(1)}, f32[1,18]{1,0:T(1,128)S(1)}, u32[]{:S(2)}, u32[]{:S(2)}) collective-permute-start(f32[1,18]{1,0:T(1,128)S(1)} %add_convert_fusion), channel_id=1, source_target_pairs={{0,4},{4,0},{8,12},{12,8},{16,20},{20,16},{24,28},{28,24},{32,36},... | collective-permute-start | bytes 224 | tf_op jit(solution)/shard_map/ppermute | solution.py:18
  22.7 0.6 fusion.11
  23.3 1.3 iota_compare_fusion.2
  24.6 0.6 fusion.10
  25.2 1.3 iota_compare_fusion
  26.5 2.5 %broadcast_select_fusion.1 = (bf16[2048,256]{1,0:T(8,128)(2,1)S(1)}, bf16[2048,256]{1,0:T(8,128)(2,1)S(1)}) fusion(pred[]{:T(512)S(6)} %eq.25, bf16[2,1,2048,256]{3,2,1,0:T(8,128)(2,1)} %param.7, pred[256]{0:T(512)(128)(4,1)S(1)} %get-tuple-element.85, pred[256]{0:T(512)(128)(4,1)S(1)} %get-tuple-element.86, ...), kind=kLoop, calls=%fused_computation.9 | loop fusion | flops 4194304 | bytes 6292481 | tf_op jit(solution)/shard_map/jit(_where)/select_n | solution.py:380
  29.0 0.8 copy-done.10
  29.8 0.6 collective-permute-done.5.refs_2_
  30.4 1.8 %collective-permute-done.6.refs_3_ = bf16[2048,128]{1,0:T(8,128)(2,1)} collective-permute-done((bf16[2048,128]{1,0:T(8,128)(2,1)S(1)}, bf16[2048,128]{1,0:T(8,128)(2,1)}, u32[]{:S(2)}, u32[]{:S(2)}) %collective-permute-start.6) | collective-permute-done | bytes 524320 | tf_op jit(solution)/shard_map/ppermute | solution.py:38
  32.2 1.0 copy-done.11
  33.3 3.9 %solve.1 = (bf16[512,768]{1,0:T(8,128)(2,1)S(1)}, bf16[128,512]{1,0:T(8,128)(2,1)S(1)}, bf16[128,512]{1,0:T(8,128)(2,1)S(1)}, bf16[128,512]{1,0:T(8,128)(2,1)S(1)}, bf16[128,512]{1,0:T(8,128)(2,1)S(1)}) custom-call(s32[4]{0:T(128)S(1)} %pad_add_fusion.1.where, bf16[2048,128]{1,0:T(8,128)(2,1)S(1)} %join.2.refs_0_, bf16[2048,128]{1,0:T(8,128)(2,1)S(1)} %copy-done.11, ...), custom_call_target="tpu_custom_call" | custom-call | flops 1610612736 | tf_op jit(solution)/shard_map/solve/pallas_call | solution.py:108
  37.2 1.3 collective-permute-start.10
  38.5 1.5 collective-permute-start.9
  39.9 1.5 collective-permute-start.11
  41.5 0.8 collective-permute-done.10
  42.3 2.9 %collective-permute-done.11 = bf16[128,512]{1,0:T(8,128)(2,1)S(1)} collective-permute-done((bf16[128,512]{1,0:T(8,128)(2,1)S(1)}, bf16[128,512]{1,0:T(8,128)(2,1)S(1)}, u32[]{:S(2)}, u32[]{:S(2)}) %collective-permute-start.11) | collective-permute-done | bytes 131104 | tf_op jit(solution)/shard_map/ppermute | solution.py:27
  45.3 0.5 collective-permute-start.12
  45.7 2.2 %collective-permute-start.18 = (bf16[512,768]{1,0:T(8,128)(2,1)S(1)}, bf16[512,768]{1,0:T(8,128)(2,1)S(1)}, u32[]{:S(2)}, u32[]{:S(2)}) collective-permute-start(bf16[512,768]{1,0:T(8,128)(2,1)S(1)} %get-tuple-element.51.refs_0_), channel_id=1, source_target_pairs={{0,1},{1,2},{2,3},{3,0},{4,7},{5,4},{6,5},{7,6},{8,9},{9,10},{10,1... | collective-permute-start | bytes 2359304 | tf_op jit(solution)/shard_map/ppermute | solution.py:27
  47.9 1.3 collective-permute-start.20
  49.2 2.5 %collective-permute-start.13 = (bf16[128,2048]{1,0:T(8,128)(2,1)S(1)}, bf16[128,2048]{1,0:T(8,128)(2,1)S(1)}, u32[]{:S(2)}, u32[]{:S(2)}) collective-permute-start(bf16[128,2048]{1,0:T(8,128)(2,1)S(1)} %constant_dynamic-update-slice_fusion.refs_0_), channel_id=1, source_target_pairs={{0,24},{4,100},{8,0},{12,108},{16,8},{20,116},{24,16},{28,124},{32... | collective-permute-start | bytes 1572872 | tf_op jit(solution)/shard_map/ppermute | solution.py:38
  51.7 2.9 %collective-permute-done.12.refs_1_ = bf16[128,2048]{1,0:T(8,128)(2,1)S(1)} collective-permute-done((bf16[128,2048]{1,0:T(8,128)(2,1)S(1)}, bf16[128,2048]{1,0:T(8,128)(2,1)S(1)}, u32[]{:S(2)}, u32[]{:S(2)}) %collective-permute-start.12) | collective-permute-done | bytes 524320 | tf_op jit(solution)/shard_map/ppermute | solution.py:38
  54.6 8.8 %collective-permute-done.13.refs_2_ = bf16[128,2048]{1,0:T(8,128)(2,1)S(1)} collective-permute-done((bf16[128,2048]{1,0:T(8,128)(2,1)S(1)}, bf16[128,2048]{1,0:T(8,128)(2,1)S(1)}, u32[]{:S(2)}, u32[]{:S(2)}) %collective-permute-start.13) | collective-permute-done | bytes 524320 | tf_op jit(solution)/shard_map/ppermute | solution.py:38
  63.4 0.7 collective-permute-done.14.refs_3_
  64.3 0.9 collective-permute-start.15
  65.2 1.8 %collective-permute-start.16 = (bf16[256,2048]{1,0:T(8,128)(2,1)S(1)}, bf16[256,2048]{1,0:T(8,128)(2,1)S(1)}, u32[]{:S(2)}, u32[]{:S(2)}) collective-permute-start(bf16[256,2048]{1,0:T(8,128)(2,1)S(1)} %get-tuple-element.47.refs_1_), channel_id=1, source_target_pairs={{0,96},{4,28},{8,104},{12,4},{16,112},{20,12},{24,120},{28,20},{32... | collective-permute-start | bytes 3145736 | tf_op jit(solution)/shard_map/ppermute | solution.py:38
  67.0 1.7 %collective-permute-done.19.refs_2_ = bf16[512,768]{1,0:T(8,128)(2,1)S(1)} collective-permute-done((bf16[512,768]{1,0:T(8,128)(2,1)S(1)}, bf16[512,768]{1,0:T(8,128)(2,1)S(1)}, u32[]{:S(2)}, u32[]{:S(2)}) %collective-permute-start.19) | collective-permute-done | bytes 786464 | tf_op jit(solution)/shard_map/ppermute | solution.py:27
  68.8 10.0 %collective-permute-done.20.refs_3_ = bf16[512,768]{1,0:T(8,128)(2,1)S(1)} collective-permute-done((bf16[512,768]{1,0:T(8,128)(2,1)S(1)}, bf16[512,768]{1,0:T(8,128)(2,1)S(1)}, u32[]{:S(2)}, u32[]{:S(2)}) %collective-permute-start.20) | collective-permute-done | bytes 786464 | tf_op jit(solution)/shard_map/ppermute | solution.py:27
  78.7 2.0 %collective-permute-start.23 = (bf16[256,2048]{1,0:T(8,128)(2,1)S(1)}, bf16[256,2048]{1,0:T(8,128)(2,1)S(1)}, u32[]{:S(2)}, u32[]{:S(2)}) collective-permute-start(bf16[256,2048]{1,0:T(8,128)(2,1)S(1)} %get-tuple-element.60.refs_1_), channel_id=1, source_target_pairs={{0,32},{4,12},{8,40},{12,20},{16,48},{20,28},{24,56},{28,4},{32,64... | collective-permute-start | bytes 3145736 | tf_op jit(solution)/shard_map/ppermute | solution.py:38
  80.7 0.7 collective-permute-start.24
  81.4 2.0 %couple.1 = (bf16[2048,768]{1,0:T(8,128)(2,1)S(1)}, f32[768,256]{1,0:T(8,128)}) custom-call(bf16[512,768]{1,0:T(8,128)(2,1)S(1)} %get-tuple-element.51.refs_0_, bf16[512,768]{1,0:T(8,128)(2,1)S(1)} %collective-permute-done.18.refs_1_, bf16[512,768]{1,0:T(8,128)(2,1)S(1)} %collective-permute-done.19.refs_2_, bf16[512,768]{1,0:T(8,128)(2,1)S(1)} %collective-permute-done.20.refs_3_), custom_call_target="tpu_custom_call" | custom-call | flops 805306368 | tf_op jit(solution)/shard_map/couple/pallas_call | solution.py:233
  83.4 1.0 collective-permute-start.22
  84.5 3.9 %multiply.2.early0 = f32[768,768]{1,0:T(8,128)S(1)} custom-call(bf16[2048,768]{1,0:T(8,128)(2,1)S(1)} %get-tuple-element.59.refs_0_.whole, bf16[256,2048]{1,0:T(8,128)(2,1)S(1)} %get-tuple-element.47.refs_1_, bf16[256,2048]{1,0:T(8,128)(2,1)} %collective-permute-done.15.refs_2_, bf16[256,2048]{1,0:T(8,128)(2,1)S(1)} %collective-permute-done.16.refs_3_), custom_call_target="tpu_custom_call" | custom-call | flops 2415919104 | tf_op jit(solution)/shard_map/multiply/pallas_call | solution.py:142
  88.4 1.4 copy-done.3
  89.8 4.1 %collective-permute-done.23.refs_2_ = bf16[256,2048]{1,0:T(8,128)(2,1)S(1)} collective-permute-done((bf16[256,2048]{1,0:T(8,128)(2,1)S(1)}, bf16[256,2048]{1,0:T(8,128)(2,1)S(1)}, u32[]{:S(2)}, u32[]{:S(2)}) %collective-permute-start.23) | collective-permute-done | bytes 1048608 | tf_op jit(solution)/shard_map/ppermute | solution.py:38
  93.9 1.0 copy-done.8
  94.9 1.7 %collective-permute-start.25 = (bf16[256,2048]{1,0:T(8,128)(2,1)}, bf16[256,2048]{1,0:T(8,128)(2,1)S(1)}, u32[]{:S(2)}, u32[]{:S(2)}) collective-permute-start(bf16[256,2048]{1,0:T(8,128)(2,1)} %collective-permute-done.24.refs_3_), channel_id=1, source_target_pairs={{0,96},{4,28},{8,104},{12,4},{16,112},{20,12},{24,120},{28,20},{32... | collective-permute-start | bytes 3145736 | tf_op jit(solution)/shard_map/ppermute | solution.py:38
  96.5 8.7 %collective-permute-start.21 = (f32[768,256]{1,0:T(8,128)}, f32[768,256]{1,0:T(8,128)}, u32[]{:S(2)}, u32[]{:S(2)}) collective-permute-start(f32[768,256]{1,0:T(8,128)} %get-tuple-element.55.small), channel_id=1, source_target_pairs={{0,4},{4,0},{8,12},{12,8},{16,20},{20,16},{24,28},{28,24},{32,36},... | collective-permute-start | bytes 2359304 | tf_op jit(solution)/shard_map/ppermute | solution.py:18
  105.7 1.9 %collective-permute-done.21.other = f32[768,256]{1,0:T(8,128)} collective-permute-done((f32[768,256]{1,0:T(8,128)}, f32[768,256]{1,0:T(8,128)}, u32[]{:S(2)}, u32[]{:S(2)}) %collective-permute-start.21) | collective-permute-done | bytes 786464 | tf_op jit(solution)/shard_map/ppermute | solution.py:18
  107.5 2.5 %finish.1 = (bf16[2,256,512]{2,1,0:T(8,128)(2,1)S(1)}, f32[256,256]{1,0:T(8,128)}, f32[256,256]{1,0:T(8,128)S(1)}) custom-call(s32[1]{0:T(128)} %bitcast.3.core, f32[768,256]{1,0:T(8,128)} %get-tuple-element.55.small, f32[768,256]{1,0:T(8,128)} %collective-permute-done.21.other), custom_call_target="tpu_custom_call" | custom-call | flops 268435456 | tf_op jit(solution)/shard_map/finish/pallas_call | solution.py:275
  110.1 1.9 %copy-done.1 = bf16[2048,768]{1,0:T(8,128)(2,1)S(1)} copy-done((bf16[2048,768]{1,0:T(8,128)(2,1)S(1)}, bf16[2048,768]{1,0:T(8,128)(2,1)}, u32[]{:S(2)}) %copy-start.1) | copy-done | bytes 3145752
  112.0 1.2 copy-done.7
  113.2 1.2 copy-done.9
  114.4 4.1 %multiply.3.early1 = f32[768,768]{1,0:T(8,128)S(1)} custom-call(bf16[2048,768]{1,0:T(8,128)(2,1)S(1)} %copy-done.1, bf16[256,2048]{1,0:T(8,128)(2,1)S(1)} %copy-done.7, bf16[256,2048]{1,0:T(8,128)(2,1)S(1)} %copy-done.9, bf16[256,2048]{1,0:T(8,128)(2,1)} %collective-permute-done.24.refs_3_), custom_call_target="tpu_custom_call" | custom-call | flops 2415919104 | tf_op jit(solution)/shard_map/multiply/pallas_call | solution.py:142
  118.6 4.5 %pick.1 = bf16[2,16,64,512]{3,2,1,0:T(8,128)(2,1)} custom-call(s32[2,16]{1,0:T(2,128)S(1)} %fusion.5.places, bf16[2,256,512]{2,1,0:T(8,128)(2,1)S(1)} %get-tuple-element.58.mats, bf16[2048,768]{1,0:T(8,128)(2,1)S(1)} %copy-done.2, bf16[256,2048]{1,0:T(8,128)(2,1)S(1)} %collective-permute-done.22.piece0, ...), custom_call_target="tpu_custom_call" | custom-call | flops 1073741824 | tf_op jit(solution)/shard_map/pick/pallas_call | solution.py:199
  123.1 5.0 %all-to-all-start = ((bf16[8,4,64,512]{3,2,1,0:T(8,128)(2,1)}), bf16[8,4,64,512]{3,2,1,0:T(8,128)(2,1)S(1)}, u32[]{:S(2)}, u32[]{:S(2)}) async-start(bf16[8,4,64,512]{3,2,1,0:T(8,128)(2,1)} %bitcast.18), calls=%async_computation | async-start | bytes 4194304 | tf_op jit(solution)/shard_map/all_to_all | solution.py:456
  128.2 0.8 pad_maximum_fusion
  129.0 2.2 %collective-permute-done.17 = bf16[512,512]{1,0:T(8,128)(2,1)} collective-permute-done((bf16[512,512]{1,0:T(8,128)(2,1)}, bf16[512,512]{1,0:T(8,128)(2,1)}, u32[]{:S(2)}, u32[]{:S(2)}) %collective-permute-start.17) | collective-permute-done | bytes 524320 | tf_op jit(solution)/shard_map/ppermute | solution.py:18
  131.3 1.9 %slice_select_fusion = (bf16[512,256]{1,0:T(8,128)(2,1)}, bf16[1,512,256]{2,1,0:T(8,128)(2,1)}, bf16[1,512,256]{2,1,0:T(8,128)(2,1)}) fusion(bf16[512,512]{1,0:T(8,128)(2,1)} %collective-permute-done.17, pred[]{:T(512)S(6)} %eq.25, bf16[512,768]{1,0:T(8,128)(2,1)S(1)} %get-tuple-element.51.refs_0_), kind=kLoop, calls=%fused_computation.12 | loop fusion | flops 524288 | bytes 2097153 | tf_op jit(solution)/shard_map/jit(_where)/select_n | solution.py:380
  133.2 0.8 constant_dynamic-slice_fusion.1.band
  134.0 1.0 constant_dynamic-slice_fusion.piece
  135.0 1.0 update.1
  136.0 18.3 %all-to-all-done = bf16[8,4,64,512]{3,2,1,0:T(8,128)(2,1)S(1)} async-done(((bf16[8,4,64,512]{3,2,1,0:T(8,128)(2,1)}), bf16[8,4,64,512]{3,2,1,0:T(8,128)(2,1)S(1)}, u32[]{:S(2)}, u32[]{:S(2)}) %all-to-all-start) | async-done | bytes 2097184 | tf_op jit(solution)/shard_map/all_to_all | solution.py:456
  154.3 2.9 %settle.1 = f32[4,512,512]{2,1,0:T(8,128)} custom-call(bf16[2,4,4,64,512]{4,3,2,1,0:T(8,128)(2,1)S(1)} %bitcast.58), custom_call_target="tpu_custom_call" | custom-call | flops 1073741824 | tf_op jit(solution)/shard_map/settle/pallas_call | solution.py:324
  (63 shorter events, 1.7 us)
Async XLA Ops:
  0.6 10.9 %copy-start.12 = (bf16[2048,256]{1,0:T(8,128)(2,1)S(1)}, bf16[2048,256]{1,0:T(8,128)(2,1)}, u32[]{:S(2)}) copy-start(bf16[2048,256]{1,0:T(8,128)(2,1)} %param.9) | copy-start | bytes 3145732
  0.6 25.9 %collective-permute-start.8 = (bf16[2,1,2048,256]{3,2,1,0:T(8,128)(2,1)}, bf16[2,1,2048,256]{3,2,1,0:T(8,128)(2,1)}, u32[]{:S(2)}, u32[]{:S(2)}) collective-permute-start(bf16[2,1,2048,256]{3,2,1,0:T(8,128)(2,1)} %param.7), channel_id=1, source_target_pairs={{0,4},{4,0},{8,12},{12,8},{16,20},{20,16},{24,28},{28,24},{32,36},... | collective-permute-start | bytes 6291464 | tf_op jit(solution)/shard_map/ppermute | solution.py:18
  3.3 8.2 %copy-start.13 = (bf16[2048,256]{1,0:T(8,128)(2,1)S(1)}, bf16[2048,256]{1,0:T(8,128)(2,1)}, u32[]{:S(2)}) copy-start(bf16[2048,256]{1,0:T(8,128)(2,1)} %param.8) | copy-start | bytes 3145732
  3.3 2.8 %collective-permute-start = (bf16[512,64]{1,0:T(8,128)(2,1)S(1)}, bf16[512,64]{1,0:T(8,128)(2,1)S(1)}, u32[]{:S(2)}, u32[]{:S(2)}) collective-permute-start(bf16[512,64]{1,0:T(8,128)(2,1)S(1)} %select_bitcast_fusion.2), channel_id=1, source_target_pairs={{0,4},{4,0},{8,12},{12,8},{16,20},{20,16},{24,28},{28,24},{32,36},... | collective-permute-start | bytes 196616 | tf_op jit(solution)/shard_map/ppermute | solution.py:18
  6.3 13.8 %copy-start.14 = (s32[1,4,4]{2,1,0:T(4,128)S(1)}, s32[1,4,4]{2,1,0:T(4,128)}, u32[]{:S(2)}) copy-start(s32[1,4,4]{2,1,0:T(4,128)} %param.13) | copy-start | bytes 196
  6.3 13.9 %copy-start.15 = (s32[2,1]{0,1:T(1,128)S(1)}, s32[2,1]{0,1:T(1,128)}, u32[]{:S(2)}) copy-start(s32[2,1]{0,1:T(1,128)} %param.12) | copy-start | bytes 28
  6.3 6.3 %collective-permute-start.1 = (bf16[512,128]{1,0:T(8,128)(2,1)S(1)}, bf16[512,128]{1,0:T(8,128)(2,1)S(1)}, u32[]{:S(2)}, u32[]{:S(2)}) collective-permute-start(bf16[512,128]{1,0:T(8,128)(2,1)S(1)} %pad_maximum_fusion.1.refs_0_), channel_id=1, source_target_pairs={{0,8},{4,36},{8,16},{12,44},{16,24},{20,52},{24,0},{28,60},{32,40}... | collective-permute-start | bytes 393224 | tf_op jit(solution)/shard_map/ppermute | solution.py:38
  8.1 4.5 %collective-permute-start.2 = (bf16[512,128]{1,0:T(8,128)(2,1)S(1)}, bf16[512,128]{1,0:T(8,128)(2,1)S(1)}, u32[]{:S(2)}, u32[]{:S(2)}) collective-permute-start(bf16[512,128]{1,0:T(8,128)(2,1)S(1)} %pad_maximum_fusion.1.refs_0_), channel_id=1, source_target_pairs={{0,24},{4,100},{8,0},{12,108},{16,8},{20,116},{24,16},{28,124},{32... | collective-permute-start | bytes 393224 | tf_op jit(solution)/shard_map/ppermute | solution.py:38
  10.3 5.6 %collective-permute-start.3 = (bf16[512,128]{1,0:T(8,128)(2,1)S(1)}, bf16[512,128]{1,0:T(8,128)(2,1)S(1)}, u32[]{:S(2)}, u32[]{:S(2)}) collective-permute-start(bf16[512,128]{1,0:T(8,128)(2,1)S(1)} %pad_maximum_fusion.1.refs_0_), channel_id=1, source_target_pairs={{0,16},{4,68},{8,24},{12,76},{16,0},{20,84},{24,8},{28,92},{32,48}... | collective-permute-start | bytes 393224 | tf_op jit(solution)/shard_map/ppermute | solution.py:38
  15.9 13.0 %collective-permute-start.4 = (bf16[2048,128]{1,0:T(8,128)(2,1)S(1)}, bf16[2048,128]{1,0:T(8,128)(2,1)S(1)}, u32[]{:S(2)}, u32[]{:S(2)}) collective-permute-start(bf16[2048,128]{1,0:T(8,128)(2,1)S(1)} %join.2.refs_0_), channel_id=1, source_target_pairs={{0,32},{4,12},{8,40},{12,20},{16,48},{20,28},{24,56},{28,4},{32,64... | collective-permute-start | bytes 1572872 | tf_op jit(solution)/shard_map/ppermute | solution.py:38
  17.0 13.4 %collective-permute-start.5 = (bf16[2048,128]{1,0:T(8,128)(2,1)S(1)}, bf16[2048,128]{1,0:T(8,128)(2,1)}, u32[]{:S(2)}, u32[]{:S(2)}) collective-permute-start(bf16[2048,128]{1,0:T(8,128)(2,1)S(1)} %join.2.refs_0_), channel_id=1, source_target_pairs={{0,96},{4,28},{8,104},{12,4},{16,112},{20,12},{24,120},{28,20},{32... | collective-permute-start | bytes 1572872 | tf_op jit(solution)/shard_map/ppermute | solution.py:38
  18.7 13.5 %collective-permute-start.6 = (bf16[2048,128]{1,0:T(8,128)(2,1)S(1)}, bf16[2048,128]{1,0:T(8,128)(2,1)}, u32[]{:S(2)}, u32[]{:S(2)}) collective-permute-start(bf16[2048,128]{1,0:T(8,128)(2,1)S(1)} %join.2.refs_0_), channel_id=1, source_target_pairs={{0,64},{4,20},{8,72},{12,28},{16,80},{20,4},{24,88},{28,12},{32,96... | collective-permute-start | bytes 1572872 | tf_op jit(solution)/shard_map/ppermute | solution.py:38
  20.3 4.3 %collective-permute-start.7 = (f32[1,18]{1,0:T(1,128)S(1)}, f32[1,18]{1,0:T(1,128)S(1)}, u32[]{:S(2)}, u32[]{:S(2)}) collective-permute-start(f32[1,18]{1,0:T(1,128)S(1)} %add_convert_fusion), channel_id=1, source_target_pairs={{0,4},{4,0},{8,12},{12,8},{16,20},{20,16},{24,28},{28,24},{32,36},... | collective-permute-start | bytes 224 | tf_op jit(solution)/shard_map/ppermute | solution.py:18
  29.0 0.8 copy-start.10
  32.2 1.0 copy-start.11
  37.2 5.1 %collective-permute-start.10 = (bf16[128,512]{1,0:T(8,128)(2,1)S(1)}, bf16[128,512]{1,0:T(8,128)(2,1)S(1)}, u32[]{:S(2)}, u32[]{:S(2)}) collective-permute-start(bf16[128,512]{1,0:T(8,128)(2,1)S(1)} %get-tuple-element.43), channel_id=1, source_target_pairs={{0,3},{1,0},{2,1},{3,2},{4,5},{5,6},{6,7},{7,4},{8,11},{9,8},{10,9... | collective-permute-start | bytes 393224 | tf_op jit(solution)/shard_map/ppermute | solution.py:27
  38.5 3.8 %collective-permute-start.9 = (bf16[128,512]{1,0:T(8,128)(2,1)S(1)}, bf16[128,512]{1,0:T(8,128)(2,1)S(1)}, u32[]{:S(2)}, u32[]{:S(2)}) collective-permute-start(bf16[128,512]{1,0:T(8,128)(2,1)S(1)} %get-tuple-element.42), channel_id=1, source_target_pairs={{0,1},{1,2},{2,3},{3,0},{4,7},{5,4},{6,5},{7,6},{8,9},{9,10},{10,1... | collective-permute-start | bytes 393224 | tf_op jit(solution)/shard_map/ppermute | solution.py:27
  39.9 5.3 %collective-permute-start.11 = (bf16[128,512]{1,0:T(8,128)(2,1)S(1)}, bf16[128,512]{1,0:T(8,128)(2,1)S(1)}, u32[]{:S(2)}, u32[]{:S(2)}) collective-permute-start(bf16[128,512]{1,0:T(8,128)(2,1)S(1)} %get-tuple-element.46), channel_id=1, source_target_pairs={{0,2},{1,3},{2,0},{3,1},{4,6},{5,7},{6,4},{7,5},{8,10},{9,11},{10,... | collective-permute-start | bytes 393224 | tf_op jit(solution)/shard_map/ppermute | solution.py:27
  45.3 9.3 %collective-permute-start.12 = (bf16[128,2048]{1,0:T(8,128)(2,1)S(1)}, bf16[128,2048]{1,0:T(8,128)(2,1)S(1)}, u32[]{:S(2)}, u32[]{:S(2)}) collective-permute-start(bf16[128,2048]{1,0:T(8,128)(2,1)S(1)} %constant_dynamic-update-slice_fusion.refs_0_), channel_id=1, source_target_pairs={{0,8},{4,36},{8,16},{12,44},{16,24},{20,52},{24,0},{28,60},{32,40}... | collective-permute-start | bytes 1572872 | tf_op jit(solution)/shard_map/ppermute | solution.py:38
  45.7 21.3 %collective-permute-start.18 = (bf16[512,768]{1,0:T(8,128)(2,1)S(1)}, bf16[512,768]{1,0:T(8,128)(2,1)S(1)}, u32[]{:S(2)}, u32[]{:S(2)}) collective-permute-start(bf16[512,768]{1,0:T(8,128)(2,1)S(1)} %get-tuple-element.51.refs_0_), channel_id=1, source_target_pairs={{0,1},{1,2},{2,3},{3,0},{4,7},{5,4},{6,5},{7,6},{8,9},{9,10},{10,1... | collective-permute-start | bytes 2359304 | tf_op jit(solution)/shard_map/ppermute | solution.py:27
  47.9 20.8 %collective-permute-start.19 = (bf16[512,768]{1,0:T(8,128)(2,1)S(1)}, bf16[512,768]{1,0:T(8,128)(2,1)S(1)}, u32[]{:S(2)}, u32[]{:S(2)}) collective-permute-start(bf16[512,768]{1,0:T(8,128)(2,1)S(1)} %get-tuple-element.51.refs_0_), channel_id=1, source_target_pairs={{0,3},{1,0},{2,1},{3,2},{4,5},{5,6},{6,7},{7,4},{8,11},{9,8},{10,9... | collective-permute-start | bytes 2359304 | tf_op jit(solution)/shard_map/ppermute | solution.py:27
  47.9 30.8 %collective-permute-start.20 = (bf16[512,768]{1,0:T(8,128)(2,1)S(1)}, bf16[512,768]{1,0:T(8,128)(2,1)S(1)}, u32[]{:S(2)}, u32[]{:S(2)}) collective-permute-start(bf16[512,768]{1,0:T(8,128)(2,1)S(1)} %get-tuple-element.51.refs_0_), channel_id=1, source_target_pairs={{0,2},{1,3},{2,0},{3,1},{4,6},{5,7},{6,4},{7,5},{8,10},{9,11},{10,... | collective-permute-start | bytes 2359304 | tf_op jit(solution)/shard_map/ppermute | solution.py:27
  49.2 14.3 %collective-permute-start.13 = (bf16[128,2048]{1,0:T(8,128)(2,1)S(1)}, bf16[128,2048]{1,0:T(8,128)(2,1)S(1)}, u32[]{:S(2)}, u32[]{:S(2)}) collective-permute-start(bf16[128,2048]{1,0:T(8,128)(2,1)S(1)} %constant_dynamic-update-slice_fusion.refs_0_), channel_id=1, source_target_pairs={{0,24},{4,100},{8,0},{12,108},{16,8},{20,116},{24,16},{28,124},{32... | collective-permute-start | bytes 1572872 | tf_op jit(solution)/shard_map/ppermute | solution.py:38
  54.6 9.5 %collective-permute-start.14 = (bf16[128,2048]{1,0:T(8,128)(2,1)S(1)}, bf16[128,2048]{1,0:T(8,128)(2,1)S(1)}, u32[]{:S(2)}, u32[]{:S(2)}) collective-permute-start(bf16[128,2048]{1,0:T(8,128)(2,1)S(1)} %constant_dynamic-update-slice_fusion.refs_0_), channel_id=1, source_target_pairs={{0,16},{4,68},{8,24},{12,76},{16,0},{20,84},{24,8},{28,92},{32,48}... | collective-permute-start | bytes 1572872 | tf_op jit(solution)/shard_map/ppermute | solution.py:38
  64.3 24.1 %copy-start.6 = (bf16[256,2048]{1,0:T(8,128)(2,1)}, bf16[256,2048]{1,0:T(8,128)(2,1)S(1)}, u32[]{:S(2)}) copy-start(bf16[256,2048]{1,0:T(8,128)(2,1)S(1)} %get-tuple-element.60.refs_1_) | copy-start | bytes 3145732
  64.3 19.1 %collective-permute-start.15 = (bf16[256,2048]{1,0:T(8,128)(2,1)S(1)}, bf16[256,2048]{1,0:T(8,128)(2,1)}, u32[]{:S(2)}, u32[]{:S(2)}) collective-permute-start(bf16[256,2048]{1,0:T(8,128)(2,1)S(1)} %get-tuple-element.47.refs_1_), channel_id=1, source_target_pairs={{0,32},{4,12},{8,40},{12,20},{16,48},{20,28},{24,56},{28,4},{32,64... | collective-permute-start | bytes 3145736 | tf_op jit(solution)/shard_map/ppermute | solution.py:38
  65.2 18.2 %collective-permute-start.16 = (bf16[256,2048]{1,0:T(8,128)(2,1)S(1)}, bf16[256,2048]{1,0:T(8,128)(2,1)S(1)}, u32[]{:S(2)}, u32[]{:S(2)}) collective-permute-start(bf16[256,2048]{1,0:T(8,128)(2,1)S(1)} %get-tuple-element.47.refs_1_), channel_id=1, source_target_pairs={{0,96},{4,28},{8,104},{12,4},{16,112},{20,12},{24,120},{28,20},{32... | collective-permute-start | bytes 3145736 | tf_op jit(solution)/shard_map/ppermute | solution.py:38
  78.7 15.2 %collective-permute-start.23 = (bf16[256,2048]{1,0:T(8,128)(2,1)S(1)}, bf16[256,2048]{1,0:T(8,128)(2,1)S(1)}, u32[]{:S(2)}, u32[]{:S(2)}) collective-permute-start(bf16[256,2048]{1,0:T(8,128)(2,1)S(1)} %get-tuple-element.60.refs_1_), channel_id=1, source_target_pairs={{0,32},{4,12},{8,40},{12,20},{16,48},{20,28},{24,56},{28,4},{32,64... | collective-permute-start | bytes 3145736 | tf_op jit(solution)/shard_map/ppermute | solution.py:38
  80.7 14.2 %collective-permute-start.24 = (bf16[256,2048]{1,0:T(8,128)(2,1)S(1)}, bf16[256,2048]{1,0:T(8,128)(2,1)}, u32[]{:S(2)}, u32[]{:S(2)}) collective-permute-start(bf16[256,2048]{1,0:T(8,128)(2,1)S(1)} %get-tuple-element.60.refs_1_), channel_id=1, source_target_pairs={{0,96},{4,28},{8,104},{12,4},{16,112},{20,12},{24,120},{28,20},{32... | collective-permute-start | bytes 3145736 | tf_op jit(solution)/shard_map/ppermute | solution.py:38
  83.4 5.0 %copy-start = (bf16[2048,768]{1,0:T(8,128)(2,1)}, bf16[2048,768]{1,0:T(8,128)(2,1)S(1)}, u32[]{:S(2)}) copy-start(bf16[2048,768]{1,0:T(8,128)(2,1)S(1)} %get-tuple-element.59.refs_0_.whole) | copy-start | bytes 9437188
  83.4 35.2 %collective-permute-start.22 = (bf16[256,2048]{1,0:T(8,128)(2,1)}, bf16[256,2048]{1,0:T(8,128)(2,1)S(1)}, u32[]{:S(2)}, u32[]{:S(2)}) collective-permute-start(bf16[256,2048]{1,0:T(8,128)(2,1)} %collective-permute-done.15.refs_2_), channel_id=1, source_target_pairs={{0,32},{4,12},{8,40},{12,20},{16,48},{20,28},{24,56},{28,4},{32,64... | collective-permute-start | bytes 3145736 | tf_op jit(solution)/shard_map/ppermute | solution.py:38
  88.4 1.4 copy-start.3
  93.9 1.0 copy-start.8
  94.9 23.7 %collective-permute-start.25 = (bf16[256,2048]{1,0:T(8,128)(2,1)}, bf16[256,2048]{1,0:T(8,128)(2,1)S(1)}, u32[]{:S(2)}, u32[]{:S(2)}) collective-permute-start(bf16[256,2048]{1,0:T(8,128)(2,1)} %collective-permute-done.24.refs_3_), channel_id=1, source_target_pairs={{0,96},{4,28},{8,104},{12,4},{16,112},{20,12},{24,120},{28,20},{32... | collective-permute-start | bytes 3145736 | tf_op jit(solution)/shard_map/ppermute | solution.py:38
  96.5 11.0 %collective-permute-start.21 = (f32[768,256]{1,0:T(8,128)}, f32[768,256]{1,0:T(8,128)}, u32[]{:S(2)}, u32[]{:S(2)}) collective-permute-start(f32[768,256]{1,0:T(8,128)} %get-tuple-element.55.small), channel_id=1, source_target_pairs={{0,4},{4,0},{8,12},{12,8},{16,20},{20,16},{24,28},{28,24},{32,36},... | collective-permute-start | bytes 2359304 | tf_op jit(solution)/shard_map/ppermute | solution.py:18
  110.1 1.9 %copy-start.1 = (bf16[2048,768]{1,0:T(8,128)(2,1)S(1)}, bf16[2048,768]{1,0:T(8,128)(2,1)}, u32[]{:S(2)}) copy-start(bf16[2048,768]{1,0:T(8,128)(2,1)} %copy-done) | copy-start | bytes 9437188
  112.0 1.2 copy-start.7
  113.2 1.2 copy-start.9
  114.4 4.2 %copy-start.2 = (bf16[2048,768]{1,0:T(8,128)(2,1)S(1)}, bf16[2048,768]{1,0:T(8,128)(2,1)}, u32[]{:S(2)}) copy-start(bf16[2048,768]{1,0:T(8,128)(2,1)} %copy-done) | copy-start | bytes 9437188
  114.4 4.2 %copy-start.4 = (f32[768,768]{1,0:T(8,128)S(1)}, f32[768,768]{1,0:T(8,128)}, u32[]{:S(2)}) copy-start(f32[768,768]{1,0:T(8,128)} %copy-done.3) | copy-start | bytes 7077892
  123.1 31.2 %all-to-all-start = ((bf16[8,4,64,512]{3,2,1,0:T(8,128)(2,1)}), bf16[8,4,64,512]{3,2,1,0:T(8,128)(2,1)S(1)}, u32[]{:S(2)}, u32[]{:S(2)}) async-start(bf16[8,4,64,512]{3,2,1,0:T(8,128)(2,1)} %bitcast.18), calls=%async_computation | async-start | bytes 4194304 | tf_op jit(solution)/shard_map/all_to_all | solution.py:456
  128.2 6.8 %copy-start.5 = (f32[64,512]{1,0:T(8,128)S(1)}, f32[64,512]{1,0:T(8,128)}, u32[]{:S(2)}) copy-start(f32[64,512]{1,0:T(8,128)} %before.1) | copy-start | bytes 393220
  129.0 2.3 %collective-permute-start.17 = (bf16[512,512]{1,0:T(8,128)(2,1)}, bf16[512,512]{1,0:T(8,128)(2,1)}, u32[]{:S(2)}, u32[]{:S(2)}) collective-permute-start(bf16[512,512]{1,0:T(8,128)(2,1)} %pad_maximum_fusion), channel_id=1, source_target_pairs={{0,4},{4,0},{8,12},{12,8},{16,20},{20,16},{24,28},{28,24},{32,36},... | collective-permute-start | bytes 1572872 | tf_op jit(solution)/shard_map/ppermute | solution.py:18
